TPU v7x, 128 devices: a whole 4x4x4 slice. The times are simulated.
128 devices in a mesh: ao: 8 (over y, core), aux: 16 (over z, x).
Axes of the slice: x: 4, y: 4, z: 4, core: 2. Of those that a mesh axis runs over, the one named last changes fastest.
Arguments:
- three_centre: bfloat16 [32768, 4096], P('ao', 'aux'), may hold values from -1 to 1
- tile_list: int32 [8, 32], P('ao', 'aux'), may hold values 0 or 1
- pair_blocks: int32 [8, 2], P('ao'), may hold values from 0 to 15
- green_occ: bfloat16 [16, 64, 64], replicated, may hold values from -0.75 to 0.75
- green_virt: bfloat16 [16, 64, 64], replicated, may hold values from -0.75 to 0.75
Outputs:
- polarizability: float32 [4096, 4096], P('aux', 'ao')
All inputs are finite; a program needn't handle non-finite values. No bound on the sum of `tile_list` on one device may be relied on, other than what follows from the above.
Results may differ from a plain program's by a relative error of at most 0.0041.
Values may be sent and summed in bfloat16 or wider, within the bound.
No kernel may reach another device: no remote copies, remote signals or barrier semaphores. Data moves between devices by JAX's collectives and lax.ppermute only.
A program may use at most 128 MiB of HBM per device.

v0:
```python
import jax
import jax.numpy as jnp
from jax import lax
from jax.sharding import PartitionSpec as P


def pick_blocks(indices, table):
    blocks_total, width = (table.shape[0], table.shape[1])
    onehot = (indices[:, None] == jnp.arange(blocks_total)[None, :]).astype(jnp.bfloat16)
    picked = jnp.dot(
        onehot, table.reshape(blocks_total, width * width), preferred_element_type=jnp.float32
    )
    return picked.astype(jnp.bfloat16).reshape(indices.shape[0], width, width)


def per_device(three_centre, tile_list, pair_blocks, green_occ, green_virt):
    width = green_occ.shape[1]
    local_rows, local_cols = three_centre.shape
    pairs = local_rows // (width * width)
    aux_blocks = tile_list.shape[1]
    weights = tile_list.astype(jnp.bfloat16)
    tiles = (
        three_centre.reshape(pairs, width * width, aux_blocks, local_cols // aux_blocks)
        * weights[:, None, :, None]
    )
    tiles = tiles.reshape(pairs, width * width, local_cols)
    occ = pick_blocks(pair_blocks[:, 0], green_occ)
    virt = pick_blocks(pair_blocks[:, 1], green_virt)
    half = jnp.einsum(
        "rlm,rmc->rlc",
        occ,
        tiles.reshape(pairs, width, width * local_cols),
        preferred_element_type=jnp.float32,
    ).astype(jnp.bfloat16)
    contracted = jnp.einsum(
        "rlnc,rsn->rlsc",
        half.reshape(pairs, width, width, local_cols),
        virt,
        preferred_element_type=jnp.float32,
    ).astype(jnp.bfloat16)
    masked_rows = tiles.reshape(local_rows, local_cols)
    contracted_rows = contracted.reshape(local_rows, local_cols)
    partial_sums = lax.dot_general(
        masked_rows,
        lax.all_gather(contracted_rows, "aux", axis=1, tiled=True),
        (((0,), (0,)), ((), ())),
        preferred_element_type=jnp.float32,
    )
    result = -2.0 * lax.psum_scatter(partial_sums, "ao", scatter_dimension=1, tiled=True)
    return result


def solution(mesh):
    in_specs = (P("ao", "aux"), P("ao", "aux"), P("ao", None), P(), P())
    out_specs = P("aux", "ao")
    return jax.shard_map(
        per_device, mesh=mesh, in_specs=in_specs, out_specs=out_specs, check_vma=False
    )
```

profile of v0, /device:TPU:1, one launch (start us, length us, event | category | flops | bytes accessed | tf_op | source)
XLA Modules:
  0.0 292.0 jit_solution(4468376146098949879)
XLA Ops:
  6.5 0.0 all-gather.2.cloned.1.call-start
  6.5 0.7 convert_bitcast_fusion
  7.2 0.1 broadcast_bitcast_fusion
  7.3 1.3 fusion.10
  8.6 1.2 reshape.92
  9.8 0.8 fusion
  10.6 0.1 reshape.93
  10.7 1.2 reshape.90
  11.9 0.8 fusion.2
  12.7 0.1 reshape.100
  12.8 1.7 broadcast_multiply_fusion
  14.5 2.3 mul.33
  16.9 2.3 convolution_convert_fusion
  19.2 0.5 copy.6
  19.7 2.0 convolution_convert_fusion.1
  21.7 0.0 all-gather.2.cloned.1.call-update
  21.7 0.0 reduce-scatter.2.cloned.1.call-start
  21.8 209.1 %all-gather.2.cloned.1.call-done = bf16[4096,4096]{1,0:T(8,128)(2,1)} async-done(((bf16[4096,256]{1,0:T(8,128)(2,1)}), bf16[4096,4096]{1,0:T(8,128)(2,1)}) %all-gather.2.cloned.1.call-update) | async-done | bytes 33554448 | tf_op jit(solution)/shard_map/all_gather | solution.py:45
  230.9 17.2 %fusion.11 = f32[256,4096]{1,0:T(8,128)} fusion(bf16[4096,256]{1,0:T(8,128)(2,1)S(1)} %broadcast_multiply_fusion, bf16[4096,4096]{1,0:T(8,128)(2,1)} %all-gather.2.cloned.1.call-done), kind=kOutput, calls=%fused_computation.17 | convolution fusion | flops 8589934592 | bytes 39845888 | tf_op jit(solution)/shard_map/dot_general | solution.py:43
  248.1 0.0 reduce-scatter.2.cloned.1.call-update
  248.1 35.2 %reduce-scatter.2.cloned.1.call-done = f32[256,512]{1,0:T(8,128)} async-done(((f32[256,4096]{1,0:T(8,128)}), f32[256,512]{1,0:T(8,128)}) %reduce-scatter.2.cloned.1.call-update) | async-done | bytes 524304 | tf_op jit(solution)/shard_map/reduce_scatter | solution.py:49
  283.2 1.9 broadcast_multiply_fusion.1
  (2 shorter events, 0.0 us)
Async XLA Ops:
  6.5 224.3 %all-gather.2.cloned.1.call-start = ((), (), s32[]{:S(2)}) async-start(), calls=%async_computation.1 | async-start | bytes 35651584 | tf_op jit(solution)/shard_map/all_gather | solution.py:45
  21.7 261.5 %reduce-scatter.2.cloned.1.call-start = ((), (), s32[]{:S(2)}) async-start(), calls=%async_computation.2 | async-start | bytes 4718592 | tf_op jit(solution)/shard_map/reduce_scatter | solution.py:49
Sparse Core Ops, SparseCore 0:
  21.9 208.9 all-gather.1
  248.2 34.9 reduce-scatter.1
where the time goes:
time: 295 us; the launch traced here: 292 us
  waiting for transfers between devices  244 us (83%)
  matrix products  23 us (8%)
  between operations  13.4 us (5%)
  local copies, waits for them, and re-layouts  6.9 us (2%)
  other arithmetic  4.28 us (1%)
    all_gather x1, waiting for transfers between devices, per_device(): lax.all_gather(contracted_rows, 'aux', axis=1, tiled=True)  209 us
    reduce_scatter x1, waiting for transfers between devices, per_device(): lax.psum_scatter(partial_sums, 'ao', scatter_dimension=1, tiled=True)  35.2 us
    dot_general x1, matrix products, per_device(): lax.dot_general(masked_rows, lax.all_gather(contracted_rows, 'aux', axis=...  17.2 us
  transfers between devices with their start and end apart: 2, of which 2 were waited for; matrix products, arithmetic and copies ran while one was open for 0% of the time, Pallas kernels for 0%

commit v1 on v0

v1 whole, which is shorter than its diff:
```python
import functools

import jax
import jax.numpy as jnp
from jax import lax
from jax.experimental import pallas as pl
from jax.experimental.pallas import tpu as pltpu
from jax.sharding import Mesh, PartitionSpec as P

SIDE = 4
BLOCK = 256


def pick_blocks(indices, table):
    blocks_total, width = (table.shape[0], table.shape[1])
    onehot = (indices[:, None] == jnp.arange(blocks_total)[None, :]).astype(jnp.bfloat16)
    picked = jnp.dot(
        onehot, table.reshape(blocks_total, width * width), preferred_element_type=jnp.float32
    )
    return picked.astype(jnp.bfloat16).reshape(indices.shape[0], width, width)


def contract(tiles, occ, virt):
    width = occ.shape[-1]
    cols = tiles.shape[1]
    half = jnp.dot(
        occ, tiles.reshape(width, width * cols), preferred_element_type=jnp.float32
    ).astype(jnp.bfloat16)
    return (
        jnp.einsum(
            "lnc,sn->lsc",
            half.reshape(width, width, cols),
            virt,
            preferred_element_type=jnp.float32,
        )
        .astype(jnp.bfloat16)
        .reshape(width * width, cols)
    )


def products_kernel(steps, where, *refs):
    a_refs, b_refs = refs[0:5], refs[5:10]
    keep_ref, send_ref, acc = refs[10:]
    k = pl.program_id(0)

    @pl.when(k == 0)
    def _():
        acc[...] = jnp.zeros_like(acc)

    def block(blocks, offset):
        if offset == 2:
            return jnp.where(k < steps // 2, blocks[3][...], blocks[4][...])
        return blocks[{0: 0, 1: 1, 3: 2}[offset]][...]

    rights = [block(b_refs, q) for q in range(SIDE)]
    for p in range(SIDE):
        left = block(a_refs, p).T
        for q in range(SIDE):
            acc[where[q], where[SIDE + p]] += jnp.dot(
                left, rights[q], preferred_element_type=jnp.float32
            )

    @pl.when(k == steps - 1)
    def _():
        keep_ref[...] = acc[0:2]
        send_ref[...] = acc[2:4].astype(jnp.bfloat16)


def products(where, lefts, rights):
    rows = lefts[0].shape[0]
    chunk = 512
    steps = rows // chunk
    whole = pl.BlockSpec((chunk, BLOCK), lambda k, where: (k, 0))
    first = pl.BlockSpec((chunk, BLOCK), lambda k, where: (jnp.minimum(k, steps // 2 - 1), 0))
    second = pl.BlockSpec((chunk, BLOCK), lambda k, where: (jnp.maximum(k - steps // 2, 0), 0))
    five = [whole, whole, whole, first, second]
    shape = (2, SIDE, BLOCK, BLOCK)
    out = pl.BlockSpec(shape, lambda k, where: (0, 0, 0, 0))
    return pl.pallas_call(
        functools.partial(products_kernel, steps),
        grid_spec=pltpu.PrefetchScalarGridSpec(
            num_scalar_prefetch=1,
            grid=(steps,),
            in_specs=five + five,
            out_specs=[out, out],
            scratch_shapes=[pltpu.VMEM((SIDE, SIDE, BLOCK, BLOCK), jnp.float32)],
        ),
        out_shape=[
            jax.ShapeDtypeStruct(shape, jnp.float32),
            jax.ShapeDtypeStruct(shape, jnp.bfloat16),
        ],
        compiler_params=pltpu.CompilerParams(vmem_limit_bytes=48 * 2**20),
        cost_estimate=pl.CostEstimate(
            flops=2 * rows * 1024 * 1024, bytes_accessed=20 * 2**20, transcendentals=0
        ),
    )(where, *lefts, *rights)


def around(block, axis):
    half = block.shape[0] // 2
    take_next = [((i + 1) % SIDE, i) for i in range(SIDE)]
    take_prev = [((i - 1) % SIDE, i) for i in range(SIDE)]
    after = lax.ppermute(block, axis, take_next)
    before = lax.ppermute(block, axis, take_prev)
    far_low = lax.ppermute(after[:half], axis, take_next)
    far_high = lax.ppermute(before[half:], axis, take_prev)
    return [block, after, before, far_low, far_high]


def per_device(three_centre, tile_list, pair_blocks, green_occ, green_virt):
    y, c, z, x = (lax.axis_index(name) for name in ("y", "c", "z", "x"))
    weights = jnp.repeat(tile_list[0].astype(jnp.bfloat16), BLOCK // tile_list.shape[1])
    tiles = three_centre * weights[None, :]
    occ = pick_blocks(pair_blocks[:, 0], green_occ)[0]
    virt = pick_blocks(pair_blocks[:, 1], green_virt)[0]
    lefts = around(tiles, "z")
    rights = around(contract(tiles, occ, virt), "x")

    column = (x + jnp.arange(SIDE)) & 3
    slot = jnp.where(column // 2 == c, 0, 2) + column % 2
    where = jnp.concatenate([slot, (z + jnp.arange(SIDE)) & 3]).astype(jnp.int32)
    keep, send = products(where, lefts, rights)

    total = keep + lax.ppermute(send, "c", [(0, 1), (1, 0)]).astype(jnp.float32)
    quarter = BLOCK // SIDE
    total = total.reshape(2, SIDE, SIDE, quarter, BLOCK)
    own = lax.dynamic_index_in_dim(total, y, 2, keepdims=False)
    for k in range(1, SIDE):
        piece = lax.dynamic_index_in_dim(total, (y + k) & 3, 2, keepdims=False)
        moved = lax.ppermute(
            piece.astype(jnp.bfloat16), "y", [(i, (i + k) % SIDE) for i in range(SIDE)]
        )
        own = own + moved.astype(jnp.float32)
    own = -2.0 * own

    arrived = []
    for k in range(SIDE):
        piece = lax.dynamic_index_in_dim(own, (y + k) & 3, 1, keepdims=False)
        perm = [
            (i * SIDE + j, j * SIDE + (i + k) % SIDE) for i in range(SIDE) for j in range(SIDE)
        ]
        arrived.append(lax.ppermute(piece, ("y", "z"), perm))
    stacked = jnp.stack(arrived[::-1] + arrived[:0:-1])
    ordered = lax.dynamic_slice_in_dim(stacked, (SIDE - 1 - z) & 3, SIDE, 0)
    return ordered.transpose(0, 2, 1, 3).reshape(BLOCK, 2 * BLOCK)


def solution(mesh):
    fine = Mesh(mesh.devices.reshape(SIDE, 2, SIDE, SIDE), ("y", "c", "z", "x"))
    ao, aux = ("y", "c"), ("z", "x")
    return jax.shard_map(
        per_device,
        mesh=fine,
        in_specs=(P(ao, aux), P(ao, aux), P(ao, None), P(), P()),
        out_specs=P(aux, ao),
        check_vma=False,
    )
```

time: 295 us -> 163 us (0.55)
  waiting for transfers between devices: 244 us -> 97.1 us
  starting transfers between devices: 0.04 us -> 27.3 us
  matrix products: 23 us -> 2.95 us
  Pallas kernels: 0 us -> 15.5 us
  between operations: 13.4 us -> 0.25 us
  local copies, waits for them, and re-layouts: 6.9 us -> 12.1 us
    all_gather x1 -> x0, waiting for transfers between devices: 209 us -> none  [per_device(): lax.all_gather(contracted_rows, 'aux', axis=1, tiled=True)]
    ppermute x0 -> x16, waiting for transfers between devices: none -> 97.1 us  [the longest x2 40.5 us: around(): after = lax.ppermute(block, axis, take_next)]
    reduce_scatter x1 -> x0, waiting for transfers between devices: 35.2 us -> none  [per_device(): lax.psum_scatter(partial_sums, 'ao', scatter_dimension=1, tiled=True)]
    ppermute x0 -> x16, starting transfers between devices: none -> 27.3 us  [the longest x2 7.18 us: around(): far_low = lax.ppermute(after[:half], axis, take_next)]
    dot_general x3 -> x2, matrix products: 21.5 us -> 1.39 us  [the longest x1 0.7 us: contract(): jnp.dot(occ, tiles.reshape(width, width * cols), preferred_element_type=j...]
    pallas_call x0 -> x1, Pallas kernels: none -> 15.5 us  [products(): pl.pallas_call(functools.partial(products_kernel, steps), grid_spec=pltpu...]
    slice x1 -> x5, local copies, waits for them, and re-layouts: 1.32 us -> 5.22 us  [the longest x2 2.36 us: around(): far_low = lax.ppermute(after[:half], axis, take_next)]
  transfers between devices with their start and end apart: 2 -> 16, of which waited for: 2 -> 11; matrix products, arithmetic and copies ran while one was open for 0% -> 3% of each run, Pallas kernels for 0% -> 0%
where the time goes in v1:
time: 163 us; the launch traced here: 162 us
  waiting for transfers between devices  97.1 us (60%)
  starting transfers between devices  27.3 us (17%)
  Pallas kernels  15.5 us (10%)
  local copies, waits for them, and re-layouts  12.1 us (7%)
  other arithmetic  6.75 us (4%)
  matrix products  2.95 us (2%)
    ppermute x2, waiting for transfers between devices, around(): after = lax.ppermute(block, axis, take_next)  40.5 us
    ppermute x4, waiting for transfers between devices, per_device(): arrived.append(lax.ppermute(piece, ('y', 'z'), perm))  19.9 us
    pallas_call x1, Pallas kernels, products(): pl.pallas_call(functools.partial(products_kernel, steps), grid_spec=pltpu...  15.5 us
    ppermute x2, waiting for transfers between devices, around(): far_low = lax.ppermute(after[:half], axis, take_next)  14.8 us
    ppermute x3, waiting for transfers between devices, per_device(): lax.ppermute(piece.astype(jnp.bfloat16), 'y', [(i, (i + k) % SIDE) for i...  10.9 us
    ppermute x2, waiting for transfers between devices, around(): far_high = lax.ppermute(before[half:], axis, take_prev)  8.55 us
    ppermute x2, starting transfers between devices, around(): far_low = lax.ppermute(after[:half], axis, take_next)  7.18 us
    ppermute x2, starting transfers between devices, around(): after = lax.ppermute(block, axis, take_next)  7.14 us
  transfers between devices with their start and end apart: 16, of which 11 were waited for; matrix products, arithmetic and copies ran while one was open for 3% of the time, Pallas kernels for 0%

profile of v1, /device:TPU:1, one launch (start us, length us, event | category | flops | bytes accessed | tf_op | source)
XLA Modules:
  0.0 162.0 jit_solution(4773274035635119427)
XLA Ops:
  0.7 3.1 %broadcast_multiply_fusion.refs_0_ = bf16[4096,256]{1,0:T(8,128)(2,1)} fusion(bf16[4096,256]{1,0:T(8,128)(2,1)} %param.5, bf16[256]{0:T(256)(128)(2,1)S(1)} %broadcast_bitcast_fusion), kind=kLoop, calls=%fused_computation.3 | loop fusion | flops 1048576 | bytes 4194816 | tf_op jit(solution)/shard_map/mul | solution.py:113
  3.8 2.9 %reshape.72 = bf16[64,16384]{1,0:T(8,128)(2,1)S(1)} reshape(bf16[4096,256]{1,0:T(8,128)(2,1)} %broadcast_multiply_fusion.refs_0_) | data formatting | bytes 4194304 | tf_op jit(solution)/shard_map/reshape | solution.py:27
  12.0 3.4 %collective-permute-start.4 = (bf16[4096,256]{1,0:T(8,128)(2,1)S(1)}, bf16[4096,256]{1,0:T(8,128)(2,1)S(1)}, u32[]{:S(2)}, u32[]{:S(2)}) collective-permute-start(bf16[4096,256]{1,0:T(8,128)(2,1)S(1)} %bitcast.73), channel_id=1, source_target_pairs={{1,0},{2,1},{3,2},{0,3},{5,4},{6,5},{7,6},{4,7},{9,8},{10,9},{11,1... | collective-permute-start | bytes 6291464 | tf_op jit(solution)/shard_map/ppermute | solution.py:103
  15.4 3.8 %collective-permute-start = (bf16[4096,256]{1,0:T(8,128)(2,1)}, bf16[4096,256]{1,0:T(8,128)(2,1)S(1)}, u32[]{:S(2)}, u32[]{:S(2)}) collective-permute-start(bf16[4096,256]{1,0:T(8,128)(2,1)} %broadcast_multiply_fusion.refs_0_), channel_id=1, source_target_pairs={{4,0},{8,4},{12,8},{0,12},{5,1},{9,5},{13,9},{1,13},{6,2},{10,6},{... | collective-permute-start | bytes 6291464 | tf_op jit(solution)/shard_map/ppermute | solution.py:103
  19.1 40.5 %collective-permute-done.4.refs_6_ = bf16[4096,256]{1,0:T(8,128)(2,1)S(1)} collective-permute-done((bf16[4096,256]{1,0:T(8,128)(2,1)S(1)}, bf16[4096,256]{1,0:T(8,128)(2,1)S(1)}, u32[]{:S(2)}, u32[]{:S(2)}) %collective-permute-start.4) | collective-permute-done | bytes 2097184 | tf_op jit(solution)/shard_map/ppermute | solution.py:103
  59.7 1.1 slice.26
  60.8 3.4 %collective-permute-start.6 = (bf16[2048,256]{1,0:T(8,128)(2,1)}, bf16[2048,256]{1,0:T(8,128)(2,1)S(1)}, u32[]{:S(2)}, u32[]{:S(2)}) collective-permute-start(bf16[2048,256]{1,0:T(8,128)(2,1)} %slice.26), channel_id=1, source_target_pairs={{1,0},{2,1},{3,2},{0,3},{5,4},{6,5},{7,6},{4,7},{9,8},{10,9},{11,1... | collective-permute-start | bytes 3145736 | tf_op jit(solution)/shard_map/ppermute | solution.py:105
  65.4 1.2 slice.24
  66.6 3.8 %collective-permute-start.2 = (bf16[2048,256]{1,0:T(8,128)(2,1)}, bf16[2048,256]{1,0:T(8,128)(2,1)S(1)}, u32[]{:S(2)}, u32[]{:S(2)}) collective-permute-start(bf16[2048,256]{1,0:T(8,128)(2,1)} %slice.24), channel_id=1, source_target_pairs={{4,0},{8,4},{12,8},{0,12},{5,1},{9,5},{13,9},{1,13},{6,2},{10,6},{... | collective-permute-start | bytes 3145736 | tf_op jit(solution)/shard_map/ppermute | solution.py:105
  72.2 13.2 %collective-permute-done.6.refs_8_ = bf16[2048,256]{1,0:T(8,128)(2,1)S(1)} collective-permute-done((bf16[2048,256]{1,0:T(8,128)(2,1)}, bf16[2048,256]{1,0:T(8,128)(2,1)S(1)}, u32[]{:S(2)}, u32[]{:S(2)}) %collective-permute-start.6) | collective-permute-done | bytes 1048608 | tf_op jit(solution)/shard_map/ppermute | solution.py:105
  85.4 4.3 %collective-permute-done.7.refs_9_ = bf16[2048,256]{1,0:T(8,128)(2,1)S(1)} collective-permute-done((bf16[2048,256]{1,0:T(8,128)(2,1)}, bf16[2048,256]{1,0:T(8,128)(2,1)S(1)}, u32[]{:S(2)}, u32[]{:S(2)}) %collective-permute-start.7) | collective-permute-done | bytes 1048608 | tf_op jit(solution)/shard_map/ppermute | solution.py:106
  89.7 1.6 collective-permute-done.2.refs_3_
  91.3 4.3 %collective-permute-done.3.refs_4_ = bf16[2048,256]{1,0:T(8,128)(2,1)} collective-permute-done((bf16[2048,256]{1,0:T(8,128)(2,1)}, bf16[2048,256]{1,0:T(8,128)(2,1)}, u32[]{:S(2)}, u32[]{:S(2)}) %collective-permute-start.3) | collective-permute-done | bytes 1048608 | tf_op jit(solution)/shard_map/ppermute | solution.py:106
  95.6 15.5 %shard_map.55 = (f32[2,4,256,256]{3,2,1,0:T(8,128)}, bf16[2,4,256,256]{3,2,1,0:T(8,128)(2,1)}) custom-call(s32[8]{0:T(128)S(1)} %pad_add_fusion.where, bf16[4096,256]{1,0:T(8,128)(2,1)} %broadcast_multiply_fusion.refs_0_, bf16[4096,256]{1,0:T(8,128)(2,1)} %copy-done.3, bf16[4096,256]{1,0:T(8,128)(2,1)} %copy-done.4, ...), custom_call_target="tpu_custom_call" | custom-call | flops 8589934592 | bytes 20971520 | tf_op jit(solution)/shard_map/pallas_call | solution.py:79
  111.1 3.0 %collective-permute-start.8 = (bf16[2,4,256,256]{3,2,1,0:T(8,128)(2,1)}, bf16[2,4,256,256]{3,2,1,0:T(8,128)(2,1)S(1)}, u32[]{:S(2)}, u32[]{:S(2)}) collective-permute-start(bf16[2,4,256,256]{3,2,1,0:T(8,128)(2,1)} %get-tuple-element.8), channel_id=1, source_target_pairs={{0,16},{16,0},{1,17},{17,1},{2,18},{18,2},{3,19},{19,3},{4,20},{20... | collective-permute-start | bytes 3145736 | tf_op jit(solution)/shard_map/ppermute | solution.py:124
  114.1 2.5 %collective-permute-done.8 = bf16[2,4,256,256]{3,2,1,0:T(8,128)(2,1)S(1)} collective-permute-done((bf16[2,4,256,256]{3,2,1,0:T(8,128)(2,1)}, bf16[2,4,256,256]{3,2,1,0:T(8,128)(2,1)S(1)}, u32[]{:S(2)}, u32[]{:S(2)}) %collective-permute-start.8) | collective-permute-done | bytes 1048608 | tf_op jit(solution)/shard_map/ppermute | solution.py:124
  116.6 1.8 %convert_add_fusion = f32[2,4,256,256]{3,2,1,0:T(8,128)S(1)} fusion(f32[2,4,256,256]{3,2,1,0:T(8,128)} %get-tuple-element.7, bf16[2,4,256,256]{3,2,1,0:T(8,128)(2,1)S(1)} %collective-permute-done.8), kind=kLoop, calls=%fused_computation.1 | loop fusion | flops 1048576 | bytes 5242880 | tf_op jit(solution)/shard_map/add | solution.py:124
  118.6 3.0 %collective-permute-start.10 = (bf16[2,4,64,256]{3,2,0,1:T(8,128)(2,1)S(1)}, bf16[2,4,64,256]{3,2,0,1:T(8,128)(2,1)S(1)}, u32[]{:S(2)}, u32[]{:S(2)}) collective-permute-start(bf16[2,4,64,256]{3,2,0,1:T(8,128)(2,1)S(1)} %bitcast.77), channel_id=1, source_target_pairs={{0,64},{32,96},{64,0},{96,32},{1,65},{33,97},{65,1},{97,33},{2,66}... | collective-permute-start | bytes 786440 | tf_op jit(solution)/shard_map/ppermute | solution.py:130
  123.2 4.5 %collective-permute-done.10 = bf16[2,4,64,256]{3,2,0,1:T(8,128)(2,1)S(1)} collective-permute-done((bf16[2,4,64,256]{3,2,0,1:T(8,128)(2,1)S(1)}, bf16[2,4,64,256]{3,2,0,1:T(8,128)(2,1)S(1)}, u32[]{:S(2)}, u32[]{:S(2)}) %collective-permute-start.10) | collective-permute-done | bytes 262176 | tf_op jit(solution)/shard_map/ppermute | solution.py:130
  127.7 6.1 %collective-permute-done.11 = bf16[2,4,64,256]{3,2,0,1:T(8,128)(2,1)S(1)} collective-permute-done((bf16[2,4,64,256]{3,2,0,1:T(8,128)(2,1)S(1)}, bf16[2,4,64,256]{3,2,0,1:T(8,128)(2,1)S(1)}, u32[]{:S(2)}, u32[]{:S(2)}) %collective-permute-start.11) | collective-permute-done | bytes 262176 | tf_op jit(solution)/shard_map/ppermute | solution.py:130
  135.4 3.1 %collective-permute-start.13 = (f32[2,64,256]{2,1,0:T(8,128)S(1)}, f32[2,64,256]{2,1,0:T(8,128)S(1)}, u32[]{:S(2)}, u32[]{:S(2)}) collective-permute-start(f32[2,64,256]{2,1,0:T(8,128)S(1)} %get-tuple-element.14), channel_id=1, source_target_pairs={{0,8},{4,40},{8,72},{12,104},{32,12},{36,44},{40,76},{44,108},{64,... | collective-permute-start | bytes 393224 | tf_op jit(solution)/shard_map/ppermute | solution.py:142
  138.4 1.6 collective-permute-start.14
  140.7 17.1 %collective-permute-done.13 = f32[2,64,256]{2,1,0:T(8,128)S(1)} collective-permute-done((f32[2,64,256]{2,1,0:T(8,128)S(1)}, f32[2,64,256]{2,1,0:T(8,128)S(1)}, u32[]{:S(2)}, u32[]{:S(2)}) %collective-permute-start.13) | collective-permute-done | bytes 131104 | tf_op jit(solution)/shard_map/ppermute | solution.py:142
  157.8 2.8 %collective-permute-done.14 = f32[2,64,256]{2,1,0:T(8,128)S(1)} collective-permute-done((f32[2,64,256]{2,1,0:T(8,128)S(1)}, f32[2,64,256]{2,1,0:T(8,128)S(1)}, u32[]{:S(2)}, u32[]{:S(2)}) %collective-permute-start.14) | collective-permute-done | bytes 131104 | tf_op jit(solution)/shard_map/ppermute | solution.py:142
  (64 shorter events, 14.3 us)
Async XLA Ops:
  3.8 2.9 %copy-start.7 = (s32[1,2]{1,0:T(1,128)S(1)}, s32[1,2]{1,0:T(1,128)}, u32[]{:S(2)}) copy-start(s32[1,2]{1,0:T(1,128)} %param.7) | copy-start | bytes 28
  3.8 3.5 %copy-start.5 = (bf16[16,64,64]{2,1,0:T(8,128)(2,1)S(1)}, bf16[16,64,64]{2,1,0:T(8,128)(2,1)}, u32[]{:S(2)}) copy-start(bf16[16,64,64]{2,1,0:T(8,128)(2,1)} %param.8) | copy-start | bytes 393220
  9.2 1.0 copy-start.6
  12.0 53.4 %copy-start = (bf16[64,64,256]{2,0,1:T(8,128)(2,1)}, bf16[64,64,256]{2,0,1:T(8,128)(2,1)S(1)}, u32[]{:S(2)}) copy-start(bf16[64,64,256]{2,0,1:T(8,128)(2,1)S(1)} %convolution_convert_fusion.1) | copy-start | bytes 6291460
  12.0 47.7 %collective-permute-start.4 = (bf16[4096,256]{1,0:T(8,128)(2,1)S(1)}, bf16[4096,256]{1,0:T(8,128)(2,1)S(1)}, u32[]{:S(2)}, u32[]{:S(2)}) collective-permute-start(bf16[4096,256]{1,0:T(8,128)(2,1)S(1)} %bitcast.73), channel_id=1, source_target_pairs={{1,0},{2,1},{3,2},{0,3},{5,4},{6,5},{7,6},{4,7},{9,8},{10,9},{11,1... | collective-permute-start | bytes 6291464 | tf_op jit(solution)/shard_map/ppermute | solution.py:103
  15.4 48.9 %collective-permute-start.5 = (bf16[4096,256]{1,0:T(8,128)(2,1)S(1)}, bf16[4096,256]{1,0:T(8,128)(2,1)S(1)}, u32[]{:S(2)}, u32[]{:S(2)}) collective-permute-start(bf16[4096,256]{1,0:T(8,128)(2,1)S(1)} %bitcast.74), channel_id=1, source_target_pairs={{3,0},{0,1},{1,2},{2,3},{7,4},{4,5},{5,6},{6,7},{11,8},{8,9},{9,10... | collective-permute-start | bytes 6291464 | tf_op jit(solution)/shard_map/ppermute | solution.py:104
  15.4 50.0 %collective-permute-start = (bf16[4096,256]{1,0:T(8,128)(2,1)}, bf16[4096,256]{1,0:T(8,128)(2,1)S(1)}, u32[]{:S(2)}, u32[]{:S(2)}) collective-permute-start(bf16[4096,256]{1,0:T(8,128)(2,1)} %broadcast_multiply_fusion.refs_0_), channel_id=1, source_target_pairs={{4,0},{8,4},{12,8},{0,12},{5,1},{9,5},{13,9},{1,13},{6,2},{10,6},{... | collective-permute-start | bytes 6291464 | tf_op jit(solution)/shard_map/ppermute | solution.py:103
  19.1 51.2 %collective-permute-start.1 = (bf16[4096,256]{1,0:T(8,128)(2,1)}, bf16[4096,256]{1,0:T(8,128)(2,1)S(1)}, u32[]{:S(2)}, u32[]{:S(2)}) collective-permute-start(bf16[4096,256]{1,0:T(8,128)(2,1)} %broadcast_multiply_fusion.refs_0_), channel_id=1, source_target_pairs={{12,0},{0,4},{4,8},{8,12},{13,1},{1,5},{5,9},{9,13},{14,2},{2,6},{... | collective-permute-start | bytes 6291464 | tf_op jit(solution)/shard_map/ppermute | solution.py:104
  59.7 5.7 %copy-start.1 = (bf16[4096,256]{1,0:T(8,128)(2,1)}, bf16[4096,256]{1,0:T(8,128)(2,1)S(1)}, u32[]{:S(2)}) copy-start(bf16[4096,256]{1,0:T(8,128)(2,1)S(1)} %collective-permute-done.4.refs_6_) | copy-start | bytes 6291460
  60.8 24.6 %collective-permute-start.6 = (bf16[2048,256]{1,0:T(8,128)(2,1)}, bf16[2048,256]{1,0:T(8,128)(2,1)S(1)}, u32[]{:S(2)}, u32[]{:S(2)}) collective-permute-start(bf16[2048,256]{1,0:T(8,128)(2,1)} %slice.26), channel_id=1, source_target_pairs={{1,0},{2,1},{3,2},{0,3},{5,4},{6,5},{7,6},{4,7},{9,8},{10,9},{11,1... | collective-permute-start | bytes 3145736 | tf_op jit(solution)/shard_map/ppermute | solution.py:105
  64.2 7.3 %copy-start.2 = (bf16[4096,256]{1,0:T(8,128)(2,1)}, bf16[4096,256]{1,0:T(8,128)(2,1)S(1)}, u32[]{:S(2)}) copy-start(bf16[4096,256]{1,0:T(8,128)(2,1)S(1)} %collective-permute-done.5.refs_7_) | copy-start | bytes 6291460
  65.4 24.3 %collective-permute-start.7 = (bf16[2048,256]{1,0:T(8,128)(2,1)}, bf16[2048,256]{1,0:T(8,128)(2,1)S(1)}, u32[]{:S(2)}, u32[]{:S(2)}) collective-permute-start(bf16[2048,256]{1,0:T(8,128)(2,1)} %slice.27), channel_id=1, source_target_pairs={{3,0},{0,1},{1,2},{2,3},{7,4},{4,5},{5,6},{6,7},{11,8},{8,9},{9,10... | collective-permute-start | bytes 3145736 | tf_op jit(solution)/shard_map/ppermute | solution.py:106
  65.4 6.2 %copy-start.3 = (bf16[4096,256]{1,0:T(8,128)(2,1)}, bf16[4096,256]{1,0:T(8,128)(2,1)S(1)}, u32[]{:S(2)}) copy-start(bf16[4096,256]{1,0:T(8,128)(2,1)S(1)} %collective-permute-done.refs_1_) | copy-start | bytes 6291460
  66.6 24.7 %collective-permute-start.2 = (bf16[2048,256]{1,0:T(8,128)(2,1)}, bf16[2048,256]{1,0:T(8,128)(2,1)S(1)}, u32[]{:S(2)}, u32[]{:S(2)}) collective-permute-start(bf16[2048,256]{1,0:T(8,128)(2,1)} %slice.24), channel_id=1, source_target_pairs={{4,0},{8,4},{12,8},{0,12},{5,1},{9,5},{13,9},{1,13},{6,2},{10,6},{... | collective-permute-start | bytes 3145736 | tf_op jit(solution)/shard_map/ppermute | solution.py:105
  70.4 1.8 %copy-start.4 = (bf16[4096,256]{1,0:T(8,128)(2,1)}, bf16[4096,256]{1,0:T(8,128)(2,1)S(1)}, u32[]{:S(2)}) copy-start(bf16[4096,256]{1,0:T(8,128)(2,1)S(1)} %collective-permute-done.1.refs_2_) | copy-start | bytes 6291460
  71.5 24.1 %collective-permute-start.3 = (bf16[2048,256]{1,0:T(8,128)(2,1)}, bf16[2048,256]{1,0:T(8,128)(2,1)}, u32[]{:S(2)}, u32[]{:S(2)}) collective-permute-start(bf16[2048,256]{1,0:T(8,128)(2,1)} %slice.25), channel_id=1, source_target_pairs={{12,0},{0,4},{4,8},{8,12},{13,1},{1,5},{5,9},{9,13},{14,2},{2,6},{... | collective-permute-start | bytes 3145736 | tf_op jit(solution)/shard_map/ppermute | solution.py:106
  111.1 5.5 %collective-permute-start.8 = (bf16[2,4,256,256]{3,2,1,0:T(8,128)(2,1)}, bf16[2,4,256,256]{3,2,1,0:T(8,128)(2,1)S(1)}, u32[]{:S(2)}, u32[]{:S(2)}) collective-permute-start(bf16[2,4,256,256]{3,2,1,0:T(8,128)(2,1)} %get-tuple-element.8), channel_id=1, source_target_pairs={{0,16},{16,0},{1,17},{17,1},{2,18},{18,2},{3,19},{19,3},{4,20},{20... | collective-permute-start | bytes 3145736 | tf_op jit(solution)/shard_map/ppermute | solution.py:124
  118.6 9.1 %collective-permute-start.10 = (bf16[2,4,64,256]{3,2,0,1:T(8,128)(2,1)S(1)}, bf16[2,4,64,256]{3,2,0,1:T(8,128)(2,1)S(1)}, u32[]{:S(2)}, u32[]{:S(2)}) collective-permute-start(bf16[2,4,64,256]{3,2,0,1:T(8,128)(2,1)S(1)} %bitcast.77), channel_id=1, source_target_pairs={{0,64},{32,96},{64,0},{96,32},{1,65},{33,97},{65,1},{97,33},{2,66}... | collective-permute-start | bytes 786440 | tf_op jit(solution)/shard_map/ppermute | solution.py:130
  121.6 12.2 %collective-permute-start.11 = (bf16[2,4,64,256]{3,2,0,1:T(8,128)(2,1)S(1)}, bf16[2,4,64,256]{3,2,0,1:T(8,128)(2,1)S(1)}, u32[]{:S(2)}, u32[]{:S(2)}) collective-permute-start(bf16[2,4,64,256]{3,2,0,1:T(8,128)(2,1)S(1)} %bitcast.78), channel_id=1, source_target_pairs={{0,96},{32,0},{64,32},{96,64},{1,97},{33,1},{65,33},{97,65},{2,98}... | collective-permute-start | bytes 786440 | tf_op jit(solution)/shard_map/ppermute | solution.py:130
  122.5 11.7 %collective-permute-start.9 = (bf16[2,4,64,256]{3,2,0,1:T(8,128)(2,1)S(1)}, bf16[2,4,64,256]{3,2,0,1:T(8,128)(2,1)}, u32[]{:S(2)}, u32[]{:S(2)}) collective-permute-start(bf16[2,4,64,256]{3,2,0,1:T(8,128)(2,1)S(1)} %bitcast.79), channel_id=1, source_target_pairs={{0,32},{32,64},{64,96},{96,0},{1,33},{33,65},{65,97},{97,1},{2,34}... | collective-permute-start | bytes 786440 | tf_op jit(solution)/shard_map/ppermute | solution.py:130
  135.3 5.4 %collective-permute-start.12 = (f32[2,64,256]{2,1,0:T(8,128)S(1)}, f32[2,64,256]{2,1,0:T(8,128)S(1)}, u32[]{:S(2)}, u32[]{:S(2)}) collective-permute-start(f32[2,64,256]{2,1,0:T(8,128)S(1)} %get-tuple-element.15), channel_id=1, source_target_pairs={{0,12},{4,44},{8,76},{12,108},{32,0},{36,32},{40,64},{44,96},{64,4... | collective-permute-start | bytes 393224 | tf_op jit(solution)/shard_map/ppermute | solution.py:142
  135.4 22.4 %collective-permute-start.13 = (f32[2,64,256]{2,1,0:T(8,128)S(1)}, f32[2,64,256]{2,1,0:T(8,128)S(1)}, u32[]{:S(2)}, u32[]{:S(2)}) collective-permute-start(f32[2,64,256]{2,1,0:T(8,128)S(1)} %get-tuple-element.14), channel_id=1, source_target_pairs={{0,8},{4,40},{8,72},{12,104},{32,12},{36,44},{40,76},{44,108},{64,... | collective-permute-start | bytes 393224 | tf_op jit(solution)/shard_map/ppermute | solution.py:142
  138.4 22.2 %collective-permute-start.14 = (f32[2,64,256]{2,1,0:T(8,128)S(1)}, f32[2,64,256]{2,1,0:T(8,128)S(1)}, u32[]{:S(2)}, u32[]{:S(2)}) collective-permute-start(f32[2,64,256]{2,1,0:T(8,128)S(1)} %get-tuple-element.13), channel_id=1, source_target_pairs={{0,4},{4,36},{8,68},{12,100},{32,8},{36,40},{40,72},{44,104},{64,1... | collective-permute-start | bytes 393224 | tf_op jit(solution)/shard_map/ppermute | solution.py:142
  140.0 20.6 %collective-permute-start.15 = (f32[2,64,256]{2,1,0:T(8,128)S(1)}, f32[2,64,256]{2,1,0:T(8,128)S(1)}, u32[]{:S(2)}, u32[]{:S(2)}) collective-permute-start(f32[2,64,256]{2,1,0:T(8,128)S(1)} %get-tuple-element.12), channel_id=1, source_target_pairs={{0,0},{4,32},{8,64},{12,96},{32,4},{36,36},{40,68},{44,100},{64,8}... | collective-permute-start | bytes 393224 | tf_op jit(solution)/shard_map/ppermute | solution.py:142

commit v2 on v1

v2 whole, which is shorter than its diff:
```python
import functools

import jax
import jax.numpy as jnp
from jax import lax
from jax.experimental import pallas as pl
from jax.experimental.pallas import tpu as pltpu
from jax.sharding import Mesh, PartitionSpec as P

SIDE = 4
BLOCK = 256
HALF = BLOCK // 2
NEAR = (0, 1, 3)
LATE = tuple((2, q) for q in NEAR + (2,)) + tuple((p, 2) for p in NEAR)
F32 = jnp.float32
BF16 = jnp.bfloat16


def iota(shape, dim):
    return lax.broadcasted_iota(jnp.int32, shape, dim)


def contract_kernel(width, group, scalars, tiles_ref, occ_ref, virt_ref, out_ref, half_ref):
    cols = tiles_ref.shape[1]
    tall = width * group
    spread = jnp.where(iota((tall, width), 0) // group == iota((tall, width), 1), 1.0, 0.0).astype(BF16)
    rows = jnp.dot(spread, occ_ref[0], preferred_element_type=F32).astype(BF16)
    wide = lax.dot_general(
        rows, spread, (((1,), (1,)), ((), ())), preferred_element_type=F32
    )
    same = (iota((tall, tall), 0) % group) == (iota((tall, tall), 1) % group)
    occ_wide = jnp.where(same, wide, 0.0).astype(BF16)
    four = 4
    side = four * width
    repeat = jnp.where(iota((side, width), 0) % width == iota((side, width), 1), 1.0, 0.0).astype(BF16)
    rows = jnp.dot(repeat, virt_ref[0], preferred_element_type=F32).astype(BF16)
    wide = lax.dot_general(
        rows, repeat, (((1,), (1,)), ((), ())), preferred_element_type=F32
    )
    same = (iota((side, side), 0) // width) == (iota((side, side), 1) // width)
    virt_wide = jnp.where(same, wide, 0.0).astype(BF16)

    tiles = tiles_ref.reshape(width, width, cols)
    for t in range(width // group):
        part = tiles[:, t * group : (t + 1) * group, :].reshape(tall, cols)
        half = jnp.dot(occ_wide, part, preferred_element_type=F32).astype(BF16)
        half_ref[:, t * group : (t + 1) * group, :] = half.reshape(width, group, cols)
    weight = jnp.where(iota((1, cols), 1) < HALF, scalars[2], scalars[3]).astype(F32)
    for g in range(width // four):
        part = half_ref[g * four : (g + 1) * four].reshape(side, cols)
        done = jnp.dot(virt_wide, part, preferred_element_type=F32) * weight
        out_ref[g * side : (g + 1) * side, :] = done.astype(BF16)


def contract(scalars, three_centre, green_occ, green_virt):
    width = green_occ.shape[1]
    rows, cols = three_centre.shape
    whole = pl.BlockSpec((rows, cols), lambda i, s: (0, 0))
    return pl.pallas_call(
        functools.partial(contract_kernel, width, 16),
        grid_spec=pltpu.PrefetchScalarGridSpec(
            num_scalar_prefetch=1,
            grid=(1,),
            in_specs=[
                whole,
                pl.BlockSpec((1, width, width), lambda i, s: (s[0], 0, 0)),
                pl.BlockSpec((1, width, width), lambda i, s: (s[1], 0, 0)),
            ],
            out_specs=whole,
            scratch_shapes=[pltpu.VMEM((width, width, cols), BF16)],
        ),
        out_shape=jax.ShapeDtypeStruct((rows, cols), BF16),
        compiler_params=pltpu.CompilerParams(vmem_limit_bytes=40 * 2**20),
        cost_estimate=pl.CostEstimate(
            flops=40 * 10**9, bytes_accessed=4 * 2**20, transcendentals=0
        ),
    )(scalars, three_centre, green_occ, green_virt)


def products_kernel(steps, pairs, has_far, scalars, *refs):
    per_side = 5 if has_far else 3
    a_refs, b_refs = refs[:per_side], refs[per_side : 2 * per_side]
    keep_ref, send_ref, acc = refs[2 * per_side :]
    k = pl.program_id(0)
    core = scalars[4]

    @pl.when(k == 0)
    def _():
        acc[...] = jnp.zeros_like(acc)

    def block(blocks, offset):
        if offset == 2:
            return jnp.where(k < steps // 2, blocks[3][...], blocks[4][...])
        return blocks[NEAR.index(offset)][...]

    rights = {q: block(b_refs, q) for q in sorted({q for _, q in pairs})}
    for p in sorted({p for p, _ in pairs}):
        left = block(a_refs, p).T
        for i, (task_p, q) in enumerate(pairs):
            if task_p == p:
                acc[i] += jnp.dot(left, rights[q], preferred_element_type=F32)

    @pl.when(k == steps - 1)
    def _():
        for i, (p, _) in enumerate(pairs):
            for half in range(2):
                rows = pl.ds(half * HALF, HALF)
                acc[i, rows, :] = acc[i, rows, :] * scalars[8 + 2 * p + half].astype(F32)
            keep_ref[i] = acc[i, pl.ds(pl.multiple_of(core * HALF, HALF), HALF), :]
            other = pl.ds(pl.multiple_of((1 - core) * HALF, HALF), HALF)
            send_ref[i] = acc[i, other, :].astype(BF16)


def products(scalars, lefts, rights, pairs):
    rows = lefts[0].shape[0]
    chunk = 1024
    steps = rows // chunk
    has_far = len(lefts) == 5
    specs = [pl.BlockSpec((chunk, BLOCK), lambda k, s: (k, 0))] * 3
    if has_far:
        specs.append(
            pl.BlockSpec((chunk, BLOCK), lambda k, s: (jnp.minimum(k, steps // 2 - 1), 0))
        )
        specs.append(
            pl.BlockSpec((chunk, BLOCK), lambda k, s: (jnp.maximum(k - steps // 2, 0), 0))
        )
    count = len(pairs)
    out = pl.BlockSpec((count, HALF, BLOCK), lambda k, s: (0, 0, 0))
    return pl.pallas_call(
        functools.partial(products_kernel, steps, pairs, has_far),
        grid_spec=pltpu.PrefetchScalarGridSpec(
            num_scalar_prefetch=1,
            grid=(steps,),
            in_specs=specs + specs,
            out_specs=[out, out],
            scratch_shapes=[pltpu.VMEM((count, BLOCK, BLOCK), F32)],
        ),
        out_shape=[
            jax.ShapeDtypeStruct((count, HALF, BLOCK), F32),
            jax.ShapeDtypeStruct((count, HALF, BLOCK), BF16),
        ],
        compiler_params=pltpu.CompilerParams(vmem_limit_bytes=48 * 2**20),
        cost_estimate=pl.CostEstimate(
            flops=2 * count * rows * BLOCK * BLOCK, bytes_accessed=20 * 2**20, transcendentals=0
        ),
    )(scalars, *lefts, *rights)


def merge_kernel(near, far, scalars, *refs):
    keep_near, got_near, keep_far, got_far = refs[:4]
    out_refs = refs[4:]
    own_ref, send_refs = out_refs[0], out_refs[1:]

    for pairs, keep, got in ((near, keep_near, got_near), (far, keep_far, got_far)):
        for i, (p, q) in enumerate(pairs):
            total = keep[i] + got[i].astype(F32)
            target = scalars[16 + q]
            row = scalars[20 + p]

            @pl.when(target == 0)
            def _():
                own_ref[row] = total

            for step in range(1, SIDE):

                @pl.when(target == step)
                def _():
                    send_refs[step - 1][row] = total.astype(BF16)


def merge(scalars, near, far, keep_near, got_near, keep_far, got_far):
    shape = (SIDE, HALF, BLOCK)
    spec = lambda n: pl.BlockSpec((n, HALF, BLOCK), lambda i, s: (0, 0, 0))
    return pl.pallas_call(
        functools.partial(merge_kernel, near, far),
        grid_spec=pltpu.PrefetchScalarGridSpec(
            num_scalar_prefetch=1,
            grid=(1,),
            in_specs=[spec(len(near))] * 2 + [spec(len(far))] * 2,
            out_specs=[spec(SIDE)] * 4,
        ),
        out_shape=[jax.ShapeDtypeStruct(shape, F32)] + [jax.ShapeDtypeStruct(shape, BF16)] * 3,
        compiler_params=pltpu.CompilerParams(vmem_limit_bytes=32 * 2**20),
        cost_estimate=pl.CostEstimate(flops=2**20, bytes_accessed=5 * 2**20, transcendentals=0),
    )(scalars, keep_near, got_near, keep_far, got_far)


def ring(block, axis):
    take_next = [((i + 1) % SIDE, i) for i in range(SIDE)]
    take_prev = [((i - 1) % SIDE, i) for i in range(SIDE)]
    return lax.ppermute(block, axis, take_next), lax.ppermute(block, axis, take_prev)


def far(after, before, axis):
    half = after.shape[0] // 2
    take_next = [((i + 1) % SIDE, i) for i in range(SIDE)]
    take_prev = [((i - 1) % SIDE, i) for i in range(SIDE)]
    return (
        lax.ppermute(after[:half], axis, take_next),
        lax.ppermute(before[half:], axis, take_prev),
    )


def per_device(three_centre, tile_list, pair_blocks, green_occ, green_virt):
    y, c, z, x = (lax.axis_index(name) for name in ("y", "c", "z", "x"))
    offsets = jnp.arange(SIDE)
    a_after, a_before = ring(three_centre, "x")
    own = contract(
        jnp.concatenate([pair_blocks[0], tile_list[0]]), three_centre, green_occ, green_virt
    )
    b_after, b_before = ring(own, "z")
    listed, own = lax.optimization_barrier((tile_list, own))
    row_weights = lax.all_gather(listed[0], "x")
    row_weights = jnp.take(row_weights, (x + offsets) & 3, axis=0).reshape(-1)
    first = 2 * (x & 1) + c
    scalars = jnp.concatenate(
        [
            jnp.stack([y, z, x, c, c, c, c, c]),
            row_weights,
            (z + offsets - y) & 3,
            (x + offsets - first) & 3,
        ]
    ).astype(jnp.int32)

    near = tuple((p, q) for p in NEAR for q in NEAR)
    lefts, rights = [three_centre, a_after, a_before], [own, b_after, b_before]
    keep_near, send_near = products(scalars, lefts, rights, near)
    lefts += far(a_after, a_before, "x")
    rights += far(b_after, b_before, "z")
    swap = [(0, 1), (1, 0)]
    got_near = lax.ppermute(send_near, "c", swap)
    keep_far, send_far = products(scalars, lefts, rights, LATE)
    got_far = lax.ppermute(send_far, "c", swap)

    own, *sends = merge(scalars, near, LATE, keep_near, got_near, keep_far, got_far)
    for k in range(1, SIDE):
        moved = lax.ppermute(sends[k - 1], "y", [(i, (i + k) % SIDE) for i in range(SIDE)])
        own = own + moved.astype(F32)
    own = -2.0 * own

    arrived = []
    for k in range(SIDE):
        perm = [
            (core * SIDE + i, (i // 2) * SIDE + (2 * (i % 2) + core + k) % SIDE)
            for core in range(2)
            for i in range(SIDE)
        ]
        arrived.append(lax.ppermute(own[k], ("c", "x"), perm))
    stacked = jnp.stack(arrived[::-1] + arrived[:0:-1])
    ordered = lax.dynamic_slice_in_dim(stacked, (SIDE - 1 - x) & 3, SIDE, 0)
    ordered = ordered.reshape(2, 2, HALF, BLOCK)
    return ordered.transpose(1, 2, 0, 3).reshape(BLOCK, 2 * BLOCK)


def solution(mesh):
    fine = Mesh(mesh.devices.reshape(SIDE, 2, SIDE, SIDE), ("y", "c", "z", "x"))
    ao, aux = ("y", "c"), ("z", "x")
    return jax.shard_map(
        per_device,
        mesh=fine,
        in_specs=(P(ao, aux), P(ao, aux), P(ao, None), P(), P()),
        out_specs=P(aux, ao),
        check_vma=False,
    )
```

time: 163 us -> 157 us (0.963)
  waiting for transfers between devices: 97.1 us -> 61.2 us
  blocking collectives: 0 us -> 25 us
  Pallas kernels: 15.5 us -> 25.9 us
  other arithmetic: 6.75 us -> 0.97 us
  starting transfers between devices: 27.3 us -> 31.8 us
  matrix products: 2.95 us -> 0 us
    ppermute x16 -> x17, waiting for transfers between devices: 97.1 us -> 61.2 us  [the longest x2 43 us: ring(): lax.ppermute(block, axis, take_prev)]
    all_gather x0 -> x1, blocking collectives: none -> 25 us  [per_device(): row_weights = lax.all_gather(listed[0], 'x')]
    pallas_call x1 -> x4, Pallas kernels: 15.5 us -> 25.9 us  [the longest x2 17.7 us: products(): pl.pallas_call(functools.partial(products_kernel, steps, pairs, has_far),...]
    ppermute x16 -> x17, starting transfers between devices: 27.3 us -> 31.8 us  [the longest x4 10 us: per_device(): arrived.append(lax.ppermute(own[k], ('c', 'x'), perm))]
    reshape x3 -> x0, local copies, waits for them, and re-layouts: 3.46 us -> none  [the longest x1 2.92 us: contract(): tiles.reshape(width, width * cols)]
    mul x1 -> x0, other arithmetic: 3.07 us -> none  [per_device(): tiles = three_centre * weights[None, :]]
    dot_general x4 -> x0, matrix products: 2.95 us -> none  [the longest x2 1.56 us: pick_blocks(): jnp.dot(onehot, table.reshape(blocks_total, width * width), preferred_ele...]
    slice x5 -> x4, local copies, waits for them, and re-layouts: 5.22 us -> 7.96 us  [the longest x2 4.56 us: far(): before[half:]]
  transfers between devices with their start and end apart: 16 -> 17, of which waited for: 11 -> 5; matrix products, arithmetic and copies ran while one was open for 3% -> 6% of each run, Pallas kernels for 0% -> 11%
where the time goes in v2:
time: 157 us
  waiting for transfers between devices  61.2 us (39%)
  starting transfers between devices  31.8 us (20%)
  Pallas kernels  25.9 us (16%)
  blocking collectives  25 us (16%)
  local copies, waits for them, and re-layouts  12 us (8%)
    ppermute x2, waiting for transfers between devices, ring(): lax.ppermute(block, axis, take_prev)  43 us
    all_gather x1, blocking collectives, per_device(): row_weights = lax.all_gather(listed[0], 'x')  25 us
    pallas_call x2, Pallas kernels, products(): pl.pallas_call(functools.partial(products_kernel, steps, pairs, has_far),...  17.7 us
    ppermute x3, waiting for transfers between devices, per_device(): lax.ppermute(sends[k - 1], 'y', [(i, (i + k) % SIDE) for i in range(SIDE)])  10.9 us
    ppermute x4, starting transfers between devices, per_device(): arrived.append(lax.ppermute(own[k], ('c', 'x'), perm))  10 us
    pallas_call x1, Pallas kernels, contract(): pl.pallas_call(functools.partial(contract_kernel, width, 16), grid_spec=p...  7.14 us
    ppermute x4, waiting for transfers between devices, per_device(): arrived.append(lax.ppermute(own[k], ('c', 'x'), perm))  5.57 us
    ppermute x3, starting transfers between devices, per_device(): lax.ppermute(sends[k - 1], 'y', [(i, (i + k) % SIDE) for i in range(SIDE)])  5.06 us
  transfers between devices with their start and end apart: 17, of which 5 were waited for; matrix products, arithmetic and copies ran while one was open for 6% of the time, Pallas kernels for 11%

profile of v2, /device:TPU:1, one launch (start us, length us, event | category | flops | bytes accessed | tf_op | source)
XLA Modules:
  0.0 157.0 jit_solution(9824551097976073876)
XLA Ops:
  2.6 7.1 %shard_map.55.refs_3_.refs_5_ = bf16[4096,256]{1,0:T(8,128)(2,1)} custom-call(s32[4]{0:T(128)S(1)} %pad_add_fusion.scalars, bf16[4096,256]{1,0:T(8,128)(2,1)} %refs_0_.3, bf16[16,64,64]{2,1,0:T(8,128)(2,1)S(1)} %copy-done.1, bf16[16,64,64]{2,1,0:T(8,128)(2,1)S(1)} %copy-done.2), custom_call_target="tpu_custom_call" | custom-call | flops 40000000000 | bytes 4194304 | tf_op jit(solution)/shard_map/pallas_call | solution.py:59
  9.8 2.5 %collective-permute-start.3 = (bf16[4096,256]{1,0:T(8,128)(2,1)}, bf16[4096,256]{1,0:T(8,128)(2,1)}, u32[]{:S(2)}, u32[]{:S(2)}) collective-permute-start(bf16[4096,256]{1,0:T(8,128)(2,1)} %shard_map.55.refs_3_.refs_5_), channel_id=1, source_target_pairs={{12,0},{0,4},{4,8},{8,12},{13,1},{1,5},{5,9},{9,13},{14,2},{2,6},{... | collective-permute-start | bytes 6291464 | tf_op jit(solution)/shard_map/ppermute | solution.py:191
  12.3 2.1 %collective-permute-start.2 = (bf16[4096,256]{1,0:T(8,128)(2,1)}, bf16[4096,256]{1,0:T(8,128)(2,1)}, u32[]{:S(2)}, u32[]{:S(2)}) collective-permute-start(bf16[4096,256]{1,0:T(8,128)(2,1)} %shard_map.55.refs_3_.refs_5_), channel_id=1, source_target_pairs={{4,0},{8,4},{12,8},{0,12},{5,1},{9,5},{13,9},{1,13},{6,2},{10,6},{... | collective-permute-start | bytes 6291464 | tf_op jit(solution)/shard_map/ppermute | solution.py:191
  15.6 1.5 collective-permute-start
  17.1 43.0 %collective-permute-done.3.refs_5_.refs_7_ = bf16[4096,256]{1,0:T(8,128)(2,1)} collective-permute-done((bf16[4096,256]{1,0:T(8,128)(2,1)}, bf16[4096,256]{1,0:T(8,128)(2,1)}, u32[]{:S(2)}, u32[]{:S(2)}) %collective-permute-start.3) | collective-permute-done | bytes 2097184 | tf_op jit(solution)/shard_map/ppermute | solution.py:191
  60.0 2.3 %slice.37 = bf16[2048,256]{1,0:T(8,128)(2,1)} slice(bf16[4096,256]{1,0:T(8,128)(2,1)} %collective-permute-done.3.refs_5_.refs_7_), slice={[2048:4096], [0:256]} | slice | bytes 2097152 | tf_op jit(solution)/shard_map/slice | solution.py:200
  62.3 2.3 %slice.36 = bf16[2048,256]{1,0:T(8,128)(2,1)} slice(bf16[4096,256]{1,0:T(8,128)(2,1)} %collective-permute-done.2.refs_4_.refs_6_), slice={[0:2048], [0:256]} | slice | bytes 2097152 | tf_op jit(solution)/shard_map/slice | solution.py:199
  64.6 2.7 %collective-permute-start.7 = (bf16[2048,256]{1,0:T(8,128)(2,1)}, bf16[2048,256]{1,0:T(8,128)(2,1)}, u32[]{:S(2)}, u32[]{:S(2)}) collective-permute-start(bf16[2048,256]{1,0:T(8,128)(2,1)} %slice.36), channel_id=1, source_target_pairs={{4,0},{8,4},{12,8},{0,12},{5,1},{9,5},{13,9},{1,13},{6,2},{10,6},{... | collective-permute-start | bytes 3145736 | tf_op jit(solution)/shard_map/ppermute | solution.py:199
  67.3 2.3 %slice.35 = bf16[2048,256]{1,0:T(8,128)(2,1)} slice(bf16[4096,256]{1,0:T(8,128)(2,1)} %collective-permute-done.1.refs_2_), slice={[2048:4096], [0:256]} | slice | bytes 2097152 | tf_op jit(solution)/shard_map/slice | solution.py:200
  69.6 1.2 collective-permute-start.6
  71.9 1.5 collective-permute-start.5
  73.4 25.0 %all-gather = s32[4,1,2]{2,1,0:T(1,128)S(1)} all-gather(s32[1,1,2]{2,1,0:T(1,128)S(1)} %bitcast.39), channel_id=1, replica_groups=mesh['y'=4,'c'=2,'z'=4,'x'=4] {'x'}, dimensions={0}, use_global_device_ids=true | all-gather | bytes 40 | tf_op jit(solution)/shard_map/all_gather | solution.py:213
  99.2 8.8 %shard_map.56 = (f32[9,128,256]{2,1,0:T(8,128)S(1)}, bf16[9,128,256]{2,1,0:T(8,128)(2,1)S(1)}) custom-call(s32[24]{0:T(128)S(1)} %concatenate.7.scalars, bf16[4096,256]{1,0:T(8,128)(2,1)} %refs_0_.3, bf16[4096,256]{1,0:T(8,128)(2,1)S(1)} %collective-permute-done.refs_1_, bf16[4096,256]{1,0:T(8,128)(2,1)} %collective-permute-done.1.refs_2_, ...), custom_call_target="tpu_custom_call" | custom-call | flops 4831838208 | bytes 20971520 | tf_op jit(solution)/shard_map/pallas_call | solution.py:129
  108.0 4.0 %collective-permute-start.4 = (bf16[9,128,256]{2,1,0:T(8,128)(2,1)S(1)}, bf16[9,128,256]{2,1,0:T(8,128)(2,1)S(1)}, u32[]{:S(2)}, u32[]{:S(2)}) collective-permute-start(bf16[9,128,256]{2,1,0:T(8,128)(2,1)S(1)} %get-tuple-element.18), channel_id=1, source_target_pairs={{0,16},{16,0},{1,17},{17,1},{2,18},{18,2},{3,19},{19,3},{4,20},{20... | collective-permute-start | bytes 1769480 | tf_op jit(solution)/shard_map/ppermute | solution.py:231
  112.0 9.0 %shard_map.57 = (f32[7,128,256]{2,1,0:T(8,128)S(1)}, bf16[7,128,256]{2,1,0:T(8,128)(2,1)S(1)}) custom-call(s32[24]{0:T(128)S(1)} %concatenate.7.scalars, bf16[4096,256]{1,0:T(8,128)(2,1)} %refs_0_.3, bf16[4096,256]{1,0:T(8,128)(2,1)} %copy-done, bf16[4096,256]{1,0:T(8,128)(2,1)} %collective-permute-done.1.refs_2_, ...), custom_call_target="tpu_custom_call" | custom-call | flops 3758096384 | bytes 20971520 | tf_op jit(solution)/shard_map/pallas_call | solution.py:129
  121.1 1.8 %collective-permute-done.9.refs_3_ = bf16[7,128,256]{2,1,0:T(8,128)(2,1)S(1)} collective-permute-done((bf16[7,128,256]{2,1,0:T(8,128)(2,1)S(1)}, bf16[7,128,256]{2,1,0:T(8,128)(2,1)S(1)}, u32[]{:S(2)}, u32[]{:S(2)}) %collective-permute-start.9) | collective-permute-done | bytes 458784 | tf_op jit(solution)/shard_map/ppermute | solution.py:233
  123.9 1.4 collective-permute-start.10
  125.2 2.6 %collective-permute-start.11 = (bf16[4,128,256]{2,1,0:T(8,128)(2,1)S(1)}, bf16[4,128,256]{2,1,0:T(8,128)(2,1)S(1)}, u32[]{:S(2)}, u32[]{:S(2)}) collective-permute-start(bf16[4,128,256]{2,1,0:T(8,128)(2,1)S(1)} %get-tuple-element.23), channel_id=1, source_target_pairs={{0,64},{32,96},{64,0},{96,32},{1,65},{33,97},{65,1},{97,33},{2,66}... | collective-permute-start | bytes 786440 | tf_op jit(solution)/shard_map/ppermute | solution.py:237
  128.9 4.1 %collective-permute-done.10 = bf16[4,128,256]{2,1,0:T(8,128)(2,1)S(1)} collective-permute-done((bf16[4,128,256]{2,1,0:T(8,128)(2,1)S(1)}, bf16[4,128,256]{2,1,0:T(8,128)(2,1)S(1)}, u32[]{:S(2)}, u32[]{:S(2)}) %collective-permute-start.10) | collective-permute-done | bytes 262176 | tf_op jit(solution)/shard_map/ppermute | solution.py:237
  133.1 6.7 %collective-permute-done.11 = bf16[4,128,256]{2,1,0:T(8,128)(2,1)S(1)} collective-permute-done((bf16[4,128,256]{2,1,0:T(8,128)(2,1)S(1)}, bf16[4,128,256]{2,1,0:T(8,128)(2,1)S(1)}, u32[]{:S(2)}, u32[]{:S(2)}) %collective-permute-start.11) | collective-permute-done | bytes 262176 | tf_op jit(solution)/shard_map/ppermute | solution.py:237
  139.9 2.9 %collective-permute-start.13 = (f32[128,256]{1,0:T(8,128)S(1)}, f32[128,256]{1,0:T(8,128)S(1)}, u32[]{:S(2)}, u32[]{:S(2)}) collective-permute-start(f32[128,256]{1,0:T(8,128)S(1)} %get-tuple-element.28), channel_id=1, source_target_pairs={{0,3},{1,1},{2,19},{3,17},{16,0},{17,2},{18,16},{19,18},{4,7},{5,5... | collective-permute-start | bytes 393224 | tf_op jit(solution)/shard_map/ppermute | solution.py:248
  142.8 1.9 %collective-permute-start.16 = (f32[128,256]{1,0:T(8,128)S(1)}, f32[128,256]{1,0:T(8,128)S(1)}, u32[]{:S(2)}, u32[]{:S(2)}) collective-permute-start(f32[128,256]{1,0:T(8,128)S(1)} %get-tuple-element.25), channel_id=1, source_target_pairs={{0,0},{1,2},{2,16},{3,18},{16,1},{17,3},{18,17},{19,19},{4,4},{5,6... | collective-permute-start | bytes 393224 | tf_op jit(solution)/shard_map/ppermute | solution.py:248
  144.8 5.1 %collective-permute-start.15 = (f32[128,256]{1,0:T(8,128)S(1)}, f32[128,256]{1,0:T(8,128)S(1)}, u32[]{:S(2)}, u32[]{:S(2)}) collective-permute-start(f32[128,256]{1,0:T(8,128)S(1)} %get-tuple-element.26), channel_id=1, source_target_pairs={{0,1},{1,3},{2,17},{3,19},{16,2},{17,0},{18,18},{19,16},{4,5},{5,7... | collective-permute-start | bytes 393224 | tf_op jit(solution)/shard_map/ppermute | solution.py:248
  150.0 5.6 %collective-permute-done.14 = f32[128,256]{1,0:T(8,128)S(1)} collective-permute-done((f32[128,256]{1,0:T(8,128)S(1)}, f32[128,256]{1,0:T(8,128)S(1)}, u32[]{:S(2)}, u32[]{:S(2)}) %collective-permute-start.14) | collective-permute-done | bytes 131104 | tf_op jit(solution)/shard_map/ppermute | solution.py:248
  (48 shorter events, 9.6 us)
Async XLA Ops:
  0.7 0.9 copy-start.1
  1.7 0.9 copy-start.2
  9.8 50.2 %collective-permute-start.3 = (bf16[4096,256]{1,0:T(8,128)(2,1)}, bf16[4096,256]{1,0:T(8,128)(2,1)}, u32[]{:S(2)}, u32[]{:S(2)}) collective-permute-start(bf16[4096,256]{1,0:T(8,128)(2,1)} %shard_map.55.refs_3_.refs_5_), channel_id=1, source_target_pairs={{12,0},{0,4},{4,8},{8,12},{13,1},{1,5},{5,9},{9,13},{14,2},{2,6},{... | collective-permute-start | bytes 6291464 | tf_op jit(solution)/shard_map/ppermute | solution.py:191
  12.3 50.1 %collective-permute-start.2 = (bf16[4096,256]{1,0:T(8,128)(2,1)}, bf16[4096,256]{1,0:T(8,128)(2,1)}, u32[]{:S(2)}, u32[]{:S(2)}) collective-permute-start(bf16[4096,256]{1,0:T(8,128)(2,1)} %shard_map.55.refs_3_.refs_5_), channel_id=1, source_target_pairs={{4,0},{8,4},{12,8},{0,12},{5,1},{9,5},{13,9},{1,13},{6,2},{10,6},{... | collective-permute-start | bytes 6291464 | tf_op jit(solution)/shard_map/ppermute | solution.py:191
  14.4 52.9 %collective-permute-start.1 = (bf16[4096,256]{1,0:T(8,128)(2,1)}, bf16[4096,256]{1,0:T(8,128)(2,1)}, u32[]{:S(2)}, u32[]{:S(2)}) collective-permute-start(bf16[4096,256]{1,0:T(8,128)(2,1)} %refs_0_.3), channel_id=1, source_target_pairs={{3,0},{0,1},{1,2},{2,3},{7,4},{4,5},{5,6},{6,7},{11,8},{8,9},{9,10... | collective-permute-start | bytes 6291464 | tf_op jit(solution)/shard_map/ppermute | solution.py:191
  15.6 55.2 %collective-permute-start = (bf16[4096,256]{1,0:T(8,128)(2,1)}, bf16[4096,256]{1,0:T(8,128)(2,1)S(1)}, u32[]{:S(2)}, u32[]{:S(2)}) collective-permute-start(bf16[4096,256]{1,0:T(8,128)(2,1)} %refs_0_.3), channel_id=1, source_target_pairs={{1,0},{2,1},{3,2},{0,3},{5,4},{6,5},{7,6},{4,7},{9,8},{10,9},{11,1... | collective-permute-start | bytes 6291464 | tf_op jit(solution)/shard_map/ppermute | solution.py:191
  62.3 49.6 %collective-permute-start.8 = (bf16[2048,256]{1,0:T(8,128)(2,1)}, bf16[2048,256]{1,0:T(8,128)(2,1)S(1)}, u32[]{:S(2)}, u32[]{:S(2)}) collective-permute-start(bf16[2048,256]{1,0:T(8,128)(2,1)} %slice.37), channel_id=1, source_target_pairs={{12,0},{0,4},{4,8},{8,12},{13,1},{1,5},{5,9},{9,13},{14,2},{2,6},{... | collective-permute-start | bytes 3145736 | tf_op jit(solution)/shard_map/ppermute | solution.py:200
  64.6 8.8 %copy-start.3 = (s32[1,2]{1,0:T(1,128)S(1)}, s32[1,2]{1,0:T(1,128)}, u32[]{:S(2)}) copy-start(s32[1,2]{1,0:T(1,128)} %param.6) | copy-start | bytes 28
  64.6 47.4 %collective-permute-start.7 = (bf16[2048,256]{1,0:T(8,128)(2,1)}, bf16[2048,256]{1,0:T(8,128)(2,1)}, u32[]{:S(2)}, u32[]{:S(2)}) collective-permute-start(bf16[2048,256]{1,0:T(8,128)(2,1)} %slice.36), channel_id=1, source_target_pairs={{4,0},{8,4},{12,8},{0,12},{5,1},{9,5},{13,9},{1,13},{6,2},{10,6},{... | collective-permute-start | bytes 3145736 | tf_op jit(solution)/shard_map/ppermute | solution.py:199
  69.6 42.4 %collective-permute-start.6 = (bf16[2048,256]{1,0:T(8,128)(2,1)}, bf16[2048,256]{1,0:T(8,128)(2,1)}, u32[]{:S(2)}, u32[]{:S(2)}) collective-permute-start(bf16[2048,256]{1,0:T(8,128)(2,1)} %slice.35), channel_id=1, source_target_pairs={{3,0},{0,1},{1,2},{2,3},{7,4},{4,5},{5,6},{6,7},{11,8},{8,9},{9,10... | collective-permute-start | bytes 3145736 | tf_op jit(solution)/shard_map/ppermute | solution.py:200
  70.8 37.2 %copy-start = (bf16[4096,256]{1,0:T(8,128)(2,1)}, bf16[4096,256]{1,0:T(8,128)(2,1)S(1)}, u32[]{:S(2)}) copy-start(bf16[4096,256]{1,0:T(8,128)(2,1)S(1)} %collective-permute-done.refs_1_) | copy-start | bytes 6291460
  71.9 40.1 %collective-permute-start.5 = (bf16[2048,256]{1,0:T(8,128)(2,1)}, bf16[2048,256]{1,0:T(8,128)(2,1)}, u32[]{:S(2)}, u32[]{:S(2)}) collective-permute-start(bf16[2048,256]{1,0:T(8,128)(2,1)} %slice.34), channel_id=1, source_target_pairs={{1,0},{2,1},{3,2},{0,3},{5,4},{6,5},{7,6},{4,7},{9,8},{10,9},{11,1... | collective-permute-start | bytes 3145736 | tf_op jit(solution)/shard_map/ppermute | solution.py:199
  108.0 13.1 %collective-permute-start.4 = (bf16[9,128,256]{2,1,0:T(8,128)(2,1)S(1)}, bf16[9,128,256]{2,1,0:T(8,128)(2,1)S(1)}, u32[]{:S(2)}, u32[]{:S(2)}) collective-permute-start(bf16[9,128,256]{2,1,0:T(8,128)(2,1)S(1)} %get-tuple-element.18), channel_id=1, source_target_pairs={{0,16},{16,0},{1,17},{17,1},{2,18},{18,2},{3,19},{19,3},{4,20},{20... | collective-permute-start | bytes 1769480 | tf_op jit(solution)/shard_map/ppermute | solution.py:231
  121.0 1.9 %collective-permute-start.9 = (bf16[7,128,256]{2,1,0:T(8,128)(2,1)S(1)}, bf16[7,128,256]{2,1,0:T(8,128)(2,1)S(1)}, u32[]{:S(2)}, u32[]{:S(2)}) collective-permute-start(bf16[7,128,256]{2,1,0:T(8,128)(2,1)S(1)} %get-tuple-element.20), channel_id=1, source_target_pairs={{0,16},{16,0},{1,17},{17,1},{2,18},{18,2},{3,19},{19,3},{4,20},{20... | collective-permute-start | bytes 1376264 | tf_op jit(solution)/shard_map/ppermute | solution.py:233
  123.9 9.2 %collective-permute-start.10 = (bf16[4,128,256]{2,1,0:T(8,128)(2,1)S(1)}, bf16[4,128,256]{2,1,0:T(8,128)(2,1)S(1)}, u32[]{:S(2)}, u32[]{:S(2)}) collective-permute-start(bf16[4,128,256]{2,1,0:T(8,128)(2,1)S(1)} %get-tuple-element.22), channel_id=1, source_target_pairs={{0,32},{32,64},{64,96},{96,0},{1,33},{33,65},{65,97},{97,1},{2,34}... | collective-permute-start | bytes 786440 | tf_op jit(solution)/shard_map/ppermute | solution.py:237
  125.2 14.5 %collective-permute-start.11 = (bf16[4,128,256]{2,1,0:T(8,128)(2,1)S(1)}, bf16[4,128,256]{2,1,0:T(8,128)(2,1)S(1)}, u32[]{:S(2)}, u32[]{:S(2)}) collective-permute-start(bf16[4,128,256]{2,1,0:T(8,128)(2,1)S(1)} %get-tuple-element.23), channel_id=1, source_target_pairs={{0,64},{32,96},{64,0},{96,32},{1,65},{33,97},{65,1},{97,33},{2,66}... | collective-permute-start | bytes 786440 | tf_op jit(solution)/shard_map/ppermute | solution.py:237
  127.9 11.9 %collective-permute-start.12 = (bf16[4,128,256]{2,1,0:T(8,128)(2,1)S(1)}, bf16[4,128,256]{2,1,0:T(8,128)(2,1)S(1)}, u32[]{:S(2)}, u32[]{:S(2)}) collective-permute-start(bf16[4,128,256]{2,1,0:T(8,128)(2,1)S(1)} %get-tuple-element.24), channel_id=1, source_target_pairs={{0,96},{32,0},{64,32},{96,64},{1,97},{33,1},{65,33},{97,65},{2,98}... | collective-permute-start | bytes 786440 | tf_op jit(solution)/shard_map/ppermute | solution.py:237
  139.9 10.0 %collective-permute-start.13 = (f32[128,256]{1,0:T(8,128)S(1)}, f32[128,256]{1,0:T(8,128)S(1)}, u32[]{:S(2)}, u32[]{:S(2)}) collective-permute-start(f32[128,256]{1,0:T(8,128)S(1)} %get-tuple-element.28), channel_id=1, source_target_pairs={{0,3},{1,1},{2,19},{3,17},{16,0},{17,2},{18,16},{19,18},{4,7},{5,5... | collective-permute-start | bytes 393224 | tf_op jit(solution)/shard_map/ppermute | solution.py:248
  142.8 12.8 %collective-permute-start.16 = (f32[128,256]{1,0:T(8,128)S(1)}, f32[128,256]{1,0:T(8,128)S(1)}, u32[]{:S(2)}, u32[]{:S(2)}) collective-permute-start(f32[128,256]{1,0:T(8,128)S(1)} %get-tuple-element.25), channel_id=1, source_target_pairs={{0,0},{1,2},{2,16},{3,18},{16,1},{17,3},{18,17},{19,19},{4,4},{5,6... | collective-permute-start | bytes 393224 | tf_op jit(solution)/shard_map/ppermute | solution.py:248
  144.8 10.8 %collective-permute-start.15 = (f32[128,256]{1,0:T(8,128)S(1)}, f32[128,256]{1,0:T(8,128)S(1)}, u32[]{:S(2)}, u32[]{:S(2)}) collective-permute-start(f32[128,256]{1,0:T(8,128)S(1)} %get-tuple-element.26), channel_id=1, source_target_pairs={{0,1},{1,3},{2,17},{3,19},{16,2},{17,0},{18,18},{19,16},{4,5},{5,7... | collective-permute-start | bytes 393224 | tf_op jit(solution)/shard_map/ppermute | solution.py:248
  149.9 5.7 %collective-permute-start.14 = (f32[128,256]{1,0:T(8,128)S(1)}, f32[128,256]{1,0:T(8,128)S(1)}, u32[]{:S(2)}, u32[]{:S(2)}) collective-permute-start(f32[128,256]{1,0:T(8,128)S(1)} %get-tuple-element.27), channel_id=1, source_target_pairs={{0,2},{1,0},{2,18},{3,16},{16,3},{17,1},{18,19},{19,17},{4,6},{5,4... | collective-permute-start | bytes 393224 | tf_op jit(solution)/shard_map/ppermute | solution.py:248

commit v3 on v2

--- a/solution.py
+++ b/solution.py
@@ -20,7 +20,7 @@
     return lax.broadcasted_iota(jnp.int32, shape, dim)
 
 
-def contract_kernel(width, group, scalars, tiles_ref, occ_ref, virt_ref, out_ref, half_ref):
+def contract_kernel(width, group, scalars, tiles_ref, occ_ref, virt_ref, out_ref, masked_ref, half_ref):
     cols = tiles_ref.shape[1]
     tall = width * group
     spread = jnp.where(iota((tall, width), 0) // group == iota((tall, width), 1), 1.0, 0.0).astype(BF16)
@@ -49,7 +49,9 @@
     for g in range(width // four):
         part = half_ref[g * four : (g + 1) * four].reshape(side, cols)
         done = jnp.dot(virt_wide, part, preferred_element_type=F32) * weight
-        out_ref[g * side : (g + 1) * side, :] = done.astype(BF16)
+        rows = slice(g * side, (g + 1) * side)
+        out_ref[rows, :] = done.astype(BF16)
+        masked_ref[rows, :] = tiles_ref[rows, :] * weight.astype(BF16)
 
 
 def contract(scalars, three_centre, green_occ, green_virt):
@@ -66,11 +68,11 @@
                 pl.BlockSpec((1, width, width), lambda i, s: (s[0], 0, 0)),
                 pl.BlockSpec((1, width, width), lambda i, s: (s[1], 0, 0)),
             ],
-            out_specs=whole,
+            out_specs=[whole, whole],
             scratch_shapes=[pltpu.VMEM((width, width, cols), BF16)],
         ),
-        out_shape=jax.ShapeDtypeStruct((rows, cols), BF16),
-        compiler_params=pltpu.CompilerParams(vmem_limit_bytes=40 * 2**20),
+        out_shape=[jax.ShapeDtypeStruct((rows, cols), BF16)] * 2,
+        compiler_params=pltpu.CompilerParams(vmem_limit_bytes=60 * 2**20),
         cost_estimate=pl.CostEstimate(
             flops=40 * 10**9, bytes_accessed=4 * 2**20, transcendentals=0
         ),
@@ -82,7 +84,7 @@
     a_refs, b_refs = refs[:per_side], refs[per_side : 2 * per_side]
     keep_ref, send_ref, acc = refs[2 * per_side :]
     k = pl.program_id(0)
-    core = scalars[4]
+    core = scalars[8]
 
     @pl.when(k == 0)
     def _():
@@ -102,10 +104,7 @@
 
     @pl.when(k == steps - 1)
     def _():
-        for i, (p, _) in enumerate(pairs):
-            for half in range(2):
-                rows = pl.ds(half * HALF, HALF)
-                acc[i, rows, :] = acc[i, rows, :] * scalars[8 + 2 * p + half].astype(F32)
+        for i in range(len(pairs)):
             keep_ref[i] = acc[i, pl.ds(pl.multiple_of(core * HALF, HALF), HALF), :]
             other = pl.ds(pl.multiple_of((1 - core) * HALF, HALF), HALF)
             send_ref[i] = acc[i, other, :].astype(BF16)
@@ -139,7 +138,7 @@
             jax.ShapeDtypeStruct((count, HALF, BLOCK), F32),
             jax.ShapeDtypeStruct((count, HALF, BLOCK), BF16),
         ],
-        compiler_params=pltpu.CompilerParams(vmem_limit_bytes=48 * 2**20),
+        compiler_params=pltpu.CompilerParams(vmem_limit_bytes=(24 if has_far else 20) * 2**20),
         cost_estimate=pl.CostEstimate(
             flops=2 * count * rows * BLOCK * BLOCK, bytes_accessed=20 * 2**20, transcendentals=0
         ),
@@ -147,29 +146,14 @@
 
 
 def merge_kernel(near, far, scalars, *refs):
-    keep_near, got_near, keep_far, got_far = refs[:4]
-    out_refs = refs[4:]
-    own_ref, send_refs = out_refs[0], out_refs[1:]
-
+    keep_near, got_near, keep_far, got_far, out_ref = refs
     for pairs, keep, got in ((near, keep_near, got_near), (far, keep_far, got_far)):
         for i, (p, q) in enumerate(pairs):
-            total = keep[i] + got[i].astype(F32)
-            target = scalars[16 + q]
-            row = scalars[20 + p]
-
-            @pl.when(target == 0)
-            def _():
-                own_ref[row] = total
-
-            for step in range(1, SIDE):
-
-                @pl.when(target == step)
-                def _():
-                    send_refs[step - 1][row] = total.astype(BF16)
+            target = scalars[SIDE + q] * SIDE + scalars[p]
+            out_ref[target] = (keep[i] + got[i].astype(F32)).astype(BF16)
 
 
 def merge(scalars, near, far, keep_near, got_near, keep_far, got_far):
-    shape = (SIDE, HALF, BLOCK)
     spec = lambda n: pl.BlockSpec((n, HALF, BLOCK), lambda i, s: (0, 0, 0))
     return pl.pallas_call(
         functools.partial(merge_kernel, near, far),
@@ -177,12 +161,61 @@
             num_scalar_prefetch=1,
             grid=(1,),
             in_specs=[spec(len(near))] * 2 + [spec(len(far))] * 2,
-            out_specs=[spec(SIDE)] * 4,
-        ),
-        out_shape=[jax.ShapeDtypeStruct(shape, F32)] + [jax.ShapeDtypeStruct(shape, BF16)] * 3,
-        compiler_params=pltpu.CompilerParams(vmem_limit_bytes=32 * 2**20),
+            out_specs=spec(SIDE * SIDE),
+        ),
+        out_shape=jax.ShapeDtypeStruct((SIDE * SIDE, HALF, BLOCK), BF16),
+        compiler_params=pltpu.CompilerParams(vmem_limit_bytes=24 * 2**20),
         cost_estimate=pl.CostEstimate(flops=2**20, bytes_accessed=5 * 2**20, transcendentals=0),
     )(scalars, keep_near, got_near, keep_far, got_far)
+
+
+def total_kernel(scalars, parts_ref, mine_ref, theirs_ref):
+    core = scalars[8]
+    for j in range(2):
+        for out_ref, base in ((mine_ref, 2 * core), (theirs_ref, 2 * (1 - core))):
+            added = parts_ref[base + j].astype(F32)
+            for y in range(1, SIDE):
+                added += parts_ref[y * SIDE + base + j].astype(F32)
+            out_ref[j] = -2.0 * added
+
+
+def total(scalars, parts):
+    return pl.pallas_call(
+        total_kernel,
+        grid_spec=pltpu.PrefetchScalarGridSpec(
+            num_scalar_prefetch=1,
+            grid=(1,),
+            in_specs=[pl.BlockSpec(parts.shape, lambda i, s: (0, 0, 0))],
+            out_specs=[pl.BlockSpec((2, HALF, BLOCK), lambda i, s: (0, 0, 0))] * 2,
+        ),
+        out_shape=[jax.ShapeDtypeStruct((2, HALF, BLOCK), F32)] * 2,
+        compiler_params=pltpu.CompilerParams(vmem_limit_bytes=16 * 2**20),
+        cost_estimate=pl.CostEstimate(flops=2**20, bytes_accessed=2 * 2**20, transcendentals=0),
+    )(scalars, parts)
+
+
+def place_kernel(scalars, mine_ref, other_ref, out_ref):
+    core = scalars[8]
+    for in_ref, half in ((mine_ref, core), (other_ref, 1 - core)):
+        rows = pl.ds(pl.multiple_of(half * HALF, HALF), HALF)
+        for j in range(2):
+            out_ref[rows, j * BLOCK : (j + 1) * BLOCK] = in_ref[j]
+
+
+def place(scalars, mine, other):
+    spec = pl.BlockSpec((2, HALF, BLOCK), lambda i, s: (0, 0, 0))
+    return pl.pallas_call(
+        place_kernel,
+        grid_spec=pltpu.PrefetchScalarGridSpec(
+            num_scalar_prefetch=1,
+            grid=(1,),
+            in_specs=[spec, spec],
+            out_specs=pl.BlockSpec((BLOCK, 2 * BLOCK), lambda i, s: (0, 0)),
+        ),
+        out_shape=jax.ShapeDtypeStruct((BLOCK, 2 * BLOCK), F32),
+        compiler_params=pltpu.CompilerParams(vmem_limit_bytes=16 * 2**20),
+        cost_estimate=pl.CostEstimate(flops=2**18, bytes_accessed=2**20, transcendentals=0),
+    )(scalars, mine, other)
 
 
 def ring(block, axis):
@@ -204,52 +237,27 @@
 def per_device(three_centre, tile_list, pair_blocks, green_occ, green_virt):
     y, c, z, x = (lax.axis_index(name) for name in ("y", "c", "z", "x"))
     offsets = jnp.arange(SIDE)
-    a_after, a_before = ring(three_centre, "x")
-    own = contract(
+    scalars = jnp.concatenate([(x + offsets) & 3, (z + offsets) & 3, c[None]]).astype(jnp.int32)
+    own, masked = contract(
         jnp.concatenate([pair_blocks[0], tile_list[0]]), three_centre, green_occ, green_virt
     )
     b_after, b_before = ring(own, "z")
-    listed, own = lax.optimization_barrier((tile_list, own))
-    row_weights = lax.all_gather(listed[0], "x")
-    row_weights = jnp.take(row_weights, (x + offsets) & 3, axis=0).reshape(-1)
-    first = 2 * (x & 1) + c
-    scalars = jnp.concatenate(
-        [
-            jnp.stack([y, z, x, c, c, c, c, c]),
-            row_weights,
-            (z + offsets - y) & 3,
-            (x + offsets - first) & 3,
-        ]
-    ).astype(jnp.int32)
+    a_after, a_before = ring(masked, "x")
 
     near = tuple((p, q) for p in NEAR for q in NEAR)
-    lefts, rights = [three_centre, a_after, a_before], [own, b_after, b_before]
+    lefts, rights = [masked, a_after, a_before], [own, b_after, b_before]
     keep_near, send_near = products(scalars, lefts, rights, near)
+    rights += far(b_after, b_before, "z")
     lefts += far(a_after, a_before, "x")
-    rights += far(b_after, b_before, "z")
     swap = [(0, 1), (1, 0)]
     got_near = lax.ppermute(send_near, "c", swap)
     keep_far, send_far = products(scalars, lefts, rights, LATE)
     got_far = lax.ppermute(send_far, "c", swap)
 
-    own, *sends = merge(scalars, near, LATE, keep_near, got_near, keep_far, got_far)
-    for k in range(1, SIDE):
-        moved = lax.ppermute(sends[k - 1], "y", [(i, (i + k) % SIDE) for i in range(SIDE)])
-        own = own + moved.astype(F32)
-    own = -2.0 * own
-
-    arrived = []
-    for k in range(SIDE):
-        perm = [
-            (core * SIDE + i, (i // 2) * SIDE + (2 * (i % 2) + core + k) % SIDE)
-            for core in range(2)
-            for i in range(SIDE)
-        ]
-        arrived.append(lax.ppermute(own[k], ("c", "x"), perm))
-    stacked = jnp.stack(arrived[::-1] + arrived[:0:-1])
-    ordered = lax.dynamic_slice_in_dim(stacked, (SIDE - 1 - x) & 3, SIDE, 0)
-    ordered = ordered.reshape(2, 2, HALF, BLOCK)
-    return ordered.transpose(1, 2, 0, 3).reshape(BLOCK, 2 * BLOCK)
+    sends = merge(scalars, near, LATE, keep_near, got_near, keep_far, got_far)
+    parts = lax.all_to_all(sends, ("y", "x"), 0, 0)
+    mine, theirs = total(scalars, parts)
+    return place(scalars, mine, lax.ppermute(theirs, "c", swap))
 
 
 def solution(mesh):

time: 157 us -> 128 us (0.82)
  waiting for transfers between devices: 61.2 us -> 47.4 us
  starting transfers between devices: 31.8 us -> 21.6 us
  blocking collectives: 25 us -> 20.5 us
    all_gather x1 -> x0, blocking collectives: 25 us -> none  [per_device(): row_weights = lax.all_gather(listed[0], 'x')]
    all_to_all x0 -> x1, blocking collectives: none -> 20.5 us  [per_device(): parts = lax.all_to_all(sends, ('y', 'x'), 0, 0)]
    ppermute x7 -> x1, waiting for transfers between devices: 16.4 us -> 1.16 us  [per_device(): return place(scalars, mine, lax.ppermute(theirs, 'c', swap))]
    ppermute x7 -> x1, starting transfers between devices: 15.1 us -> 1.85 us  [per_device(): return place(scalars, mine, lax.ppermute(theirs, 'c', swap))]
    unnamed x15 -> x20, local copies, waits for them, and re-layouts: 2.8 us -> 7.97 us
    pallas_call x2, Pallas kernels: 17.7 us -> 13.6 us  [products(): pl.pallas_call(functools.partial(products_kernel, steps, pairs, has_far),...]
    ppermute x2, waiting for transfers between devices: 0.01 us -> 3.37 us  [far(): lax.ppermute(before[half:], axis, take_prev)]
    ppermute x1, starting transfers between devices: 0.11 us -> 3.22 us  [per_device(): got_far = lax.ppermute(send_far, 'c', swap)]
  transfers between devices with their start and end apart: 17 -> 11, of which waited for: 5 -> 5; matrix products, arithmetic and copies ran while one was open for 6% -> 4% of each run, Pallas kernels for 11% -> 11%
where the time goes in v3:
time: 128 us
  waiting for transfers between devices  47.4 us (37%)
  Pallas kernels  24.4 us (19%)
  starting transfers between devices  21.6 us (17%)
  blocking collectives  20.5 us (16%)
  local copies, waits for them, and re-layouts  12.4 us (10%)
  other arithmetic  1.34 us (1%)
    ppermute x2, waiting for transfers between devices, ring(): lax.ppermute(block, axis, take_prev)  41.2 us
    all_to_all x1, blocking collectives, per_device(): parts = lax.all_to_all(sends, ('y', 'x'), 0, 0)  20.5 us
    pallas_call x2, Pallas kernels, products(): pl.pallas_call(functools.partial(products_kernel, steps, pairs, has_far),...  13.6 us
    pallas_call x1, Pallas kernels, contract(): pl.pallas_call(functools.partial(contract_kernel, width, 16), grid_spec=p...  8.02 us
    unnamed x20, local copies, waits for them, and re-layouts  7.97 us
    ppermute x2, starting transfers between devices, far(): lax.ppermute(after[:half], axis, take_next)  4.48 us
    ppermute x2, starting transfers between devices, ring(): lax.ppermute(block, axis, take_prev)  3.87 us
    ppermute x2, starting transfers between devices, ring(): lax.ppermute(block, axis, take_next)  3.39 us
  transfers between devices with their start and end apart: 11, of which 5 were waited for; matrix products, arithmetic and copies ran while one was open for 4% of the time, Pallas kernels for 11%

profile of v3, /device:TPU:1, one launch (start us, length us, event | category | flops | bytes accessed | tf_op | source)
XLA Modules:
  0.0 127.6 jit_solution(8708038814597304942)
XLA Ops:
  0.0 1.3 pad_add_fusion.1.scalars
  1.3 8.0 %shard_map.55 = (bf16[4096,256]{1,0:T(8,128)(2,1)}, bf16[4096,256]{1,0:T(8,128)(2,1)}) custom-call(s32[4]{0:T(128)} %pad_add_fusion.1.scalars, bf16[4096,256]{1,0:T(8,128)(2,1)} %tiles_ref.1, bf16[16,64,64]{2,1,0:T(8,128)(2,1)} %occ_ref.1, bf16[16,64,64]{2,1,0:T(8,128)(2,1)} %virt_ref.1), custom_call_target="tpu_custom_call" | custom-call | flops 40000000000 | bytes 4194304 | tf_op jit(solution)/shard_map/pallas_call | solution.py:61
  9.3 2.0 %collective-permute-start.1 = (bf16[4096,256]{1,0:T(8,128)(2,1)}, bf16[4096,256]{1,0:T(8,128)(2,1)S(1)}, u32[]{:S(2)}, u32[]{:S(2)}) collective-permute-start(bf16[4096,256]{1,0:T(8,128)(2,1)} %get-tuple-element.13.refs_0_), channel_id=1, source_target_pairs={{3,0},{0,1},{1,2},{2,3},{7,4},{4,5},{5,6},{6,7},{11,8},{8,9},{9,10... | collective-permute-start | bytes 6291464 | tf_op jit(solution)/shard_map/ppermute | solution.py:224
  11.3 1.3 collective-permute-start
  12.6 1.8 %collective-permute-start.3 = (bf16[4096,256]{1,0:T(8,128)(2,1)}, bf16[4096,256]{1,0:T(8,128)(2,1)S(1)}, u32[]{:S(2)}, u32[]{:S(2)}) collective-permute-start(bf16[4096,256]{1,0:T(8,128)(2,1)} %get-tuple-element.14.refs_3_.refs_5_), channel_id=1, source_target_pairs={{12,0},{0,4},{4,8},{8,12},{13,1},{1,5},{5,9},{9,13},{14,2},{2,6},{... | collective-permute-start | bytes 6291464 | tf_op jit(solution)/shard_map/ppermute | solution.py:224
  14.4 2.1 %collective-permute-start.2 = (bf16[4096,256]{1,0:T(8,128)(2,1)}, bf16[4096,256]{1,0:T(8,128)(2,1)S(1)}, u32[]{:S(2)}, u32[]{:S(2)}) collective-permute-start(bf16[4096,256]{1,0:T(8,128)(2,1)} %get-tuple-element.14.refs_3_.refs_5_), channel_id=1, source_target_pairs={{4,0},{8,4},{12,8},{0,12},{5,1},{9,5},{13,9},{1,13},{6,2},{10,6},{... | collective-permute-start | bytes 6291464 | tf_op jit(solution)/shard_map/ppermute | solution.py:224
  16.5 41.2 %collective-permute-done.1.refs_2_ = bf16[4096,256]{1,0:T(8,128)(2,1)S(1)} collective-permute-done((bf16[4096,256]{1,0:T(8,128)(2,1)}, bf16[4096,256]{1,0:T(8,128)(2,1)S(1)}, u32[]{:S(2)}, u32[]{:S(2)}) %collective-permute-start.1) | collective-permute-done | bytes 2097184 | tf_op jit(solution)/shard_map/ppermute | solution.py:224
  60.3 2.4 %collective-permute-start.5 = (bf16[2048,256]{1,0:T(8,128)(2,1)}, bf16[2048,256]{1,0:T(8,128)(2,1)}, u32[]{:S(2)}, u32[]{:S(2)}) collective-permute-start(bf16[2048,256]{1,0:T(8,128)(2,1)} %slice.16), channel_id=1, source_target_pairs={{1,0},{2,1},{3,2},{0,3},{5,4},{6,5},{7,6},{4,7},{9,8},{10,9},{11,1... | collective-permute-start | bytes 3145736 | tf_op jit(solution)/shard_map/ppermute | solution.py:232
  63.7 2.0 %collective-permute-start.8 = (bf16[2048,256]{1,0:T(8,128)(2,1)}, bf16[2048,256]{1,0:T(8,128)(2,1)}, u32[]{:S(2)}, u32[]{:S(2)}) collective-permute-start(bf16[2048,256]{1,0:T(8,128)(2,1)} %slice.19), channel_id=1, source_target_pairs={{12,0},{0,4},{4,8},{8,12},{13,1},{1,5},{5,9},{9,13},{14,2},{2,6},{... | collective-permute-start | bytes 3145736 | tf_op jit(solution)/shard_map/ppermute | solution.py:233
  66.8 2.1 %collective-permute-start.7 = (bf16[2048,256]{1,0:T(8,128)(2,1)}, bf16[2048,256]{1,0:T(8,128)(2,1)}, u32[]{:S(2)}, u32[]{:S(2)}) collective-permute-start(bf16[2048,256]{1,0:T(8,128)(2,1)} %slice.18), channel_id=1, source_target_pairs={{4,0},{8,4},{12,8},{0,12},{5,1},{9,5},{13,9},{1,13},{6,2},{10,6},{... | collective-permute-start | bytes 3145736 | tf_op jit(solution)/shard_map/ppermute | solution.py:232
  69.0 1.6 %copy-done.1 = bf16[4096,256]{1,0:T(8,128)(2,1)S(1)} copy-done((bf16[4096,256]{1,0:T(8,128)(2,1)S(1)}, bf16[4096,256]{1,0:T(8,128)(2,1)}, u32[]{:S(2)}) %copy-start.1) | copy-done | bytes 2097176
  70.6 1.6 %copy-done.4 = bf16[4096,256]{1,0:T(8,128)(2,1)S(1)} copy-done((bf16[4096,256]{1,0:T(8,128)(2,1)S(1)}, bf16[4096,256]{1,0:T(8,128)(2,1)}, u32[]{:S(2)}) %copy-start.4) | copy-done | bytes 2097176
  72.2 1.6 %copy-done.7 = bf16[4096,256]{1,0:T(8,128)(2,1)S(1)} copy-done((bf16[4096,256]{1,0:T(8,128)(2,1)S(1)}, bf16[4096,256]{1,0:T(8,128)(2,1)}, u32[]{:S(2)}) %copy-start.7) | copy-done | bytes 2097176
  73.8 1.6 %copy-done.8 = bf16[4096,256]{1,0:T(8,128)(2,1)S(1)} copy-done((bf16[4096,256]{1,0:T(8,128)(2,1)S(1)}, bf16[4096,256]{1,0:T(8,128)(2,1)}, u32[]{:S(2)}) %copy-start.8) | copy-done | bytes 2097176
  75.4 1.6 %copy-done.9 = bf16[4096,256]{1,0:T(8,128)(2,1)S(1)} copy-done((bf16[4096,256]{1,0:T(8,128)(2,1)S(1)}, bf16[4096,256]{1,0:T(8,128)(2,1)}, u32[]{:S(2)}) %copy-start.9) | copy-done | bytes 2097176
  77.0 6.6 %shard_map.56 = (f32[9,128,256]{2,1,0:T(8,128)S(1)}, bf16[9,128,256]{2,1,0:T(8,128)(2,1)S(1)}) custom-call(s32[9]{0:T(128)S(1)} %pad_add_fusion.scalars, bf16[4096,256]{1,0:T(8,128)(2,1)S(1)} %copy-done.9, bf16[4096,256]{1,0:T(8,128)(2,1)S(1)} %copy-done.1, bf16[4096,256]{1,0:T(8,128)(2,1)S(1)} %collective-permute-done.1.refs_2_, ...), custom_call_target="tpu_custom_call" | custom-call | flops 4831838208 | bytes 20971520 | tf_op jit(solution)/shard_map/pallas_call | solution.py:128
  83.6 2.5 %collective-permute-start.4 = (bf16[9,128,256]{2,1,0:T(8,128)(2,1)S(1)}, bf16[9,128,256]{2,1,0:T(8,128)(2,1)S(1)}, u32[]{:S(2)}, u32[]{:S(2)}) collective-permute-start(bf16[9,128,256]{2,1,0:T(8,128)(2,1)S(1)} %get-tuple-element.16), channel_id=1, source_target_pairs={{0,16},{16,0},{1,17},{17,1},{2,18},{18,2},{3,19},{19,3},{4,20},{20... | collective-permute-start | bytes 1769480 | tf_op jit(solution)/shard_map/ppermute | solution.py:253
  86.1 3.4 %collective-permute-done.8.refs_9_ = bf16[2048,256]{1,0:T(8,128)(2,1)} collective-permute-done((bf16[2048,256]{1,0:T(8,128)(2,1)}, bf16[2048,256]{1,0:T(8,128)(2,1)}, u32[]{:S(2)}, u32[]{:S(2)}) %collective-permute-start.8) | collective-permute-done | bytes 1048608 | tf_op jit(solution)/shard_map/ppermute | solution.py:233
  89.7 6.9 %shard_map.57 = (f32[7,128,256]{2,1,0:T(8,128)S(1)}, bf16[7,128,256]{2,1,0:T(8,128)(2,1)S(1)}) custom-call(s32[9]{0:T(128)S(1)} %pad_add_fusion.scalars, bf16[4096,256]{1,0:T(8,128)(2,1)S(1)} %copy-done.9, bf16[4096,256]{1,0:T(8,128)(2,1)S(1)} %copy-done.2, bf16[4096,256]{1,0:T(8,128)(2,1)S(1)} %collective-permute-done.1.refs_2_, ...), custom_call_target="tpu_custom_call" | custom-call | flops 3758096384 | bytes 20971520 | tf_op jit(solution)/shard_map/pallas_call | solution.py:128
  96.7 3.2 %collective-permute-start.9 = (bf16[7,128,256]{2,1,0:T(8,128)(2,1)S(1)}, bf16[7,128,256]{2,1,0:T(8,128)(2,1)S(1)}, u32[]{:S(2)}, u32[]{:S(2)}) collective-permute-start(bf16[7,128,256]{2,1,0:T(8,128)(2,1)S(1)} %get-tuple-element.18), channel_id=1, source_target_pairs={{0,16},{16,0},{1,17},{17,1},{2,18},{18,2},{3,19},{19,3},{4,20},{20... | collective-permute-start | bytes 1376264 | tf_op jit(solution)/shard_map/ppermute | solution.py:255
  99.9 1.4 %collective-permute-done.9.refs_3_ = bf16[7,128,256]{2,1,0:T(8,128)(2,1)S(1)} collective-permute-done((bf16[7,128,256]{2,1,0:T(8,128)(2,1)S(1)}, bf16[7,128,256]{2,1,0:T(8,128)(2,1)S(1)}, u32[]{:S(2)}, u32[]{:S(2)}) %collective-permute-start.9) | collective-permute-done | bytes 458784 | tf_op jit(solution)/shard_map/ppermute | solution.py:255
  102.1 20.5 %all_to_all.5.parts_ref = bf16[16,128,256]{2,1,0:T(8,128)(2,1)S(1)} all-to-all(bf16[16,128,256]{2,1,0:T(8,128)(2,1)S(1)} %shard_map.58), channel_id=1, replica_groups=mesh['y'=4,'c'=2,'z'=4,'x'=4] {'y','x'}, dimensions={0} | all-to-all | bytes 2097152 | tf_op jit(solution)/shard_map/all_to_all | solution.py:258
  123.3 1.9 %collective-permute-start.10 = (f32[2,128,256]{2,1,0:T(8,128)S(1)}, f32[2,128,256]{2,1,0:T(8,128)S(1)}, u32[]{:S(2)}, u32[]{:S(2)}) collective-permute-start(f32[2,128,256]{2,1,0:T(8,128)S(1)} %get-tuple-element.20), channel_id=1, source_target_pairs={{0,16},{16,0},{1,17},{17,1},{2,18},{18,2},{3,19},{19,3},{4,20},{20... | collective-permute-start | bytes 786440 | tf_op jit(solution)/shard_map/ppermute | solution.py:260
  126.3 1.4 %shard_map.60 = f32[256,512]{1,0:T(8,128)} custom-call(s32[9]{0:T(128)S(1)} %pad_add_fusion.scalars, f32[2,128,256]{2,1,0:T(8,128)S(1)} %get-tuple-element.19.mine_ref, f32[2,128,256]{2,1,0:T(8,128)S(1)} %collective-permute-done.10.other_ref), custom_call_target="tpu_custom_call" | custom-call | flops 262144 | bytes 1048576 | tf_op jit(solution)/shard_map/pallas_call | solution.py:207
  (32 shorter events, 7.7 us)
Async XLA Ops:
  9.3 48.4 %collective-permute-start.1 = (bf16[4096,256]{1,0:T(8,128)(2,1)}, bf16[4096,256]{1,0:T(8,128)(2,1)S(1)}, u32[]{:S(2)}, u32[]{:S(2)}) collective-permute-start(bf16[4096,256]{1,0:T(8,128)(2,1)} %get-tuple-element.13.refs_0_), channel_id=1, source_target_pairs={{3,0},{0,1},{1,2},{2,3},{7,4},{4,5},{5,6},{6,7},{11,8},{8,9},{9,10... | collective-permute-start | bytes 6291464 | tf_op jit(solution)/shard_map/ppermute | solution.py:224
  11.3 47.8 %collective-permute-start = (bf16[4096,256]{1,0:T(8,128)(2,1)}, bf16[4096,256]{1,0:T(8,128)(2,1)S(1)}, u32[]{:S(2)}, u32[]{:S(2)}) collective-permute-start(bf16[4096,256]{1,0:T(8,128)(2,1)} %get-tuple-element.13.refs_0_), channel_id=1, source_target_pairs={{1,0},{2,1},{3,2},{0,3},{5,4},{6,5},{7,6},{4,7},{9,8},{10,9},{11,1... | collective-permute-start | bytes 6291464 | tf_op jit(solution)/shard_map/ppermute | solution.py:224
  12.6 50.0 %collective-permute-start.3 = (bf16[4096,256]{1,0:T(8,128)(2,1)}, bf16[4096,256]{1,0:T(8,128)(2,1)S(1)}, u32[]{:S(2)}, u32[]{:S(2)}) collective-permute-start(bf16[4096,256]{1,0:T(8,128)(2,1)} %get-tuple-element.14.refs_3_.refs_5_), channel_id=1, source_target_pairs={{12,0},{0,4},{4,8},{8,12},{13,1},{1,5},{5,9},{9,13},{14,2},{2,6},{... | collective-permute-start | bytes 6291464 | tf_op jit(solution)/shard_map/ppermute | solution.py:224
  14.4 51.3 %collective-permute-start.2 = (bf16[4096,256]{1,0:T(8,128)(2,1)}, bf16[4096,256]{1,0:T(8,128)(2,1)S(1)}, u32[]{:S(2)}, u32[]{:S(2)}) collective-permute-start(bf16[4096,256]{1,0:T(8,128)(2,1)} %get-tuple-element.14.refs_3_.refs_5_), channel_id=1, source_target_pairs={{4,0},{8,4},{12,8},{0,12},{5,1},{9,5},{13,9},{1,13},{6,2},{10,6},{... | collective-permute-start | bytes 6291464 | tf_op jit(solution)/shard_map/ppermute | solution.py:224
  58.8 27.3 %collective-permute-start.6 = (bf16[2048,256]{1,0:T(8,128)(2,1)}, bf16[2048,256]{1,0:T(8,128)(2,1)S(1)}, u32[]{:S(2)}, u32[]{:S(2)}) collective-permute-start(bf16[2048,256]{1,0:T(8,128)(2,1)} %slice.17), channel_id=1, source_target_pairs={{3,0},{0,1},{1,2},{2,3},{7,4},{4,5},{5,6},{6,7},{11,8},{8,9},{9,10... | collective-permute-start | bytes 3145736 | tf_op jit(solution)/shard_map/ppermute | solution.py:233
  59.1 4.6 %copy-start = (bf16[4096,256]{1,0:T(8,128)(2,1)}, bf16[4096,256]{1,0:T(8,128)(2,1)S(1)}, u32[]{:S(2)}) copy-start(bf16[4096,256]{1,0:T(8,128)(2,1)S(1)} %collective-permute-done.refs_1_) | copy-start | bytes 6291460
  60.3 25.8 %collective-permute-start.5 = (bf16[2048,256]{1,0:T(8,128)(2,1)}, bf16[2048,256]{1,0:T(8,128)(2,1)}, u32[]{:S(2)}, u32[]{:S(2)}) collective-permute-start(bf16[2048,256]{1,0:T(8,128)(2,1)} %slice.16), channel_id=1, source_target_pairs={{1,0},{2,1},{3,2},{0,3},{5,4},{6,5},{7,6},{4,7},{9,8},{10,9},{11,1... | collective-permute-start | bytes 3145736 | tf_op jit(solution)/shard_map/ppermute | solution.py:232
  62.6 4.2 %copy-start.3 = (bf16[4096,256]{1,0:T(8,128)(2,1)}, bf16[4096,256]{1,0:T(8,128)(2,1)S(1)}, u32[]{:S(2)}) copy-start(bf16[4096,256]{1,0:T(8,128)(2,1)S(1)} %collective-permute-done.3.refs_5_.refs_7_) | copy-start | bytes 6291460
  63.7 25.8 %collective-permute-start.8 = (bf16[2048,256]{1,0:T(8,128)(2,1)}, bf16[2048,256]{1,0:T(8,128)(2,1)}, u32[]{:S(2)}, u32[]{:S(2)}) collective-permute-start(bf16[2048,256]{1,0:T(8,128)(2,1)} %slice.19), channel_id=1, source_target_pairs={{12,0},{0,4},{4,8},{8,12},{13,1},{1,5},{5,9},{9,13},{14,2},{2,6},{... | collective-permute-start | bytes 3145736 | tf_op jit(solution)/shard_map/ppermute | solution.py:233
  65.7 3.3 %copy-start.6 = (bf16[4096,256]{1,0:T(8,128)(2,1)}, bf16[4096,256]{1,0:T(8,128)(2,1)S(1)}, u32[]{:S(2)}) copy-start(bf16[4096,256]{1,0:T(8,128)(2,1)S(1)} %collective-permute-done.2.refs_4_.refs_6_) | copy-start | bytes 6291460
  66.8 22.9 %collective-permute-start.7 = (bf16[2048,256]{1,0:T(8,128)(2,1)}, bf16[2048,256]{1,0:T(8,128)(2,1)}, u32[]{:S(2)}, u32[]{:S(2)}) collective-permute-start(bf16[2048,256]{1,0:T(8,128)(2,1)} %slice.18), channel_id=1, source_target_pairs={{4,0},{8,4},{12,8},{0,12},{5,1},{9,5},{13,9},{1,13},{6,2},{10,6},{... | collective-permute-start | bytes 3145736 | tf_op jit(solution)/shard_map/ppermute | solution.py:232
  69.0 1.6 %copy-start.1 = (bf16[4096,256]{1,0:T(8,128)(2,1)S(1)}, bf16[4096,256]{1,0:T(8,128)(2,1)}, u32[]{:S(2)}) copy-start(bf16[4096,256]{1,0:T(8,128)(2,1)} %copy-done) | copy-start | bytes 6291460
  70.6 1.6 %copy-start.4 = (bf16[4096,256]{1,0:T(8,128)(2,1)S(1)}, bf16[4096,256]{1,0:T(8,128)(2,1)}, u32[]{:S(2)}) copy-start(bf16[4096,256]{1,0:T(8,128)(2,1)} %copy-done.3) | copy-start | bytes 6291460
  72.2 1.6 %copy-start.7 = (bf16[4096,256]{1,0:T(8,128)(2,1)S(1)}, bf16[4096,256]{1,0:T(8,128)(2,1)}, u32[]{:S(2)}) copy-start(bf16[4096,256]{1,0:T(8,128)(2,1)} %copy-done.6) | copy-start | bytes 6291460
  73.8 1.6 %copy-start.8 = (bf16[4096,256]{1,0:T(8,128)(2,1)S(1)}, bf16[4096,256]{1,0:T(8,128)(2,1)}, u32[]{:S(2)}) copy-start(bf16[4096,256]{1,0:T(8,128)(2,1)} %get-tuple-element.14.refs_3_.refs_5_) | copy-start | bytes 6291460
  75.4 1.6 %copy-start.9 = (bf16[4096,256]{1,0:T(8,128)(2,1)S(1)}, bf16[4096,256]{1,0:T(8,128)(2,1)}, u32[]{:S(2)}) copy-start(bf16[4096,256]{1,0:T(8,128)(2,1)} %get-tuple-element.13.refs_0_) | copy-start | bytes 6291460
  77.0 12.7 %copy-start.2 = (bf16[4096,256]{1,0:T(8,128)(2,1)S(1)}, bf16[4096,256]{1,0:T(8,128)(2,1)}, u32[]{:S(2)}) copy-start(bf16[4096,256]{1,0:T(8,128)(2,1)} %copy-done) | copy-start | bytes 6291460
  77.0 12.7 %copy-start.5 = (bf16[4096,256]{1,0:T(8,128)(2,1)S(1)}, bf16[4096,256]{1,0:T(8,128)(2,1)}, u32[]{:S(2)}) copy-start(bf16[4096,256]{1,0:T(8,128)(2,1)} %copy-done.3) | copy-start | bytes 6291460
  83.6 16.3 %collective-permute-start.4 = (bf16[9,128,256]{2,1,0:T(8,128)(2,1)S(1)}, bf16[9,128,256]{2,1,0:T(8,128)(2,1)S(1)}, u32[]{:S(2)}, u32[]{:S(2)}) collective-permute-start(bf16[9,128,256]{2,1,0:T(8,128)(2,1)S(1)} %get-tuple-element.16), channel_id=1, source_target_pairs={{0,16},{16,0},{1,17},{17,1},{2,18},{18,2},{3,19},{19,3},{4,20},{20... | collective-permute-start | bytes 1769480 | tf_op jit(solution)/shard_map/ppermute | solution.py:253
  96.7 4.7 %collective-permute-start.9 = (bf16[7,128,256]{2,1,0:T(8,128)(2,1)S(1)}, bf16[7,128,256]{2,1,0:T(8,128)(2,1)S(1)}, u32[]{:S(2)}, u32[]{:S(2)}) collective-permute-start(bf16[7,128,256]{2,1,0:T(8,128)(2,1)S(1)} %get-tuple-element.18), channel_id=1, source_target_pairs={{0,16},{16,0},{1,17},{17,1},{2,18},{18,2},{3,19},{19,3},{4,20},{20... | collective-permute-start | bytes 1376264 | tf_op jit(solution)/shard_map/ppermute | solution.py:255
  123.3 3.0 %collective-permute-start.10 = (f32[2,128,256]{2,1,0:T(8,128)S(1)}, f32[2,128,256]{2,1,0:T(8,128)S(1)}, u32[]{:S(2)}, u32[]{:S(2)}) collective-permute-start(f32[2,128,256]{2,1,0:T(8,128)S(1)} %get-tuple-element.20), channel_id=1, source_target_pairs={{0,16},{16,0},{1,17},{17,1},{2,18},{18,2},{3,19},{19,3},{4,20},{20... | collective-permute-start | bytes 786440 | tf_op jit(solution)/shard_map/ppermute | solution.py:260

commit v4 on v3

v4 whole, which is shorter than its diff:
```python
import functools

import jax
import jax.numpy as jnp
from jax import lax
from jax.experimental import pallas as pl
from jax.experimental.pallas import tpu as pltpu
from jax.sharding import Mesh, PartitionSpec as P

SIDE = 4
BLOCK = 256
HALF = BLOCK // 2
GROUPS = (
    ((0, 0), (1, 0), (3, 0)),
    ((0, 1), (1, 1), (3, 1), (0, 3), (1, 3), (3, 3)),
    ((2, 0), (2, 1), (2, 3), (0, 2), (1, 2), (3, 2), (2, 2)),
)
COSTS = (10, 1, 1)
F32 = jnp.float32
BF16 = jnp.bfloat16


def iota(shape, dim):
    return lax.broadcasted_iota(jnp.int32, shape, dim)


def contract_kernel(width, group, pairs, tiles_ref, occ_ref, virt_ref, low_ref, high_ref, half_ref):
    cols = tiles_ref.shape[1]
    tall = width * group
    spread = jnp.where(iota((width, tall), 1) // group == iota((width, tall), 0), 1.0, 0.0)
    wide = jnp.dot(occ_ref[0], spread.astype(BF16), preferred_element_type=F32).astype(BF16)
    same = iota((group, tall), 0) == iota((group, tall), 1) % group
    same = jnp.where(same, 1.0, 0.0).astype(BF16)
    occ_wide = (wide[:, None, :] * same[None]).reshape(tall, tall)
    four = 4
    side = four * width
    spread = jnp.where(iota((width, side), 1) % width == iota((width, side), 0), 1.0, 0.0)
    wide = jnp.dot(virt_ref[0], spread.astype(BF16), preferred_element_type=F32)
    same = iota((side, side), 0) // width == iota((side, side), 1) // width
    virt_wide = jnp.where(same, jnp.concatenate([wide] * four), 0.0).astype(BF16)

    tiles = tiles_ref.reshape(width, width, cols)
    for t in range(width // group):
        part = tiles[:, t * group : (t + 1) * group, :].reshape(tall, cols)
        half = jnp.dot(occ_wide, part, preferred_element_type=F32).astype(BF16)
        half_ref[:, t * group : (t + 1) * group, :] = half.reshape(width, group, cols)
    for g in range(width // four):
        part = half_ref[g * four : (g + 1) * four].reshape(side, cols)
        done = jnp.dot(virt_wide, part, preferred_element_type=F32).astype(BF16)
        out_ref, h = (low_ref, g) if g < width // 8 else (high_ref, g - width // 8)
        out_ref[h * side : (h + 1) * side, :] = done


def contract(pairs, tiles, green_occ, green_virt):
    width = green_occ.shape[1]
    rows, cols = tiles.shape
    whole = pl.BlockSpec((rows, cols), lambda i, s: (0, 0))
    return pl.pallas_call(
        functools.partial(contract_kernel, width, 16),
        grid_spec=pltpu.PrefetchScalarGridSpec(
            num_scalar_prefetch=1,
            grid=(1,),
            in_specs=[
                whole,
                pl.BlockSpec((1, width, width), lambda i, s: (s[0, 0], 0, 0)),
                pl.BlockSpec((1, width, width), lambda i, s: (s[0, 1], 0, 0)),
            ],
            out_specs=[pl.BlockSpec((rows // 2, cols), lambda i, s: (0, 0))] * 2,
            scratch_shapes=[pltpu.VMEM((width, width, cols), BF16)],
        ),
        out_shape=[jax.ShapeDtypeStruct((rows // 2, cols), BF16)] * 2,
        compiler_params=pltpu.CompilerParams(vmem_limit_bytes=24 * 2**20),
        cost_estimate=pl.CostEstimate(
            flops=40 * 10**9, bytes_accessed=4 * 2**20, transcendentals=0
        ),
    )(pairs, tiles, green_occ, green_virt)


def products_kernel(steps, pairs, left_at, right_at, scalars, *refs):
    keep_ref, send_ref, acc = refs[-3:]
    k = pl.program_id(0)
    core = scalars[8]

    @pl.when(k == 0)
    def _():
        acc[...] = jnp.zeros_like(acc)

    def step(second):
        rights = {q: refs[places[second % len(places)]][...] for q, places in right_at.items()}
        for p, places in left_at.items():
            left = refs[places[second % len(places)]][...].T
            for i, (task_p, q) in enumerate(pairs):
                if task_p == p:
                    acc[i] += jnp.dot(left, rights[q], preferred_element_type=F32)

    @pl.when(k < steps // 2)
    def _():
        step(0)

    @pl.when(k >= steps // 2)
    def _():
        step(1)

    @pl.when(k == steps - 1)
    def _():
        for i in range(len(pairs)):
            keep_ref[i] = acc[i, pl.ds(pl.multiple_of(core * HALF, HALF), HALF), :]
            other = pl.ds(pl.multiple_of((1 - core) * HALF, HALF), HALF)
            send_ref[i] = acc[i, other, :].astype(BF16)


def products(scalars, lefts, rights, pairs, cost, after):
    rows = sum(half.shape[0] for half in lefts[pairs[0][0]])
    chunk = 1024
    steps = rows // chunk
    operands, specs = [], []

    def places(blocks):
        first = len(operands)
        for half, array in enumerate(blocks):
            operands.append(array)
            if len(blocks) == 1:
                index = lambda k, s: (k, 0)
            elif half == 0:
                index = lambda k, s: (jnp.minimum(k, steps // 2 - 1), 0)
            else:
                index = lambda k, s: (jnp.maximum(k - steps // 2, 0), 0)
            specs.append(pl.BlockSpec((chunk, BLOCK), index))
        return tuple(range(first, len(operands)))

    left_at = {p: places(lefts[p]) for p in sorted({p for p, _ in pairs})}
    right_at = {q: places(rights[q]) for q in sorted({q for _, q in pairs})}
    for array in after:
        operands.append(array)
        specs.append(pl.BlockSpec(memory_space=pl.ANY))
    count = len(pairs)
    out = pl.BlockSpec((count, HALF, BLOCK), lambda k, s: (0, 0, 0))
    return pl.pallas_call(
        functools.partial(products_kernel, steps, pairs, left_at, right_at),
        grid_spec=pltpu.PrefetchScalarGridSpec(
            num_scalar_prefetch=1,
            grid=(steps,),
            in_specs=specs,
            out_specs=[out, out],
            scratch_shapes=[pltpu.VMEM((count, BLOCK, BLOCK), F32)],
        ),
        out_shape=[
            jax.ShapeDtypeStruct((count, HALF, BLOCK), F32),
            jax.ShapeDtypeStruct((count, HALF, BLOCK), BF16),
        ],
        compiler_params=pltpu.CompilerParams(vmem_limit_bytes=16 * 2**20),
        cost_estimate=pl.CostEstimate(
            flops=cost * 2 * count * rows * BLOCK * BLOCK,
            bytes_accessed=2**20,
            transcendentals=0,
        ),
    )(scalars, *operands)


def merge_kernel(groups, scalars, *refs):
    out_ref = refs[-1]
    for n, pairs in enumerate(groups):
        keep, got = refs[2 * n], refs[2 * n + 1]
        for i, (p, q) in enumerate(pairs):
            target = scalars[SIDE + q] * SIDE + scalars[p]
            out_ref[target] = (keep[i] + got[i].astype(F32)).astype(BF16)


def merge(scalars, groups, halves):
    spec = lambda n: pl.BlockSpec((n, HALF, BLOCK), lambda i, s: (0, 0, 0))
    return pl.pallas_call(
        functools.partial(merge_kernel, groups),
        grid_spec=pltpu.PrefetchScalarGridSpec(
            num_scalar_prefetch=1,
            grid=(1,),
            in_specs=[spec(len(pairs)) for pairs in groups for _ in range(2)],
            out_specs=spec(SIDE * SIDE),
        ),
        out_shape=jax.ShapeDtypeStruct((SIDE * SIDE, HALF, BLOCK), BF16),
        compiler_params=pltpu.CompilerParams(vmem_limit_bytes=24 * 2**20),
        cost_estimate=pl.CostEstimate(flops=2**20, bytes_accessed=5 * 2**20, transcendentals=0),
    )(scalars, *halves)


def added(core, parts_ref, j):
    total = parts_ref[2 * core + j].astype(F32)
    for y in range(1, SIDE):
        total += parts_ref[y * SIDE + 2 * core + j].astype(F32)
    return -2.0 * total


def theirs_kernel(scalars, parts_ref, out_ref):
    for j in range(2):
        out_ref[j] = added(1 - scalars[8], parts_ref, j)


def theirs(scalars, parts):
    return pl.pallas_call(
        theirs_kernel,
        grid_spec=pltpu.PrefetchScalarGridSpec(
            num_scalar_prefetch=1,
            grid=(1,),
            in_specs=[pl.BlockSpec(parts.shape, lambda i, s: (0, 0, 0))],
            out_specs=pl.BlockSpec((2, HALF, BLOCK), lambda i, s: (0, 0, 0)),
        ),
        out_shape=jax.ShapeDtypeStruct((2, HALF, BLOCK), F32),
        compiler_params=pltpu.CompilerParams(vmem_limit_bytes=16 * 2**20),
        cost_estimate=pl.CostEstimate(flops=2**20, bytes_accessed=2 * 2**20, transcendentals=0),
    )(scalars, parts)


def place_kernel(scalars, parts_ref, other_ref, out_ref):
    core = scalars[8]
    own = pl.ds(pl.multiple_of(core * HALF, HALF), HALF)
    rest = pl.ds(pl.multiple_of((1 - core) * HALF, HALF), HALF)
    for j in range(2):
        out_ref[own, j * BLOCK : (j + 1) * BLOCK] = added(core, parts_ref, j)
        out_ref[rest, j * BLOCK : (j + 1) * BLOCK] = other_ref[j]


def place(scalars, parts, other):
    return pl.pallas_call(
        place_kernel,
        grid_spec=pltpu.PrefetchScalarGridSpec(
            num_scalar_prefetch=1,
            grid=(1,),
            in_specs=[
                pl.BlockSpec(parts.shape, lambda i, s: (0, 0, 0)),
                pl.BlockSpec((2, HALF, BLOCK), lambda i, s: (0, 0, 0)),
            ],
            out_specs=pl.BlockSpec((BLOCK, 2 * BLOCK), lambda i, s: (0, 0)),
        ),
        out_shape=jax.ShapeDtypeStruct((BLOCK, 2 * BLOCK), F32),
        compiler_params=pltpu.CompilerParams(vmem_limit_bytes=16 * 2**20),
        cost_estimate=pl.CostEstimate(flops=2**18, bytes_accessed=2**20, transcendentals=0),
    )(scalars, parts, other)


def ring(block, axis):
    take_next = [((i + 1) % SIDE, i) for i in range(SIDE)]
    take_prev = [((i - 1) % SIDE, i) for i in range(SIDE)]
    return lax.ppermute(block, axis, take_next), lax.ppermute(block, axis, take_prev)


def far(after, before, axis):
    half = after.shape[0] // 2
    take_next = [((i + 1) % SIDE, i) for i in range(SIDE)]
    take_prev = [((i - 1) % SIDE, i) for i in range(SIDE)]
    return (
        lax.ppermute(after[:half], axis, take_next),
        lax.ppermute(before[half:], axis, take_prev),
    )


def around(low, high, axis):
    take_next = [((i + 1) % SIDE, i) for i in range(SIDE)]
    take_prev = [((i - 1) % SIDE, i) for i in range(SIDE)]
    after_low = lax.ppermute(low, axis, take_next)
    before_high = lax.ppermute(high, axis, take_prev)
    after_high = lax.ppermute(high, axis, take_next)
    before_low = lax.ppermute(low, axis, take_prev)
    far_low = lax.ppermute(after_low, axis, take_next)
    far_high = lax.ppermute(before_high, axis, take_prev)
    return {
        0: (low, high),
        1: (after_low, after_high),
        3: (before_low, before_high),
        2: (far_low, far_high),
    }


def per_device(three_centre, tile_list, pair_blocks, green_occ, green_virt):
    y, c, z, x = (lax.axis_index(name) for name in ("y", "c", "z", "x"))
    offsets = jnp.arange(SIDE)
    scalars = jnp.concatenate([(x + offsets) & 3, (z + offsets) & 3, c[None]]).astype(jnp.int32)
    weights = jnp.repeat(tile_list[0].astype(BF16), BLOCK // tile_list.shape[1])
    masked = three_centre * weights[None, :]
    a_after, a_before = ring(masked, "x")
    rights = around(*contract(pair_blocks, masked, green_occ, green_virt), "z")
    lefts = {0: (masked,), 1: (a_after,), 3: (a_before,), 2: far(a_after, a_before, "x")}

    swap = [(0, 1), (1, 0)]
    halves = []
    for pairs, cost in zip(GROUPS, COSTS):
        keep, send = products(scalars, lefts, rights, pairs, cost, halves[-2:-1])
        halves += [keep, lax.ppermute(send, "c", swap)]
    sends = merge(scalars, GROUPS, halves)
    parts = lax.all_to_all(sends, ("y", "x"), 0, 0)
    return place(scalars, parts, lax.ppermute(theirs(scalars, parts), "c", swap))


def solution(mesh):
    fine = Mesh(mesh.devices.reshape(SIDE, 2, SIDE, SIDE), ("y", "c", "z", "x"))
    ao, aux = ("y", "c"), ("z", "x")
    return jax.shard_map(
        per_device,
        mesh=fine,
        in_specs=(P(ao, aux), P(ao, aux), P(ao, None), P(), P()),
        out_specs=P(aux, ao),
        check_vma=False,
    )
```

time: 128 us -> 126 us (0.984)
  local copies, waits for them, and re-layouts: 12.4 us -> 2.67 us
  Pallas kernels: 24.4 us -> 27.8 us
  blocking collectives: 20.5 us -> 22.8 us
    ppermute x2 -> x1, waiting for transfers between devices: 41.2 us -> 0.26 us  [ring(): lax.ppermute(block, axis, take_prev)]
    ppermute x3 -> x10, waiting for transfers between devices: 2.6 us -> 36.6 us  [the longest x1 18.8 us: around(): after_low = lax.ppermute(low, axis, take_next)]
    ppermute x2 -> x1, waiting for transfers between devices: 0.01 us -> 10.9 us  [ring(): lax.ppermute(block, axis, take_next)]
    unnamed x20 -> x6, local copies, waits for them, and re-layouts: 7.97 us -> 0.01 us
    ppermute x3 -> x10, starting transfers between devices: 7.55 us -> 14.8 us  [the longest x3 4.23 us: per_device(): halves += [keep, lax.ppermute(send, 'c', swap)]]
    pallas_call x4 -> x5, Pallas kernels: 15 us -> 21.8 us  [the longest x3 20.5 us: products(): pl.pallas_call(functools.partial(products_kernel, steps, pairs, left_at,...]
    ppermute x2 -> x1, starting transfers between devices: 3.87 us -> 0.01 us  [ring(): lax.ppermute(block, axis, take_prev)]
    pallas_call x1, Pallas kernels: 8.02 us -> 4.56 us  [contract(): pl.pallas_call(functools.partial(contract_kernel, width, 16), grid_spec=p...]
  transfers between devices with their start and end apart: 11 -> 14, of which waited for: 5 -> 9; matrix products, arithmetic and copies ran while one was open for 4% -> 2% of each run, Pallas kernels for 11% -> 14%
where the time goes in v4:
time: 126 us; the launch traced here: 125 us
  waiting for transfers between devices  47.7 us (38%)
  Pallas kernels  27.8 us (22%)
  blocking collectives  22.8 us (18%)
  starting transfers between devices  21.5 us (17%)
  local copies, waits for them, and re-layouts  2.67 us (2%)
  other arithmetic  2.53 us (2%)
    all_to_all x1, blocking collectives, per_device(): parts = lax.all_to_all(sends, ('y', 'x'), 0, 0)  22.8 us
    pallas_call x3, Pallas kernels, products(): pl.pallas_call(functools.partial(products_kernel, steps, pairs, left_at,...  20.5 us
    ppermute x1, waiting for transfers between devices, around(): after_low = lax.ppermute(low, axis, take_next)  18.8 us
    ppermute x1, waiting for transfers between devices, ring(): lax.ppermute(block, axis, take_next)  10.9 us
    ppermute x1, waiting for transfers between devices, around(): far_low = lax.ppermute(after_low, axis, take_next)  9.92 us
    pallas_call x1, Pallas kernels, contract(): pl.pallas_call(functools.partial(contract_kernel, width, 16), grid_spec=p...  4.56 us
    ppermute x3, starting transfers between devices, per_device(): halves += [keep, lax.ppermute(send, 'c', swap)]  4.23 us
    ppermute x1, starting transfers between devices, around(): after_low = lax.ppermute(low, axis, take_next)  3.76 us
  transfers between devices with their start and end apart: 14, of which 9 were waited for; matrix products, arithmetic and copies ran while one was open for 2% of the time, Pallas kernels for 14%

profile of v4, /device:TPU:1, one launch (start us, length us, event | category | flops | bytes accessed | tf_op | source)
XLA Modules:
  0.0 125.1 jit_solution(14569337935054397709)
XLA Ops:
  0.7 1.8 %broadcast_multiply_fusion.tiles_ref.refs_0_ = bf16[4096,256]{1,0:T(8,128)(2,1)S(1)} fusion(bf16[4096,256]{1,0:T(8,128)(2,1)} %param.5, bf16[256]{0:T(256)(128)(2,1)S(1)} %broadcast_bitcast_fusion), kind=kLoop, calls=%fused_computation | loop fusion | flops 1048576 | bytes 4194816 | tf_op jit(solution)/shard_map/mul | solution.py:277
  2.5 3.4 %collective-permute-start = (bf16[4096,256]{1,0:T(8,128)(2,1)S(1)}, bf16[4096,256]{1,0:T(8,128)(2,1)}, u32[]{:S(2)}, u32[]{:S(2)}) collective-permute-start(bf16[4096,256]{1,0:T(8,128)(2,1)S(1)} %broadcast_multiply_fusion.tiles_ref.refs_0_), channel_id=1, source_target_pairs={{1,0},{2,1},{3,2},{0,3},{5,4},{6,5},{7,6},{4,7},{9,8},{10,9},{11,1... | collective-permute-start | bytes 6291464 | tf_op jit(solution)/shard_map/ppermute | solution.py:242
  5.9 4.6 %shard_map.55 = (bf16[2048,256]{1,0:T(8,128)(2,1)S(1)}, bf16[2048,256]{1,0:T(8,128)(2,1)}) custom-call(s32[1,2]{1,0:T(1,128)S(1)} %copy-done.2, bf16[4096,256]{1,0:T(8,128)(2,1)S(1)} %broadcast_multiply_fusion.tiles_ref.refs_0_, bf16[16,64,64]{2,1,0:T(8,128)(2,1)S(1)} %copy-done, bf16[16,64,64]{2,1,0:T(8,128)(2,1)S(1)} %copy-done.1), custom_call_target="tpu_custom_call" | custom-call | flops 40000000000 | bytes 4194304 | tf_op jit(solution)/shard_map/pallas_call | solution.py:58
  10.5 3.8 %collective-permute-start.3 = (bf16[2048,256]{1,0:T(8,128)(2,1)S(1)}, bf16[2048,256]{1,0:T(8,128)(2,1)}, u32[]{:S(2)}, u32[]{:S(2)}) collective-permute-start(bf16[2048,256]{1,0:T(8,128)(2,1)S(1)} %get-tuple-element.13.refs_3_.refs_5_), channel_id=1, source_target_pairs={{4,0},{8,4},{12,8},{0,12},{5,1},{9,5},{13,9},{1,13},{6,2},{10,6},{... | collective-permute-start | bytes 3145736 | tf_op jit(solution)/shard_map/ppermute | solution.py:258
  14.3 2.7 %collective-permute-start.4 = (bf16[2048,256]{1,0:T(8,128)(2,1)}, bf16[2048,256]{1,0:T(8,128)(2,1)}, u32[]{:S(2)}, u32[]{:S(2)}) collective-permute-start(bf16[2048,256]{1,0:T(8,128)(2,1)} %get-tuple-element.14.refs_4_.refs_6_), channel_id=1, source_target_pairs={{4,0},{8,4},{12,8},{0,12},{5,1},{9,5},{13,9},{1,13},{6,2},{10,6},{... | collective-permute-start | bytes 3145736 | tf_op jit(solution)/shard_map/ppermute | solution.py:260
  17.0 18.8 %collective-permute-done.3.refs_3_.refs_7_ = bf16[2048,256]{1,0:T(8,128)(2,1)} collective-permute-done((bf16[2048,256]{1,0:T(8,128)(2,1)S(1)}, bf16[2048,256]{1,0:T(8,128)(2,1)}, u32[]{:S(2)}, u32[]{:S(2)}) %collective-permute-start.3) | collective-permute-done | bytes 1048608 | tf_op jit(solution)/shard_map/ppermute | solution.py:258
  36.3 2.9 %collective-permute-done.6.refs_6_.refs_12_ = bf16[2048,256]{1,0:T(8,128)(2,1)} collective-permute-done((bf16[2048,256]{1,0:T(8,128)(2,1)}, bf16[2048,256]{1,0:T(8,128)(2,1)}, u32[]{:S(2)}, u32[]{:S(2)}) %collective-permute-start.6) | collective-permute-done | bytes 1048608 | tf_op jit(solution)/shard_map/ppermute | solution.py:259
  39.3 10.9 %collective-permute-done.refs_1_ = bf16[4096,256]{1,0:T(8,128)(2,1)} collective-permute-done((bf16[4096,256]{1,0:T(8,128)(2,1)S(1)}, bf16[4096,256]{1,0:T(8,128)(2,1)}, u32[]{:S(2)}, u32[]{:S(2)}) %collective-permute-start) | collective-permute-done | bytes 2097184 | tf_op jit(solution)/shard_map/ppermute | solution.py:242
  50.2 1.6 %collective-permute-start.11 = (bf16[2048,256]{1,0:T(8,128)(2,1)}, bf16[2048,256]{1,0:T(8,128)(2,1)S(1)}, u32[]{:S(2)}, u32[]{:S(2)}) collective-permute-start(bf16[2048,256]{1,0:T(8,128)(2,1)} %collective-permute-done.6.refs_6_.refs_12_), channel_id=1, source_target_pairs={{12,0},{0,4},{4,8},{8,12},{13,1},{1,5},{5,9},{9,13},{14,2},{2,6},{... | collective-permute-start | bytes 3145736 | tf_op jit(solution)/shard_map/ppermute | solution.py:263
  51.8 1.3 %slice.8 = bf16[2048,256]{1,0:T(8,128)(2,1)S(1)} slice(bf16[4096,256]{1,0:T(8,128)(2,1)} %collective-permute-done.refs_1_), slice={[0:2048], [0:256]} | slice | bytes 2097152 | tf_op jit(solution)/shard_map/slice | solution.py:250
  53.4 3.3 %collective-permute-start.8 = (bf16[2048,256]{1,0:T(8,128)(2,1)S(1)}, bf16[2048,256]{1,0:T(8,128)(2,1)S(1)}, u32[]{:S(2)}, u32[]{:S(2)}) collective-permute-start(bf16[2048,256]{1,0:T(8,128)(2,1)S(1)} %slice.8), channel_id=1, source_target_pairs={{1,0},{2,1},{3,2},{0,3},{5,4},{6,5},{7,6},{4,7},{9,8},{10,9},{11,1... | collective-permute-start | bytes 3145736 | tf_op jit(solution)/shard_map/ppermute | solution.py:250
  56.7 1.3 %slice.9 = bf16[2048,256]{1,0:T(8,128)(2,1)S(1)} slice(bf16[4096,256]{1,0:T(8,128)(2,1)} %collective-permute-done.1.refs_2_.refs_4_), slice={[2048:4096], [0:256]} | slice | bytes 2097152 | tf_op jit(solution)/shard_map/slice | solution.py:251
  58.3 5.4 %shard_map.56 = (f32[3,128,256]{2,1,0:T(8,128)S(1)}, bf16[3,128,256]{2,1,0:T(8,128)(2,1)S(1)}) custom-call(s32[9]{0:T(128)S(1)} %pad_add_fusion.scalars, bf16[4096,256]{1,0:T(8,128)(2,1)S(1)} %broadcast_multiply_fusion.tiles_ref.refs_0_, bf16[4096,256]{1,0:T(8,128)(2,1)} %collective-permute-done.refs_1_, ...), custom_call_target="tpu_custom_call" | custom-call | flops 16106127360 | bytes 1048576 | tf_op jit(solution)/shard_map/pallas_call | solution.py:138
  63.8 7.1 %shard_map.57 = (f32[6,128,256]{2,1,0:T(8,128)S(1)}, bf16[6,128,256]{2,1,0:T(8,128)(2,1)S(1)}) custom-call(s32[9]{0:T(128)S(1)} %pad_add_fusion.scalars, bf16[4096,256]{1,0:T(8,128)(2,1)S(1)} %broadcast_multiply_fusion.tiles_ref.refs_0_, bf16[4096,256]{1,0:T(8,128)(2,1)} %collective-permute-done.refs_1_, ...), custom_call_target="tpu_custom_call" | custom-call | flops 3221225472 | bytes 1048576 | tf_op jit(solution)/shard_map/pallas_call | solution.py:138
  70.9 9.9 %collective-permute-done.10.refs_9_ = bf16[2048,256]{1,0:T(8,128)(2,1)S(1)} collective-permute-done((bf16[2048,256]{1,0:T(8,128)(2,1)}, bf16[2048,256]{1,0:T(8,128)(2,1)S(1)}, u32[]{:S(2)}, u32[]{:S(2)}) %collective-permute-start.10) | collective-permute-done | bytes 1048608 | tf_op jit(solution)/shard_map/ppermute | solution.py:262
  80.8 1.7 %collective-permute-done.11.refs_10_ = bf16[2048,256]{1,0:T(8,128)(2,1)S(1)} collective-permute-done((bf16[2048,256]{1,0:T(8,128)(2,1)}, bf16[2048,256]{1,0:T(8,128)(2,1)S(1)}, u32[]{:S(2)}, u32[]{:S(2)}) %collective-permute-start.11) | collective-permute-done | bytes 1048608 | tf_op jit(solution)/shard_map/ppermute | solution.py:263
  82.6 8.0 %shard_map.58 = (f32[7,128,256]{2,1,0:T(8,128)S(1)}, bf16[7,128,256]{2,1,0:T(8,128)(2,1)S(1)}) custom-call(s32[9]{0:T(128)S(1)} %pad_add_fusion.scalars, bf16[4096,256]{1,0:T(8,128)(2,1)S(1)} %broadcast_multiply_fusion.tiles_ref.refs_0_, bf16[4096,256]{1,0:T(8,128)(2,1)} %collective-permute-done.refs_1_, ...), custom_call_target="tpu_custom_call" | custom-call | flops 3758096384 | bytes 1048576 | tf_op jit(solution)/shard_map/pallas_call | solution.py:138
  90.5 3.7 %collective-permute-start.12 = (bf16[7,128,256]{2,1,0:T(8,128)(2,1)S(1)}, bf16[7,128,256]{2,1,0:T(8,128)(2,1)S(1)}, u32[]{:S(2)}, u32[]{:S(2)}) collective-permute-start(bf16[7,128,256]{2,1,0:T(8,128)(2,1)S(1)} %get-tuple-element.20), channel_id=1, source_target_pairs={{0,16},{16,0},{1,17},{17,1},{2,18},{18,2},{3,19},{19,3},{4,20},{20... | collective-permute-start | bytes 1376264 | tf_op jit(solution)/shard_map/ppermute | solution.py:286
  94.8 1.8 %collective-permute-done.2.refs_1_ = bf16[3,128,256]{2,1,0:T(8,128)(2,1)S(1)} collective-permute-done((bf16[3,128,256]{2,1,0:T(8,128)(2,1)S(1)}, bf16[3,128,256]{2,1,0:T(8,128)(2,1)S(1)}, u32[]{:S(2)}, u32[]{:S(2)}) %collective-permute-start.2) | collective-permute-done | bytes 196640 | tf_op jit(solution)/shard_map/ppermute | solution.py:286
  96.5 0.7 shard_map.59
  97.3 22.8 %all_to_all.5.parts_ref = bf16[16,128,256]{2,1,0:T(8,128)(2,1)S(1)} all-to-all(bf16[16,128,256]{2,1,0:T(8,128)(2,1)S(1)} %shard_map.59), channel_id=1, replica_groups=mesh['y'=4,'c'=2,'z'=4,'x'=4] {'y','x'}, dimensions={0} | all-to-all | bytes 2097152 | tf_op jit(solution)/shard_map/all_to_all | solution.py:288
  120.7 1.9 %collective-permute-start.13 = (f32[2,128,256]{2,1,0:T(8,128)S(1)}, f32[2,128,256]{2,1,0:T(8,128)S(1)}, u32[]{:S(2)}, u32[]{:S(2)}) collective-permute-start(f32[2,128,256]{2,1,0:T(8,128)S(1)} %shard_map.60), channel_id=1, source_target_pairs={{0,16},{16,0},{1,17},{17,1},{2,18},{18,2},{3,19},{19,3},{4,20},{20... | collective-permute-start | bytes 786440 | tf_op jit(solution)/shard_map/ppermute | solution.py:289
  122.5 1.2 collective-permute-done.13.other_ref
  123.7 1.4 %shard_map.61 = f32[256,512]{1,0:T(8,128)} custom-call(s32[9]{0:T(128)S(1)} %pad_add_fusion.scalars, bf16[16,128,256]{2,1,0:T(8,128)(2,1)S(1)} %all_to_all.5.parts_ref, f32[2,128,256]{2,1,0:T(8,128)S(1)} %collective-permute-done.13.other_ref), custom_call_target="tpu_custom_call" | custom-call | flops 262144 | bytes 1048576 | tf_op jit(solution)/shard_map/pallas_call | solution.py:222
  (25 shorter events, 3.2 us)
Async XLA Ops:
  0.7 5.2 %copy-start = (bf16[16,64,64]{2,1,0:T(8,128)(2,1)S(1)}, bf16[16,64,64]{2,1,0:T(8,128)(2,1)}, u32[]{:S(2)}) copy-start(bf16[16,64,64]{2,1,0:T(8,128)(2,1)} %occ_ref.1) | copy-start | bytes 393220
  0.7 5.2 %copy-start.1 = (bf16[16,64,64]{2,1,0:T(8,128)(2,1)S(1)}, bf16[16,64,64]{2,1,0:T(8,128)(2,1)}, u32[]{:S(2)}) copy-start(bf16[16,64,64]{2,1,0:T(8,128)(2,1)} %virt_ref.1) | copy-start | bytes 393220
  0.7 5.2 %copy-start.2 = (s32[1,2]{1,0:T(1,128)S(1)}, s32[1,2]{1,0:T(1,128)}, u32[]{:S(2)}) copy-start(s32[1,2]{1,0:T(1,128)} %pairs.1) | copy-start | bytes 28
  2.5 47.7 %collective-permute-start = (bf16[4096,256]{1,0:T(8,128)(2,1)S(1)}, bf16[4096,256]{1,0:T(8,128)(2,1)}, u32[]{:S(2)}, u32[]{:S(2)}) collective-permute-start(bf16[4096,256]{1,0:T(8,128)(2,1)S(1)} %broadcast_multiply_fusion.tiles_ref.refs_0_), channel_id=1, source_target_pairs={{1,0},{2,1},{3,2},{0,3},{5,4},{6,5},{7,6},{4,7},{9,8},{10,9},{11,1... | collective-permute-start | bytes 6291464 | tf_op jit(solution)/shard_map/ppermute | solution.py:242
  5.9 47.5 %collective-permute-start.1 = (bf16[4096,256]{1,0:T(8,128)(2,1)S(1)}, bf16[4096,256]{1,0:T(8,128)(2,1)}, u32[]{:S(2)}, u32[]{:S(2)}) collective-permute-start(bf16[4096,256]{1,0:T(8,128)(2,1)S(1)} %broadcast_multiply_fusion.tiles_ref.refs_0_), channel_id=1, source_target_pairs={{3,0},{0,1},{1,2},{2,3},{7,4},{4,5},{5,6},{6,7},{11,8},{8,9},{9,10... | collective-permute-start | bytes 6291464 | tf_op jit(solution)/shard_map/ppermute | solution.py:242
  10.5 25.3 %collective-permute-start.3 = (bf16[2048,256]{1,0:T(8,128)(2,1)S(1)}, bf16[2048,256]{1,0:T(8,128)(2,1)}, u32[]{:S(2)}, u32[]{:S(2)}) collective-permute-start(bf16[2048,256]{1,0:T(8,128)(2,1)S(1)} %get-tuple-element.13.refs_3_.refs_5_), channel_id=1, source_target_pairs={{4,0},{8,4},{12,8},{0,12},{5,1},{9,5},{13,9},{1,13},{6,2},{10,6},{... | collective-permute-start | bytes 3145736 | tf_op jit(solution)/shard_map/ppermute | solution.py:258
  14.3 24.9 %collective-permute-start.6 = (bf16[2048,256]{1,0:T(8,128)(2,1)}, bf16[2048,256]{1,0:T(8,128)(2,1)}, u32[]{:S(2)}, u32[]{:S(2)}) collective-permute-start(bf16[2048,256]{1,0:T(8,128)(2,1)} %get-tuple-element.14.refs_4_.refs_6_), channel_id=1, source_target_pairs={{12,0},{0,4},{4,8},{8,12},{13,1},{1,5},{5,9},{9,13},{14,2},{2,6},{... | collective-permute-start | bytes 3145736 | tf_op jit(solution)/shard_map/ppermute | solution.py:259
  14.3 44.1 %collective-permute-start.4 = (bf16[2048,256]{1,0:T(8,128)(2,1)}, bf16[2048,256]{1,0:T(8,128)(2,1)}, u32[]{:S(2)}, u32[]{:S(2)}) collective-permute-start(bf16[2048,256]{1,0:T(8,128)(2,1)} %get-tuple-element.14.refs_4_.refs_6_), channel_id=1, source_target_pairs={{4,0},{8,4},{12,8},{0,12},{5,1},{9,5},{13,9},{1,13},{6,2},{10,6},{... | collective-permute-start | bytes 3145736 | tf_op jit(solution)/shard_map/ppermute | solution.py:260
  35.8 28.0 %collective-permute-start.5 = (bf16[2048,256]{1,0:T(8,128)(2,1)S(1)}, bf16[2048,256]{1,0:T(8,128)(2,1)S(1)}, u32[]{:S(2)}, u32[]{:S(2)}) collective-permute-start(bf16[2048,256]{1,0:T(8,128)(2,1)S(1)} %get-tuple-element.13.refs_3_.refs_5_), channel_id=1, source_target_pairs={{12,0},{0,4},{4,8},{8,12},{13,1},{1,5},{5,9},{9,13},{14,2},{2,6},{... | collective-permute-start | bytes 3145736 | tf_op jit(solution)/shard_map/ppermute | solution.py:261
  39.2 41.6 %collective-permute-start.10 = (bf16[2048,256]{1,0:T(8,128)(2,1)}, bf16[2048,256]{1,0:T(8,128)(2,1)S(1)}, u32[]{:S(2)}, u32[]{:S(2)}) collective-permute-start(bf16[2048,256]{1,0:T(8,128)(2,1)} %collective-permute-done.3.refs_3_.refs_7_), channel_id=1, source_target_pairs={{4,0},{8,4},{12,8},{0,12},{5,1},{9,5},{13,9},{1,13},{6,2},{10,6},{... | collective-permute-start | bytes 3145736 | tf_op jit(solution)/shard_map/ppermute | solution.py:262
  50.2 32.3 %collective-permute-start.11 = (bf16[2048,256]{1,0:T(8,128)(2,1)}, bf16[2048,256]{1,0:T(8,128)(2,1)S(1)}, u32[]{:S(2)}, u32[]{:S(2)}) collective-permute-start(bf16[2048,256]{1,0:T(8,128)(2,1)} %collective-permute-done.6.refs_6_.refs_12_), channel_id=1, source_target_pairs={{12,0},{0,4},{4,8},{8,12},{13,1},{1,5},{5,9},{9,13},{14,2},{2,6},{... | collective-permute-start | bytes 3145736 | tf_op jit(solution)/shard_map/ppermute | solution.py:263
  53.4 29.1 %collective-permute-start.8 = (bf16[2048,256]{1,0:T(8,128)(2,1)S(1)}, bf16[2048,256]{1,0:T(8,128)(2,1)S(1)}, u32[]{:S(2)}, u32[]{:S(2)}) collective-permute-start(bf16[2048,256]{1,0:T(8,128)(2,1)S(1)} %slice.8), channel_id=1, source_target_pairs={{1,0},{2,1},{3,2},{0,3},{5,4},{6,5},{7,6},{4,7},{9,8},{10,9},{11,1... | collective-permute-start | bytes 3145736 | tf_op jit(solution)/shard_map/ppermute | solution.py:250
  58.3 24.2 %collective-permute-start.9 = (bf16[2048,256]{1,0:T(8,128)(2,1)S(1)}, bf16[2048,256]{1,0:T(8,128)(2,1)S(1)}, u32[]{:S(2)}, u32[]{:S(2)}) collective-permute-start(bf16[2048,256]{1,0:T(8,128)(2,1)S(1)} %slice.9), channel_id=1, source_target_pairs={{3,0},{0,1},{1,2},{2,3},{7,4},{4,5},{5,6},{6,7},{11,8},{8,9},{9,10... | collective-permute-start | bytes 3145736 | tf_op jit(solution)/shard_map/ppermute | solution.py:251
  90.5 6.0 %collective-permute-start.12 = (bf16[7,128,256]{2,1,0:T(8,128)(2,1)S(1)}, bf16[7,128,256]{2,1,0:T(8,128)(2,1)S(1)}, u32[]{:S(2)}, u32[]{:S(2)}) collective-permute-start(bf16[7,128,256]{2,1,0:T(8,128)(2,1)S(1)} %get-tuple-element.20), channel_id=1, source_target_pairs={{0,16},{16,0},{1,17},{17,1},{2,18},{18,2},{3,19},{19,3},{4,20},{20... | collective-permute-start | bytes 1376264 | tf_op jit(solution)/shard_map/ppermute | solution.py:286
  94.2 2.3 %collective-permute-start.7 = (bf16[6,128,256]{2,1,0:T(8,128)(2,1)S(1)}, bf16[6,128,256]{2,1,0:T(8,128)(2,1)S(1)}, u32[]{:S(2)}, u32[]{:S(2)}) collective-permute-start(bf16[6,128,256]{2,1,0:T(8,128)(2,1)S(1)} %get-tuple-element.18), channel_id=1, source_target_pairs={{0,16},{16,0},{1,17},{17,1},{2,18},{18,2},{3,19},{19,3},{4,20},{20... | collective-permute-start | bytes 1179656 | tf_op jit(solution)/shard_map/ppermute | solution.py:286
  94.3 2.2 %collective-permute-start.2 = (bf16[3,128,256]{2,1,0:T(8,128)(2,1)S(1)}, bf16[3,128,256]{2,1,0:T(8,128)(2,1)S(1)}, u32[]{:S(2)}, u32[]{:S(2)}) collective-permute-start(bf16[3,128,256]{2,1,0:T(8,128)(2,1)S(1)} %get-tuple-element.16), channel_id=1, source_target_pairs={{0,16},{16,0},{1,17},{17,1},{2,18},{18,2},{3,19},{19,3},{4,20},{20... | collective-permute-start | bytes 589832 | tf_op jit(solution)/shard_map/ppermute | solution.py:286
  120.7 3.0 %collective-permute-start.13 = (f32[2,128,256]{2,1,0:T(8,128)S(1)}, f32[2,128,256]{2,1,0:T(8,128)S(1)}, u32[]{:S(2)}, u32[]{:S(2)}) collective-permute-start(f32[2,128,256]{2,1,0:T(8,128)S(1)} %shard_map.60), channel_id=1, source_target_pairs={{0,16},{16,0},{1,17},{17,1},{2,18},{18,2},{3,19},{19,3},{4,20},{20... | collective-permute-start | bytes 786440 | tf_op jit(solution)/shard_map/ppermute | solution.py:289

commit v5 on v4

v5 whole, which is shorter than its diff:
```python
import functools

import jax
import jax.numpy as jnp
from jax import lax
from jax.experimental import pallas as pl
from jax.experimental.pallas import tpu as pltpu
from jax.sharding import Mesh, PartitionSpec as P

SIDE = 4
BLOCK = 256
HALF = BLOCK // 2
GROUPS = (
    ((0, 0), (1, 0), (3, 0)),
    ((0, 1), (1, 1), (3, 1), (0, 3), (1, 3), (3, 3)),
    ((2, 0), (2, 1), (2, 3), (0, 2), (1, 2), (3, 2), (2, 2)),
)
COSTS = (10, 1, 1)
NEAR = (0, 1, 3)
LIMIT = 12
IN_VMEM = pl.BlockSpec(memory_space=pltpu.VMEM)
IN_SMEM = pl.BlockSpec(memory_space=pltpu.SMEM)
F32 = jnp.float32
BF16 = jnp.bfloat16


def iota(shape, dim):
    return lax.broadcasted_iota(jnp.int32, shape, dim)


def contract_kernel(width, group, pairs, tiles_ref, occ_ref, virt_ref, low_ref, high_ref, half_ref):
    cols = tiles_ref.shape[1]
    tall = width * group
    spread = jnp.where(iota((width, tall), 1) // group == iota((width, tall), 0), 1.0, 0.0)
    wide = jnp.dot(occ_ref[pairs[0, 0]], spread.astype(BF16), preferred_element_type=F32).astype(BF16)
    same = iota((group, tall), 0) == iota((group, tall), 1) % group
    same = jnp.where(same, 1.0, 0.0).astype(BF16)
    occ_wide = (wide[:, None, :] * same[None]).reshape(tall, tall)
    four = 4
    side = four * width
    spread = jnp.where(iota((width, side), 1) % width == iota((width, side), 0), 1.0, 0.0)
    wide = jnp.dot(virt_ref[pairs[0, 1]], spread.astype(BF16), preferred_element_type=F32)
    same = iota((side, side), 0) // width == iota((side, side), 1) // width
    virt_wide = jnp.where(same, jnp.concatenate([wide] * four), 0.0).astype(BF16)

    tiles = tiles_ref.reshape(width, width, cols)
    for t in range(width // group):
        part = tiles[:, t * group : (t + 1) * group, :].reshape(tall, cols)
        half = jnp.dot(occ_wide, part, preferred_element_type=F32).astype(BF16)
        half_ref[:, t * group : (t + 1) * group, :] = half.reshape(width, group, cols)
    for g in range(width // four):
        part = half_ref[g * four : (g + 1) * four].reshape(side, cols)
        done = jnp.dot(virt_wide, part, preferred_element_type=F32).astype(BF16)
        out_ref, h = (low_ref, g) if g < width // 8 else (high_ref, g - width // 8)
        out_ref[h * side : (h + 1) * side, :] = done


def contract(pairs, tiles, green_occ, green_virt):
    width = green_occ.shape[1]
    rows, cols = tiles.shape
    return pl.pallas_call(
        functools.partial(contract_kernel, width, 16),
        in_specs=[IN_SMEM, IN_VMEM, IN_VMEM, IN_VMEM],
        out_specs=[IN_VMEM, IN_VMEM],
        out_shape=[jax.ShapeDtypeStruct((rows // 2, cols), BF16)] * 2,
        scratch_shapes=[pltpu.VMEM((width, width, cols), BF16)],
        compiler_params=pltpu.CompilerParams(vmem_limit_bytes=12 * 2**20),
        cost_estimate=pl.CostEstimate(
            flops=40 * 10**9, bytes_accessed=4 * 2**20, transcendentals=0
        ),
    )(pairs, tiles, green_occ, green_virt)


def products_kernel(pairs, left_at, right_at, turned_at, emit, inputs, scalars, *refs):
    keep_ref, send_ref = refs[inputs : inputs + 2]
    kept = refs[inputs + 2 : -1]
    acc = refs[-1]
    core = scalars[8]

    for h in range(2):
        rights = {q: refs[places[h]][...] for q, places in right_at.items()}
        if emit:
            for n, q in enumerate(right_at):
                kept[2 * n + h][...] = rights[q]
        for p in sorted({p for p, _ in pairs}):
            if p in left_at:
                places = left_at[p]
                rows = rights[pairs[0][1]].shape[0]
                if len(places) == 2:
                    left = refs[places[h]][...].T
                else:
                    left = refs[places[0]][h * rows : (h + 1) * rows, :].T
                if emit:
                    kept[-1][NEAR.index(p), h] = left
            else:
                left = refs[turned_at][NEAR.index(p), h]
            for i, (task_p, q) in enumerate(pairs):
                if task_p == p:
                    part = jnp.dot(left, rights[q], preferred_element_type=F32)
                    acc[i] = part if h == 0 else acc[i] + part
    for i in range(len(pairs)):
        keep_ref[i] = acc[i, pl.ds(pl.multiple_of(core * HALF, HALF), HALF), :]
        other = pl.ds(pl.multiple_of((1 - core) * HALF, HALF), HALF)
        send_ref[i] = acc[i, other, :].astype(BF16)


def products(scalars, lefts, rights, pairs, cost, turned, emit, after):
    operands = []

    def places(blocks):
        operands.extend(blocks)
        return tuple(range(len(operands) - len(blocks), len(operands)))

    raw = sorted({p for p, _ in pairs if turned is None or p not in NEAR})
    left_at = {p: places(lefts[p]) for p in raw}
    right_at = {q: places(rights[q]) for q in sorted({q for _, q in pairs})}
    turned_at = len(operands)
    if turned is not None:
        operands.append(turned)
    specs = [IN_SMEM] + [IN_VMEM] * len(operands)
    for array in after:
        operands.append(array)
        specs.append(pl.BlockSpec(memory_space=pl.ANY))
    count = len(pairs)
    half = rights[pairs[0][1]][0].shape
    shapes = [
        jax.ShapeDtypeStruct((count, HALF, BLOCK), F32),
        jax.ShapeDtypeStruct((count, HALF, BLOCK), BF16),
    ]
    if emit:
        shapes += [jax.ShapeDtypeStruct(half, BF16)] * (2 * len(right_at))
        if turned is None:
            shapes.append(jax.ShapeDtypeStruct((len(NEAR), 2, BLOCK, half[0]), BF16))
    outs = pl.pallas_call(
        functools.partial(
            products_kernel, pairs, left_at, right_at, turned_at, emit, len(operands)
        ),
        in_specs=specs,
        out_specs=[IN_VMEM] * len(shapes),
        out_shape=shapes,
        scratch_shapes=[pltpu.VMEM((count, BLOCK, BLOCK), F32)],
        compiler_params=pltpu.CompilerParams(vmem_limit_bytes=LIMIT * 2**20),
        cost_estimate=pl.CostEstimate(
            flops=cost * 2 * count * 2 * half[0] * BLOCK * BLOCK,
            bytes_accessed=2**20,
            transcendentals=0,
        ),
    )(scalars, *operands)
    kept = {q: tuple(outs[2 + 2 * n : 4 + 2 * n]) for n, q in enumerate(right_at)} if emit else {}
    if emit and turned is None:
        turned = outs[-1]
    return outs[0], outs[1], turned, kept


def merge_kernel(groups, scalars, *refs):
    out_ref = refs[-1]
    for n, pairs in enumerate(groups):
        keep, got = refs[2 * n], refs[2 * n + 1]
        for i, (p, q) in enumerate(pairs):
            target = scalars[SIDE + q] * SIDE + scalars[p]
            out_ref[target] = (keep[i] + got[i].astype(F32)).astype(BF16)


def merge(scalars, groups, halves):
    return pl.pallas_call(
        functools.partial(merge_kernel, groups),
        in_specs=[IN_SMEM] + [IN_VMEM] * len(halves),
        out_specs=IN_VMEM,
        out_shape=jax.ShapeDtypeStruct((SIDE * SIDE, HALF, BLOCK), BF16),
        compiler_params=pltpu.CompilerParams(vmem_limit_bytes=8 * 2**20),
        cost_estimate=pl.CostEstimate(flops=2**20, bytes_accessed=5 * 2**20, transcendentals=0),
    )(scalars, *halves)


def added(core, parts_ref, j):
    total = parts_ref[2 * core + j].astype(F32)
    for y in range(1, SIDE):
        total += parts_ref[y * SIDE + 2 * core + j].astype(F32)
    return -2.0 * total


def theirs_kernel(scalars, parts_ref, out_ref):
    for j in range(2):
        out_ref[j] = added(1 - scalars[8], parts_ref, j)


def theirs(scalars, parts):
    return pl.pallas_call(
        theirs_kernel,
        in_specs=[IN_SMEM, IN_VMEM],
        out_specs=IN_VMEM,
        out_shape=jax.ShapeDtypeStruct((2, HALF, BLOCK), F32),
        compiler_params=pltpu.CompilerParams(vmem_limit_bytes=12 * 2**20),
        cost_estimate=pl.CostEstimate(flops=2**20, bytes_accessed=2 * 2**20, transcendentals=0),
    )(scalars, parts)


def place_kernel(scalars, parts_ref, other_ref, out_ref):
    core = scalars[8]
    own = pl.ds(pl.multiple_of(core * HALF, HALF), HALF)
    rest = pl.ds(pl.multiple_of((1 - core) * HALF, HALF), HALF)
    for j in range(2):
        out_ref[own, j * BLOCK : (j + 1) * BLOCK] = added(core, parts_ref, j)
        out_ref[rest, j * BLOCK : (j + 1) * BLOCK] = other_ref[j]


def place(scalars, parts, other):
    return pl.pallas_call(
        place_kernel,
        in_specs=[IN_SMEM, IN_VMEM, IN_VMEM],
        out_specs=IN_VMEM,
        out_shape=jax.ShapeDtypeStruct((BLOCK, 2 * BLOCK), F32),
        compiler_params=pltpu.CompilerParams(vmem_limit_bytes=12 * 2**20),
        cost_estimate=pl.CostEstimate(flops=2**18, bytes_accessed=2**20, transcendentals=0),
    )(scalars, parts, other)


def ring(block, axis):
    take_next = [((i + 1) % SIDE, i) for i in range(SIDE)]
    take_prev = [((i - 1) % SIDE, i) for i in range(SIDE)]
    return lax.ppermute(block, axis, take_next), lax.ppermute(block, axis, take_prev)


def far(after, before, axis):
    half = after.shape[0] // 2
    take_next = [((i + 1) % SIDE, i) for i in range(SIDE)]
    take_prev = [((i - 1) % SIDE, i) for i in range(SIDE)]
    return (
        lax.ppermute(after[:half], axis, take_next),
        lax.ppermute(before[half:], axis, take_prev),
    )


def around(low, high, axis):
    take_next = [((i + 1) % SIDE, i) for i in range(SIDE)]
    take_prev = [((i - 1) % SIDE, i) for i in range(SIDE)]
    after_low = lax.ppermute(low, axis, take_next)
    before_high = lax.ppermute(high, axis, take_prev)
    after_high = lax.ppermute(high, axis, take_next)
    before_low = lax.ppermute(low, axis, take_prev)
    far_low = lax.ppermute(after_low, axis, take_next)
    far_high = lax.ppermute(before_high, axis, take_prev)
    return {
        0: (low, high),
        1: (after_low, after_high),
        3: (before_low, before_high),
        2: (far_low, far_high),
    }


def per_device(three_centre, tile_list, pair_blocks, green_occ, green_virt):
    y, c, z, x = (lax.axis_index(name) for name in ("y", "c", "z", "x"))
    offsets = jnp.arange(SIDE)
    scalars = jnp.concatenate([(x + offsets) & 3, (z + offsets) & 3, c[None]]).astype(jnp.int32)
    weights = jnp.repeat(tile_list[0].astype(BF16), BLOCK // tile_list.shape[1])
    masked = three_centre * weights[None, :]
    a_after, a_before = ring(masked, "x")
    rights = around(*contract(pair_blocks, masked, green_occ, green_virt), "z")
    lefts = {0: (masked,), 1: (a_after,), 3: (a_before,), 2: far(a_after, a_before, "x")}

    swap = [(0, 1), (1, 0)]
    halves = []
    turned = None
    for pairs, cost in zip(GROUPS, COSTS):
        after = halves[1::2] if pairs == GROUPS[-1] else halves[-2:-1]
        keep, send, turned, kept = products(
            scalars, lefts, rights, pairs, cost, turned, pairs != GROUPS[-1], after
        )
        rights.update(kept)
        halves += [keep, lax.ppermute(send, "c", swap)]
    sends = merge(scalars, GROUPS, halves)
    parts = lax.all_to_all(sends, ("y", "x"), 0, 0)
    return place(scalars, parts, lax.ppermute(theirs(scalars, parts), "c", swap))


def solution(mesh):
    fine = Mesh(mesh.devices.reshape(SIDE, 2, SIDE, SIDE), ("y", "c", "z", "x"))
    ao, aux = ("y", "c"), ("z", "x")
    return jax.shard_map(
        per_device,
        mesh=fine,
        in_specs=(P(ao, aux), P(ao, aux), P(ao, None), P(), P()),
        out_specs=P(aux, ao),
        check_vma=False,
    )
```

time: 126 us -> 121 us (0.960)
  Pallas kernels: 27.8 us -> 22.1 us
  starting transfers between devices: 21.5 us -> 25.8 us
  waiting for transfers between devices: 47.7 us -> 45.1 us
    pallas_call x7, Pallas kernels: 27.8 us -> 22.1 us  [the longest x3 14.7 us: products(): pl.pallas_call(functools.partial(products_kernel, pairs, left_at, right_a...]
    ppermute x3, starting transfers between devices: 4.23 us -> 8.44 us  [per_device(): halves += [keep, lax.ppermute(send, 'c', swap)]]
    ppermute x1, waiting for transfers between devices: 1.74 us -> 0.01 us  [around(): far_high = lax.ppermute(before_high, axis, take_prev)]
    ppermute x1, waiting for transfers between devices: 9.92 us -> 8.22 us  [around(): far_low = lax.ppermute(after_low, axis, take_next)]
  transfers between devices with their start and end apart: 14 -> 14, of which waited for: 9 -> 9; matrix products, arithmetic and copies ran while one was open for 2% -> 2% of each run, Pallas kernels for 14% -> 12%
where the time goes in v5:
time: 121 us
  waiting for transfers between devices  45.1 us (37%)
  starting transfers between devices  25.8 us (21%)
  blocking collectives  22.7 us (19%)
  Pallas kernels  22.1 us (18%)
  local copies, waits for them, and re-layouts  2.67 us (2%)
  other arithmetic  2.53 us (2%)
    all_to_all x1, blocking collectives, per_device(): parts = lax.all_to_all(sends, ('y', 'x'), 0, 0)  22.7 us
    ppermute x1, waiting for transfers between devices, around(): after_low = lax.ppermute(low, axis, take_next)  19.1 us
    pallas_call x3, Pallas kernels, products(): pl.pallas_call(functools.partial(products_kernel, pairs, left_at, right_a...  14.7 us
    ppermute x1, waiting for transfers between devices, ring(): lax.ppermute(block, axis, take_next)  10.6 us
    ppermute x3, starting transfers between devices, per_device(): halves += [keep, lax.ppermute(send, 'c', swap)]  8.44 us
    ppermute x1, waiting for transfers between devices, around(): far_low = lax.ppermute(after_low, axis, take_next)  8.22 us
    pallas_call x1, Pallas kernels, contract(): pl.pallas_call(functools.partial(contract_kernel, width, 16), in_specs=[I...  4.67 us
    ppermute x1, starting transfers between devices, around(): after_low = lax.ppermute(low, axis, take_next)  3.75 us
  transfers between devices with their start and end apart: 14, of which 9 were waited for; matrix products, arithmetic and copies ran while one was open for 2% of the time, Pallas kernels for 12%

profile of v5, /device:TPU:1, one launch (start us, length us, event | category | flops | bytes accessed | tf_op | source)
XLA Modules:
  0.0 121.1 jit_solution(1582789815125123657)
XLA Ops:
  0.7 1.8 %broadcast_multiply_fusion.tiles_ref.refs_0_ = bf16[4096,256]{1,0:T(8,128)(2,1)S(1)} fusion(bf16[4096,256]{1,0:T(8,128)(2,1)} %param.5, bf16[256]{0:T(256)(128)(2,1)S(1)} %broadcast_bitcast_fusion), kind=kLoop, calls=%fused_computation | loop fusion | flops 1048576 | bytes 4194816 | tf_op jit(solution)/shard_map/mul | solution.py:256
  2.5 3.4 %collective-permute-start = (bf16[4096,256]{1,0:T(8,128)(2,1)S(1)}, bf16[4096,256]{1,0:T(8,128)(2,1)}, u32[]{:S(2)}, u32[]{:S(2)}) collective-permute-start(bf16[4096,256]{1,0:T(8,128)(2,1)S(1)} %broadcast_multiply_fusion.tiles_ref.refs_0_), channel_id=1, source_target_pairs={{1,0},{2,1},{3,2},{0,3},{5,4},{6,5},{7,6},{4,7},{9,8},{10,9},{11,1... | collective-permute-start | bytes 6291464 | tf_op jit(solution)/shard_map/ppermute | solution.py:221
  5.9 4.7 %shard_map.55 = (bf16[2048,256]{1,0:T(8,128)(2,1)}, bf16[2048,256]{1,0:T(8,128)(2,1)}) custom-call(s32[1,2]{1,0:T(1,128)S(1)} %copy-done.2, bf16[4096,256]{1,0:T(8,128)(2,1)S(1)} %broadcast_multiply_fusion.tiles_ref.refs_0_, bf16[16,64,64]{2,1,0:T(8,128)(2,1)S(1)} %copy-done, bf16[16,64,64]{2,1,0:T(8,128)(2,1)S(1)} %copy-done.1), custom_call_target="tpu_custom_call" | custom-call | flops 40000000000 | bytes 4194304 | tf_op jit(solution)/shard_map/pallas_call | solution.py:61
  10.6 3.8 %collective-permute-start.3 = (bf16[2048,256]{1,0:T(8,128)(2,1)}, bf16[2048,256]{1,0:T(8,128)(2,1)}, u32[]{:S(2)}, u32[]{:S(2)}) collective-permute-start(bf16[2048,256]{1,0:T(8,128)(2,1)} %get-tuple-element.20.refs_3_), channel_id=1, source_target_pairs={{4,0},{8,4},{12,8},{0,12},{5,1},{9,5},{13,9},{1,13},{6,2},{10,6},{... | collective-permute-start | bytes 3145736 | tf_op jit(solution)/shard_map/ppermute | solution.py:237
  14.3 2.7 %collective-permute-start.4 = (bf16[2048,256]{1,0:T(8,128)(2,1)}, bf16[2048,256]{1,0:T(8,128)(2,1)}, u32[]{:S(2)}, u32[]{:S(2)}) collective-permute-start(bf16[2048,256]{1,0:T(8,128)(2,1)} %get-tuple-element.21.refs_4_), channel_id=1, source_target_pairs={{4,0},{8,4},{12,8},{0,12},{5,1},{9,5},{13,9},{1,13},{6,2},{10,6},{... | collective-permute-start | bytes 3145736 | tf_op jit(solution)/shard_map/ppermute | solution.py:239
  17.1 19.1 %collective-permute-done.3.refs_0_ = bf16[2048,256]{1,0:T(8,128)(2,1)} collective-permute-done((bf16[2048,256]{1,0:T(8,128)(2,1)}, bf16[2048,256]{1,0:T(8,128)(2,1)}, u32[]{:S(2)}, u32[]{:S(2)}) %collective-permute-start.3) | collective-permute-done | bytes 1048608 | tf_op jit(solution)/shard_map/ppermute | solution.py:237
  36.6 2.7 %collective-permute-done.6.refs_3_ = bf16[2048,256]{1,0:T(8,128)(2,1)S(1)} collective-permute-done((bf16[2048,256]{1,0:T(8,128)(2,1)}, bf16[2048,256]{1,0:T(8,128)(2,1)S(1)}, u32[]{:S(2)}, u32[]{:S(2)}) %collective-permute-start.6) | collective-permute-done | bytes 1048608 | tf_op jit(solution)/shard_map/ppermute | solution.py:238
  39.6 10.6 %collective-permute-done.refs_1_ = bf16[4096,256]{1,0:T(8,128)(2,1)} collective-permute-done((bf16[4096,256]{1,0:T(8,128)(2,1)S(1)}, bf16[4096,256]{1,0:T(8,128)(2,1)}, u32[]{:S(2)}, u32[]{:S(2)}) %collective-permute-start) | collective-permute-done | bytes 2097184 | tf_op jit(solution)/shard_map/ppermute | solution.py:221
  50.2 1.6 %collective-permute-start.11 = (bf16[2048,256]{1,0:T(8,128)(2,1)S(1)}, bf16[2048,256]{1,0:T(8,128)(2,1)S(1)}, u32[]{:S(2)}, u32[]{:S(2)}) collective-permute-start(bf16[2048,256]{1,0:T(8,128)(2,1)S(1)} %collective-permute-done.6.refs_3_), channel_id=1, source_target_pairs={{12,0},{0,4},{4,8},{8,12},{13,1},{1,5},{5,9},{9,13},{14,2},{2,6},{... | collective-permute-start | bytes 3145736 | tf_op jit(solution)/shard_map/ppermute | solution.py:242
  51.8 1.3 %slice.8 = bf16[2048,256]{1,0:T(8,128)(2,1)S(1)} slice(bf16[4096,256]{1,0:T(8,128)(2,1)} %collective-permute-done.refs_1_), slice={[0:2048], [0:256]} | slice | bytes 2097152 | tf_op jit(solution)/shard_map/slice | solution.py:229
  53.4 3.3 %collective-permute-start.8 = (bf16[2048,256]{1,0:T(8,128)(2,1)S(1)}, bf16[2048,256]{1,0:T(8,128)(2,1)S(1)}, u32[]{:S(2)}, u32[]{:S(2)}) collective-permute-start(bf16[2048,256]{1,0:T(8,128)(2,1)S(1)} %slice.8), channel_id=1, source_target_pairs={{1,0},{2,1},{3,2},{0,3},{5,4},{6,5},{7,6},{4,7},{9,8},{10,9},{11,1... | collective-permute-start | bytes 3145736 | tf_op jit(solution)/shard_map/ppermute | solution.py:229
  56.7 1.3 %slice.9 = bf16[2048,256]{1,0:T(8,128)(2,1)S(1)} slice(bf16[4096,256]{1,0:T(8,128)(2,1)} %collective-permute-done.1.refs_2_), slice={[2048:4096], [0:256]} | slice | bytes 2097152 | tf_op jit(solution)/shard_map/slice | solution.py:230
  58.6 4.9 %shard_map.56 = (f32[3,128,256]{2,1,0:T(8,128)S(1)}, bf16[3,128,256]{2,1,0:T(8,128)(2,1)S(1)}, bf16[2048,256]{1,0:T(8,128)(2,1)S(1)}, bf16[2048,256]{1,0:T(8,128)(2,1)S(1)}, bf16[3,2,256,2048]{3,2,1,0:T(8,128)(2,1)S(1)}) custom-call(s32[9]{0:T(128)S(1)} %pad_add_fusion.scalars, bf16[4096,256]{1,0:T(8,128)(2,1)S(1)} %broadcast_multiply_fusion.tiles_ref.refs_0_, ...), custom_call_target="tpu_custom_call" | custom-call | flops 16106127360 | bytes 1048576 | tf_op jit(solution)/shard_map/pallas_call | solution.py:134
  63.5 5.2 %shard_map.57 = (f32[6,128,256]{2,1,0:T(8,128)S(1)}, bf16[6,128,256]{2,1,0:T(8,128)(2,1)S(1)}, bf16[2048,256]{1,0:T(8,128)(2,1)S(1)}, bf16[2048,256]{1,0:T(8,128...) custom-call(s32[9]{0:T(128)S(1)} %pad_add_fusion.scalars, ...), custom_call_target="tpu_custom_call" | custom-call | flops 3221225472 | bytes 1048576 | tf_op jit(solution)/shard_map/pallas_call | solution.py:134
  68.7 4.2 %collective-permute-start.7 = (bf16[6,128,256]{2,1,0:T(8,128)(2,1)S(1)}, bf16[6,128,256]{2,1,0:T(8,128)(2,1)S(1)}, u32[]{:S(2)}, u32[]{:S(2)}) collective-permute-start(bf16[6,128,256]{2,1,0:T(8,128)(2,1)S(1)} %get-tuple-element.26), channel_id=1, source_target_pairs={{0,16},{16,0},{1,17},{17,1},{2,18},{18,2},{3,19},{19,3},{4,20},{20... | collective-permute-start | bytes 1179656 | tf_op jit(solution)/shard_map/ppermute | solution.py:270
  72.9 8.2 %collective-permute-done.10.refs_6_ = bf16[2048,256]{1,0:T(8,128)(2,1)S(1)} collective-permute-done((bf16[2048,256]{1,0:T(8,128)(2,1)}, bf16[2048,256]{1,0:T(8,128)(2,1)S(1)}, u32[]{:S(2)}, u32[]{:S(2)}) %collective-permute-start.10) | collective-permute-done | bytes 1048608 | tf_op jit(solution)/shard_map/ppermute | solution.py:241
  81.1 1.9 %collective-permute-start.2 = (bf16[3,128,256]{2,1,0:T(8,128)(2,1)S(1)}, bf16[3,128,256]{2,1,0:T(8,128)(2,1)S(1)}, u32[]{:S(2)}, u32[]{:S(2)}) collective-permute-start(bf16[3,128,256]{2,1,0:T(8,128)(2,1)S(1)} %get-tuple-element.23), channel_id=1, source_target_pairs={{0,16},{16,0},{1,17},{17,1},{2,18},{18,2},{3,19},{19,3},{4,20},{20... | collective-permute-start | bytes 589832 | tf_op jit(solution)/shard_map/ppermute | solution.py:270
  84.1 4.7 %shard_map.58 = (f32[7,128,256]{2,1,0:T(8,128)S(1)}, bf16[7,128,256]{2,1,0:T(8,128)(2,1)S(1)}) custom-call(s32[9]{0:T(128)S(1)} %pad_add_fusion.scalars, bf16[2048,256]{1,0:T(8,128)(2,1)S(1)} %collective-permute-done.8.refs_0_, bf16[2048,256]{1,0:T(8,128)(2,1)S(1)} %collective-permute-done.9.refs_1_, bf16[2048,256]{1,0:T(8,128)(2,1)S(1)} %get-tuple-element.27.refs_2_, ...), custom_call_target="tpu_custom_call" | custom-call | flops 3758096384 | bytes 1048576 | tf_op jit(solution)/shard_map/pallas_call | solution.py:134
  88.7 2.4 %collective-permute-start.12 = (bf16[7,128,256]{2,1,0:T(8,128)(2,1)S(1)}, bf16[7,128,256]{2,1,0:T(8,128)(2,1)S(1)}, u32[]{:S(2)}, u32[]{:S(2)}) collective-permute-start(bf16[7,128,256]{2,1,0:T(8,128)(2,1)S(1)} %get-tuple-element.34), channel_id=1, source_target_pairs={{0,16},{16,0},{1,17},{17,1},{2,18},{18,2},{3,19},{19,3},{4,20},{20... | collective-permute-start | bytes 1376264 | tf_op jit(solution)/shard_map/ppermute | solution.py:270
  91.2 1.4 %collective-permute-done.12.refs_5_ = bf16[7,128,256]{2,1,0:T(8,128)(2,1)S(1)} collective-permute-done((bf16[7,128,256]{2,1,0:T(8,128)(2,1)S(1)}, bf16[7,128,256]{2,1,0:T(8,128)(2,1)S(1)}, u32[]{:S(2)}, u32[]{:S(2)}) %collective-permute-start.12) | collective-permute-done | bytes 458784 | tf_op jit(solution)/shard_map/ppermute | solution.py:270
  93.3 22.7 %all_to_all.5.parts_ref = bf16[16,128,256]{2,1,0:T(8,128)(2,1)S(1)} all-to-all(bf16[16,128,256]{2,1,0:T(8,128)(2,1)S(1)} %shard_map.59), channel_id=1, replica_groups=mesh['y'=4,'c'=2,'z'=4,'x'=4] {'y','x'}, dimensions={0} | all-to-all | bytes 2097152 | tf_op jit(solution)/shard_map/all_to_all | solution.py:272
  116.7 1.9 %collective-permute-start.13 = (f32[2,128,256]{2,1,0:T(8,128)S(1)}, f32[2,128,256]{2,1,0:T(8,128)S(1)}, u32[]{:S(2)}, u32[]{:S(2)}) collective-permute-start(f32[2,128,256]{2,1,0:T(8,128)S(1)} %shard_map.60), channel_id=1, source_target_pairs={{0,16},{16,0},{1,17},{17,1},{2,18},{18,2},{3,19},{19,3},{4,20},{20... | collective-permute-start | bytes 786440 | tf_op jit(solution)/shard_map/ppermute | solution.py:273
  118.5 1.2 collective-permute-done.13.other_ref
  119.7 1.4 %shard_map.61 = f32[256,512]{1,0:T(8,128)} custom-call(s32[9]{0:T(128)S(1)} %pad_add_fusion.scalars, bf16[16,128,256]{2,1,0:T(8,128)(2,1)S(1)} %all_to_all.5.parts_ref, f32[2,128,256]{2,1,0:T(8,128)S(1)} %collective-permute-done.13.other_ref), custom_call_target="tpu_custom_call" | custom-call | flops 262144 | bytes 1048576 | tf_op jit(solution)/shard_map/pallas_call | solution.py:208
  (25 shorter events, 4.9 us)
Async XLA Ops:
  0.7 5.2 %copy-start = (bf16[16,64,64]{2,1,0:T(8,128)(2,1)S(1)}, bf16[16,64,64]{2,1,0:T(8,128)(2,1)}, u32[]{:S(2)}) copy-start(bf16[16,64,64]{2,1,0:T(8,128)(2,1)} %occ_ref.1) | copy-start | bytes 393220
  0.7 5.2 %copy-start.1 = (bf16[16,64,64]{2,1,0:T(8,128)(2,1)S(1)}, bf16[16,64,64]{2,1,0:T(8,128)(2,1)}, u32[]{:S(2)}) copy-start(bf16[16,64,64]{2,1,0:T(8,128)(2,1)} %virt_ref.1) | copy-start | bytes 393220
  0.7 5.2 %copy-start.2 = (s32[1,2]{1,0:T(1,128)S(1)}, s32[1,2]{1,0:T(1,128)}, u32[]{:S(2)}) copy-start(s32[1,2]{1,0:T(1,128)} %pairs.1) | copy-start | bytes 28
  2.5 47.7 %collective-permute-start = (bf16[4096,256]{1,0:T(8,128)(2,1)S(1)}, bf16[4096,256]{1,0:T(8,128)(2,1)}, u32[]{:S(2)}, u32[]{:S(2)}) collective-permute-start(bf16[4096,256]{1,0:T(8,128)(2,1)S(1)} %broadcast_multiply_fusion.tiles_ref.refs_0_), channel_id=1, source_target_pairs={{1,0},{2,1},{3,2},{0,3},{5,4},{6,5},{7,6},{4,7},{9,8},{10,9},{11,1... | collective-permute-start | bytes 6291464 | tf_op jit(solution)/shard_map/ppermute | solution.py:221
  5.9 47.5 %collective-permute-start.1 = (bf16[4096,256]{1,0:T(8,128)(2,1)S(1)}, bf16[4096,256]{1,0:T(8,128)(2,1)}, u32[]{:S(2)}, u32[]{:S(2)}) collective-permute-start(bf16[4096,256]{1,0:T(8,128)(2,1)S(1)} %broadcast_multiply_fusion.tiles_ref.refs_0_), channel_id=1, source_target_pairs={{3,0},{0,1},{1,2},{2,3},{7,4},{4,5},{5,6},{6,7},{11,8},{8,9},{9,10... | collective-permute-start | bytes 6291464 | tf_op jit(solution)/shard_map/ppermute | solution.py:221
  10.6 25.6 %collective-permute-start.3 = (bf16[2048,256]{1,0:T(8,128)(2,1)}, bf16[2048,256]{1,0:T(8,128)(2,1)}, u32[]{:S(2)}, u32[]{:S(2)}) collective-permute-start(bf16[2048,256]{1,0:T(8,128)(2,1)} %get-tuple-element.20.refs_3_), channel_id=1, source_target_pairs={{4,0},{8,4},{12,8},{0,12},{5,1},{9,5},{13,9},{1,13},{6,2},{10,6},{... | collective-permute-start | bytes 3145736 | tf_op jit(solution)/shard_map/ppermute | solution.py:237
  14.3 24.9 %collective-permute-start.6 = (bf16[2048,256]{1,0:T(8,128)(2,1)}, bf16[2048,256]{1,0:T(8,128)(2,1)S(1)}, u32[]{:S(2)}, u32[]{:S(2)}) collective-permute-start(bf16[2048,256]{1,0:T(8,128)(2,1)} %get-tuple-element.21.refs_4_), channel_id=1, source_target_pairs={{12,0},{0,4},{4,8},{8,12},{13,1},{1,5},{5,9},{9,13},{14,2},{2,6},{... | collective-permute-start | bytes 3145736 | tf_op jit(solution)/shard_map/ppermute | solution.py:238
  14.3 44.3 %collective-permute-start.4 = (bf16[2048,256]{1,0:T(8,128)(2,1)}, bf16[2048,256]{1,0:T(8,128)(2,1)}, u32[]{:S(2)}, u32[]{:S(2)}) collective-permute-start(bf16[2048,256]{1,0:T(8,128)(2,1)} %get-tuple-element.21.refs_4_), channel_id=1, source_target_pairs={{4,0},{8,4},{12,8},{0,12},{5,1},{9,5},{13,9},{1,13},{6,2},{10,6},{... | collective-permute-start | bytes 3145736 | tf_op jit(solution)/shard_map/ppermute | solution.py:239
  36.2 27.4 %collective-permute-start.5 = (bf16[2048,256]{1,0:T(8,128)(2,1)}, bf16[2048,256]{1,0:T(8,128)(2,1)S(1)}, u32[]{:S(2)}, u32[]{:S(2)}) collective-permute-start(bf16[2048,256]{1,0:T(8,128)(2,1)} %get-tuple-element.20.refs_3_), channel_id=1, source_target_pairs={{12,0},{0,4},{4,8},{8,12},{13,1},{1,5},{5,9},{9,13},{14,2},{2,6},{... | collective-permute-start | bytes 3145736 | tf_op jit(solution)/shard_map/ppermute | solution.py:240
  39.3 41.8 %collective-permute-start.10 = (bf16[2048,256]{1,0:T(8,128)(2,1)}, bf16[2048,256]{1,0:T(8,128)(2,1)S(1)}, u32[]{:S(2)}, u32[]{:S(2)}) collective-permute-start(bf16[2048,256]{1,0:T(8,128)(2,1)} %collective-permute-done.3.refs_0_), channel_id=1, source_target_pairs={{4,0},{8,4},{12,8},{0,12},{5,1},{9,5},{13,9},{1,13},{6,2},{10,6},{... | collective-permute-start | bytes 3145736 | tf_op jit(solution)/shard_map/ppermute | solution.py:241
  50.2 32.8 %collective-permute-start.11 = (bf16[2048,256]{1,0:T(8,128)(2,1)S(1)}, bf16[2048,256]{1,0:T(8,128)(2,1)S(1)}, u32[]{:S(2)}, u32[]{:S(2)}) collective-permute-start(bf16[2048,256]{1,0:T(8,128)(2,1)S(1)} %collective-permute-done.6.refs_3_), channel_id=1, source_target_pairs={{12,0},{0,4},{4,8},{8,12},{13,1},{1,5},{5,9},{9,13},{14,2},{2,6},{... | collective-permute-start | bytes 3145736 | tf_op jit(solution)/shard_map/ppermute | solution.py:242
  53.4 30.7 %collective-permute-start.8 = (bf16[2048,256]{1,0:T(8,128)(2,1)S(1)}, bf16[2048,256]{1,0:T(8,128)(2,1)S(1)}, u32[]{:S(2)}, u32[]{:S(2)}) collective-permute-start(bf16[2048,256]{1,0:T(8,128)(2,1)S(1)} %slice.8), channel_id=1, source_target_pairs={{1,0},{2,1},{3,2},{0,3},{5,4},{6,5},{7,6},{4,7},{9,8},{10,9},{11,1... | collective-permute-start | bytes 3145736 | tf_op jit(solution)/shard_map/ppermute | solution.py:229
  58.6 25.4 %collective-permute-start.9 = (bf16[2048,256]{1,0:T(8,128)(2,1)S(1)}, bf16[2048,256]{1,0:T(8,128)(2,1)S(1)}, u32[]{:S(2)}, u32[]{:S(2)}) collective-permute-start(bf16[2048,256]{1,0:T(8,128)(2,1)S(1)} %slice.9), channel_id=1, source_target_pairs={{3,0},{0,1},{1,2},{2,3},{7,4},{4,5},{5,6},{6,7},{11,8},{8,9},{9,10... | collective-permute-start | bytes 3145736 | tf_op jit(solution)/shard_map/ppermute | solution.py:230
  68.7 15.3 %collective-permute-start.7 = (bf16[6,128,256]{2,1,0:T(8,128)(2,1)S(1)}, bf16[6,128,256]{2,1,0:T(8,128)(2,1)S(1)}, u32[]{:S(2)}, u32[]{:S(2)}) collective-permute-start(bf16[6,128,256]{2,1,0:T(8,128)(2,1)S(1)} %get-tuple-element.26), channel_id=1, source_target_pairs={{0,16},{16,0},{1,17},{17,1},{2,18},{18,2},{3,19},{19,3},{4,20},{20... | collective-permute-start | bytes 1179656 | tf_op jit(solution)/shard_map/ppermute | solution.py:270
  81.1 2.9 %collective-permute-start.2 = (bf16[3,128,256]{2,1,0:T(8,128)(2,1)S(1)}, bf16[3,128,256]{2,1,0:T(8,128)(2,1)S(1)}, u32[]{:S(2)}, u32[]{:S(2)}) collective-permute-start(bf16[3,128,256]{2,1,0:T(8,128)(2,1)S(1)} %get-tuple-element.23), channel_id=1, source_target_pairs={{0,16},{16,0},{1,17},{17,1},{2,18},{18,2},{3,19},{19,3},{4,20},{20... | collective-permute-start | bytes 589832 | tf_op jit(solution)/shard_map/ppermute | solution.py:270
  88.7 3.9 %collective-permute-start.12 = (bf16[7,128,256]{2,1,0:T(8,128)(2,1)S(1)}, bf16[7,128,256]{2,1,0:T(8,128)(2,1)S(1)}, u32[]{:S(2)}, u32[]{:S(2)}) collective-permute-start(bf16[7,128,256]{2,1,0:T(8,128)(2,1)S(1)} %get-tuple-element.34), channel_id=1, source_target_pairs={{0,16},{16,0},{1,17},{17,1},{2,18},{18,2},{3,19},{19,3},{4,20},{20... | collective-permute-start | bytes 1376264 | tf_op jit(solution)/shard_map/ppermute | solution.py:270
  116.7 3.0 %collective-permute-start.13 = (f32[2,128,256]{2,1,0:T(8,128)S(1)}, f32[2,128,256]{2,1,0:T(8,128)S(1)}, u32[]{:S(2)}, u32[]{:S(2)}) collective-permute-start(f32[2,128,256]{2,1,0:T(8,128)S(1)} %shard_map.60), channel_id=1, source_target_pairs={{0,16},{16,0},{1,17},{17,1},{2,18},{18,2},{3,19},{19,3},{4,20},{20... | collective-permute-start | bytes 786440 | tf_op jit(solution)/shard_map/ppermute | solution.py:273

commit v6 on v5

--- a/solution.py
+++ b/solution.py
@@ -18,6 +18,7 @@
 COSTS = (10, 1, 1)
 NEAR = (0, 1, 3)
 LIMIT = 12
+LOW = 1920
 IN_VMEM = pl.BlockSpec(memory_space=pltpu.VMEM)
 IN_SMEM = pl.BlockSpec(memory_space=pltpu.SMEM)
 F32 = jnp.float32
@@ -51,8 +52,12 @@
     for g in range(width // four):
         part = half_ref[g * four : (g + 1) * four].reshape(side, cols)
         done = jnp.dot(virt_wide, part, preferred_element_type=F32).astype(BF16)
-        out_ref, h = (low_ref, g) if g < width // 8 else (high_ref, g - width // 8)
-        out_ref[h * side : (h + 1) * side, :] = done
+        start = g * side
+        cut = min(max(LOW - start, 0), side)
+        if cut > 0:
+            low_ref[start : start + cut, :] = done[:cut]
+        if cut < side:
+            high_ref[start + cut - LOW : start + side - LOW, :] = done[cut:]
 
 
 def contract(pairs, tiles, green_occ, green_virt):
@@ -62,7 +67,7 @@
         functools.partial(contract_kernel, width, 16),
         in_specs=[IN_SMEM, IN_VMEM, IN_VMEM, IN_VMEM],
         out_specs=[IN_VMEM, IN_VMEM],
-        out_shape=[jax.ShapeDtypeStruct((rows // 2, cols), BF16)] * 2,
+        out_shape=[jax.ShapeDtypeStruct((n, cols), BF16) for n in (LOW, rows - LOW)],
         scratch_shapes=[pltpu.VMEM((width, width, cols), BF16)],
         compiler_params=pltpu.CompilerParams(vmem_limit_bytes=12 * 2**20),
         cost_estimate=pl.CostEstimate(
@@ -78,6 +83,7 @@
     core = scalars[8]
 
     for h in range(2):
+        part_of = slice(0, LOW) if h == 0 else slice(LOW, None)
         rights = {q: refs[places[h]][...] for q, places in right_at.items()}
         if emit:
             for n, q in enumerate(right_at):
@@ -85,15 +91,14 @@
         for p in sorted({p for p, _ in pairs}):
             if p in left_at:
                 places = left_at[p]
-                rows = rights[pairs[0][1]].shape[0]
                 if len(places) == 2:
                     left = refs[places[h]][...].T
                 else:
-                    left = refs[places[0]][h * rows : (h + 1) * rows, :].T
+                    left = refs[places[0]][part_of, :].T
                 if emit:
-                    kept[-1][NEAR.index(p), h] = left
+                    kept[-1][NEAR.index(p), :, part_of] = left
             else:
-                left = refs[turned_at][NEAR.index(p), h]
+                left = refs[turned_at][NEAR.index(p), :, part_of]
             for i, (task_p, q) in enumerate(pairs):
                 if task_p == p:
                     part = jnp.dot(left, rights[q], preferred_element_type=F32)
@@ -122,15 +127,15 @@
         operands.append(array)
         specs.append(pl.BlockSpec(memory_space=pl.ANY))
     count = len(pairs)
-    half = rights[pairs[0][1]][0].shape
+    rows = sum(half.shape[0] for half in rights[pairs[0][1]])
     shapes = [
         jax.ShapeDtypeStruct((count, HALF, BLOCK), F32),
         jax.ShapeDtypeStruct((count, HALF, BLOCK), BF16),
     ]
     if emit:
-        shapes += [jax.ShapeDtypeStruct(half, BF16)] * (2 * len(right_at))
+        shapes += [jax.ShapeDtypeStruct((n, BLOCK), BF16) for n in (LOW, rows - LOW)] * len(right_at)
         if turned is None:
-            shapes.append(jax.ShapeDtypeStruct((len(NEAR), 2, BLOCK, half[0]), BF16))
+            shapes.append(jax.ShapeDtypeStruct((len(NEAR), BLOCK, rows), BF16))
     outs = pl.pallas_call(
         functools.partial(
             products_kernel, pairs, left_at, right_at, turned_at, emit, len(operands)
@@ -141,7 +146,7 @@
         scratch_shapes=[pltpu.VMEM((count, BLOCK, BLOCK), F32)],
         compiler_params=pltpu.CompilerParams(vmem_limit_bytes=LIMIT * 2**20),
         cost_estimate=pl.CostEstimate(
-            flops=cost * 2 * count * 2 * half[0] * BLOCK * BLOCK,
+            flops=cost * 2 * count * rows * BLOCK * BLOCK,
             bytes_accessed=2**20,
             transcendentals=0,
         ),
@@ -195,24 +200,45 @@
     )(scalars, parts)
 
 
-def place_kernel(scalars, parts_ref, other_ref, out_ref):
-    core = scalars[8]
-    own = pl.ds(pl.multiple_of(core * HALF, HALF), HALF)
-    rest = pl.ds(pl.multiple_of((1 - core) * HALF, HALF), HALF)
+def mine_kernel(scalars, parts_ref, out_ref):
     for j in range(2):
-        out_ref[own, j * BLOCK : (j + 1) * BLOCK] = added(core, parts_ref, j)
-        out_ref[rest, j * BLOCK : (j + 1) * BLOCK] = other_ref[j]
-
-
-def place(scalars, parts, other):
-    return pl.pallas_call(
-        place_kernel,
-        in_specs=[IN_SMEM, IN_VMEM, IN_VMEM],
-        out_specs=IN_VMEM,
+        out_ref[:, j * BLOCK : (j + 1) * BLOCK] = added(scalars[8], parts_ref, j)
+
+
+def mine(scalars, parts):
+    return pl.pallas_call(
+        mine_kernel,
+        grid_spec=pltpu.PrefetchScalarGridSpec(
+            num_scalar_prefetch=1,
+            grid=(1,),
+            in_specs=[IN_VMEM],
+            out_specs=pl.BlockSpec((HALF, 2 * BLOCK), lambda i, s: (s[8], 0)),
+        ),
         out_shape=jax.ShapeDtypeStruct((BLOCK, 2 * BLOCK), F32),
         compiler_params=pltpu.CompilerParams(vmem_limit_bytes=12 * 2**20),
-        cost_estimate=pl.CostEstimate(flops=2**18, bytes_accessed=2**20, transcendentals=0),
-    )(scalars, parts, other)
+        cost_estimate=pl.CostEstimate(flops=2**20, bytes_accessed=2**20, transcendentals=0),
+    )(scalars, parts)
+
+
+def place_kernel(scalars, other_ref, whole_ref, out_ref):
+    for j in range(2):
+        out_ref[:, j * BLOCK : (j + 1) * BLOCK] = other_ref[j]
+
+
+def place(scalars, other, whole):
+    return pl.pallas_call(
+        place_kernel,
+        grid_spec=pltpu.PrefetchScalarGridSpec(
+            num_scalar_prefetch=1,
+            grid=(1,),
+            in_specs=[IN_VMEM, pl.BlockSpec(memory_space=pl.ANY)],
+            out_specs=pl.BlockSpec((HALF, 2 * BLOCK), lambda i, s: (1 - s[8], 0)),
+        ),
+        out_shape=jax.ShapeDtypeStruct((BLOCK, 2 * BLOCK), F32),
+        input_output_aliases={2: 0},
+        compiler_params=pltpu.CompilerParams(vmem_limit_bytes=12 * 2**20),
+        cost_estimate=pl.CostEstimate(flops=2**18, bytes_accessed=2**19, transcendentals=0),
+    )(scalars, other, whole)
 
 
 def ring(block, axis):
@@ -222,12 +248,11 @@
 
 
 def far(after, before, axis):
-    half = after.shape[0] // 2
     take_next = [((i + 1) % SIDE, i) for i in range(SIDE)]
     take_prev = [((i - 1) % SIDE, i) for i in range(SIDE)]
     return (
-        lax.ppermute(after[:half], axis, take_next),
-        lax.ppermute(before[half:], axis, take_prev),
+        lax.ppermute(after[:LOW], axis, take_next),
+        lax.ppermute(before[LOW:], axis, take_prev),
     )
 
 
@@ -270,7 +295,8 @@
         halves += [keep, lax.ppermute(send, "c", swap)]
     sends = merge(scalars, GROUPS, halves)
     parts = lax.all_to_all(sends, ("y", "x"), 0, 0)
-    return place(scalars, parts, lax.ppermute(theirs(scalars, parts), "c", swap))
+    other = lax.ppermute(theirs(scalars, parts), "c", swap)
+    return place(scalars, other, mine(scalars, parts))
 
 
 def solution(mesh):

time: 121 us -> 121 us (level)
  Pallas kernels: 22.1 us -> 23.6 us
  starting transfers between devices: 25.8 us -> 24.4 us
    ppermute x1, waiting for transfers between devices: 0.26 us -> 13.6 us  [ring(): lax.ppermute(block, axis, take_prev)]
    ppermute x1, waiting for transfers between devices: 10.6 us -> 0.01 us  [ring(): lax.ppermute(block, axis, take_next)]
    ppermute x1, waiting for transfers between devices: 8.22 us -> 5.68 us  [around(): far_low = lax.ppermute(after_low, axis, take_next)]
    ppermute x1, waiting for transfers between devices: 2.67 us -> 0.45 us  [around(): before_high = lax.ppermute(high, axis, take_prev)]
    ppermute x1, waiting for transfers between devices: 0.01 us -> 1.98 us  [around(): before_low = lax.ppermute(low, axis, take_prev)]
    ppermute x1, starting transfers between devices: 3.75 us -> 2.12 us  [around(): after_low = lax.ppermute(low, axis, take_next)]
    ppermute x1, starting transfers between devices: 0.01 us -> 1.63 us  [around(): before_high = lax.ppermute(high, axis, take_prev)]
    ppermute x3, starting transfers between devices: 8.44 us -> 6.94 us  [per_device(): halves += [keep, lax.ppermute(send, 'c', swap)]]
  transfers between devices with their start and end apart: 14 -> 14, of which waited for: 9 -> 7; matrix products, arithmetic and copies ran while one was open for 2% -> 2% of each run, Pallas kernels for 12% -> 13%
where the time goes in v6:
time: 121 us
  waiting for transfers between devices  44.7 us (37%)
  starting transfers between devices  24.4 us (20%)
  Pallas kernels  23.6 us (20%)
  blocking collectives  22.5 us (19%)
  local copies, waits for them, and re-layouts  2.67 us (2%)
  other arithmetic  2.53 us (2%)
    all_to_all x1, blocking collectives, per_device(): parts = lax.all_to_all(sends, ('y', 'x'), 0, 0)  22.5 us
    ppermute x1, waiting for transfers between devices, around(): after_low = lax.ppermute(low, axis, take_next)  20.5 us
    pallas_call x3, Pallas kernels, products(): pl.pallas_call(functools.partial(products_kernel, pairs, left_at, right_a...  15 us
    ppermute x1, waiting for transfers between devices, ring(): lax.ppermute(block, axis, take_prev)  13.6 us
    ppermute x3, starting transfers between devices, per_device(): halves += [keep, lax.ppermute(send, 'c', swap)]  6.94 us
    ppermute x1, waiting for transfers between devices, around(): far_low = lax.ppermute(after_low, axis, take_next)  5.68 us
    pallas_call x1, Pallas kernels, contract(): pl.pallas_call(functools.partial(contract_kernel, width, 16), in_specs=[I...  4.68 us
    ppermute x1, starting transfers between devices, ring(): lax.ppermute(block, axis, take_next)  3.38 us
  transfers between devices with their start and end apart: 14, of which 7 were waited for; matrix products, arithmetic and copies ran while one was open for 2% of the time, Pallas kernels for 13%

profile of v6, /device:TPU:1, one launch (start us, length us, event | category | flops | bytes accessed | tf_op | source)
XLA Modules:
  0.0 120.5 jit_solution(2617751793238974885)
XLA Ops:
  0.7 1.8 %broadcast_multiply_fusion.tiles_ref.refs_0_ = bf16[4096,256]{1,0:T(8,128)(2,1)S(1)} fusion(bf16[4096,256]{1,0:T(8,128)(2,1)} %param.5, bf16[256]{0:T(256)(128)(2,1)S(1)} %broadcast_bitcast_fusion), kind=kLoop, calls=%fused_computation | loop fusion | flops 1048576 | bytes 4194816 | tf_op jit(solution)/shard_map/mul | solution.py:281
  2.5 3.4 %collective-permute-start = (bf16[4096,256]{1,0:T(8,128)(2,1)S(1)}, bf16[4096,256]{1,0:T(8,128)(2,1)}, u32[]{:S(2)}, u32[]{:S(2)}) collective-permute-start(bf16[4096,256]{1,0:T(8,128)(2,1)S(1)} %broadcast_multiply_fusion.tiles_ref.refs_0_), channel_id=1, source_target_pairs={{1,0},{2,1},{3,2},{0,3},{5,4},{6,5},{7,6},{4,7},{9,8},{10,9},{11,1... | collective-permute-start | bytes 6291464 | tf_op jit(solution)/shard_map/ppermute | solution.py:247
  5.9 4.7 %shard_map.55 = (bf16[1920,256]{1,0:T(8,128)(2,1)}, bf16[2176,256]{1,0:T(8,128)(2,1)}) custom-call(s32[1,2]{1,0:T(1,128)S(1)} %copy-done.2, bf16[4096,256]{1,0:T(8,128)(2,1)S(1)} %broadcast_multiply_fusion.tiles_ref.refs_0_, bf16[16,64,64]{2,1,0:T(8,128)(2,1)S(1)} %copy-done, bf16[16,64,64]{2,1,0:T(8,128)(2,1)S(1)} %copy-done.1), custom_call_target="tpu_custom_call" | custom-call | flops 40000000000 | bytes 4194304 | tf_op jit(solution)/shard_map/pallas_call | solution.py:66
  10.6 1.6 %collective-permute-start.6 = (bf16[2176,256]{1,0:T(8,128)(2,1)}, bf16[2176,256]{1,0:T(8,128)(2,1)S(1)}, u32[]{:S(2)}, u32[]{:S(2)}) collective-permute-start(bf16[2176,256]{1,0:T(8,128)(2,1)} %get-tuple-element.21.refs_4_), channel_id=1, source_target_pairs={{12,0},{0,4},{4,8},{8,12},{13,1},{1,5},{5,9},{9,13},{14,2},{2,6},{... | collective-permute-start | bytes 3342344 | tf_op jit(solution)/shard_map/ppermute | solution.py:263
  12.2 2.1 %collective-permute-start.3 = (bf16[1920,256]{1,0:T(8,128)(2,1)}, bf16[1920,256]{1,0:T(8,128)(2,1)}, u32[]{:S(2)}, u32[]{:S(2)}) collective-permute-start(bf16[1920,256]{1,0:T(8,128)(2,1)} %get-tuple-element.20.refs_3_), channel_id=1, source_target_pairs={{4,0},{8,4},{12,8},{0,12},{5,1},{9,5},{13,9},{1,13},{6,2},{10,6},{... | collective-permute-start | bytes 2949128 | tf_op jit(solution)/shard_map/ppermute | solution.py:262
  14.5 20.5 %collective-permute-done.3.refs_0_ = bf16[1920,256]{1,0:T(8,128)(2,1)} collective-permute-done((bf16[1920,256]{1,0:T(8,128)(2,1)}, bf16[1920,256]{1,0:T(8,128)(2,1)}, u32[]{:S(2)}, u32[]{:S(2)}) %collective-permute-start.3) | collective-permute-done | bytes 983072 | tf_op jit(solution)/shard_map/ppermute | solution.py:262
  34.9 3.3 %collective-permute-start.4 = (bf16[2176,256]{1,0:T(8,128)(2,1)}, bf16[2176,256]{1,0:T(8,128)(2,1)S(1)}, u32[]{:S(2)}, u32[]{:S(2)}) collective-permute-start(bf16[2176,256]{1,0:T(8,128)(2,1)} %get-tuple-element.21.refs_4_), channel_id=1, source_target_pairs={{4,0},{8,4},{12,8},{0,12},{5,1},{9,5},{13,9},{1,13},{6,2},{10,6},{... | collective-permute-start | bytes 3342344 | tf_op jit(solution)/shard_map/ppermute | solution.py:264
  39.8 13.6 %collective-permute-done.1.refs_2_ = bf16[4096,256]{1,0:T(8,128)(2,1)} collective-permute-done((bf16[4096,256]{1,0:T(8,128)(2,1)S(1)}, bf16[4096,256]{1,0:T(8,128)(2,1)}, u32[]{:S(2)}, u32[]{:S(2)}) %collective-permute-start.1) | collective-permute-done | bytes 2097184 | tf_op jit(solution)/shard_map/ppermute | solution.py:247
  53.4 1.6 %collective-permute-start.11 = (bf16[2176,256]{1,0:T(8,128)(2,1)S(1)}, bf16[2176,256]{1,0:T(8,128)(2,1)S(1)}, u32[]{:S(2)}, u32[]{:S(2)}) collective-permute-start(bf16[2176,256]{1,0:T(8,128)(2,1)S(1)} %collective-permute-done.6.refs_3_), channel_id=1, source_target_pairs={{12,0},{0,4},{4,8},{8,12},{13,1},{1,5},{5,9},{9,13},{14,2},{2,6},{... | collective-permute-start | bytes 3342344 | tf_op jit(solution)/shard_map/ppermute | solution.py:267
  55.0 1.3 %slice.9 = bf16[2176,256]{1,0:T(8,128)(2,1)S(1)} slice(bf16[4096,256]{1,0:T(8,128)(2,1)} %collective-permute-done.1.refs_2_), slice={[1920:4096], [0:256]} | slice | bytes 2228224 | tf_op jit(solution)/shard_map/slice | solution.py:255
  56.5 1.3 %slice.8 = bf16[1920,256]{1,0:T(8,128)(2,1)S(1)} slice(bf16[4096,256]{1,0:T(8,128)(2,1)} %collective-permute-done.refs_1_), slice={[0:1920], [0:256]} | slice | bytes 1966080 | tf_op jit(solution)/shard_map/slice | solution.py:254
  57.7 2.0 %collective-permute-done.5.refs_2_ = bf16[1920,256]{1,0:T(8,128)(2,1)} collective-permute-done((bf16[1920,256]{1,0:T(8,128)(2,1)}, bf16[1920,256]{1,0:T(8,128)(2,1)}, u32[]{:S(2)}, u32[]{:S(2)}) %collective-permute-start.5) | collective-permute-done | bytes 983072 | tf_op jit(solution)/shard_map/ppermute | solution.py:265
  59.7 2.4 %collective-permute-start.8 = (bf16[1920,256]{1,0:T(8,128)(2,1)S(1)}, bf16[1920,256]{1,0:T(8,128)(2,1)S(1)}, u32[]{:S(2)}, u32[]{:S(2)}) collective-permute-start(bf16[1920,256]{1,0:T(8,128)(2,1)S(1)} %slice.8), channel_id=1, source_target_pairs={{1,0},{2,1},{3,2},{0,3},{5,4},{6,5},{7,6},{4,7},{9,8},{10,9},{11,1... | collective-permute-start | bytes 2949128 | tf_op jit(solution)/shard_map/ppermute | solution.py:254
  62.1 4.8 %shard_map.56 = (f32[3,128,256]{2,1,0:T(8,128)S(1)}, bf16[3,128,256]{2,1,0:T(8,128)(2,1)S(1)}, bf16[1920,256]{1,0:T(8,128)(2,1)S(1)}, bf16[2176,256]{1,0:T(8,128)(2,1)S(1)}, bf16[3,256,4096]{2,1,0:T(8,128)(2,1)S(1)}) custom-call(s32[9]{0:T(128)S(1)} %pad_add_fusion.scalars, bf16[4096,256]{1,0:T(8,128)(2,1)S(1)} %broadcast_multiply_fusion.tiles_ref.refs_0_, ...), custom_call_target="tpu_custom_call" | custom-call | flops 16106127360 | bytes 1048576 | tf_op jit(solution)/shard_map/pallas_call | solution.py:139
  66.9 5.3 %shard_map.57 = (f32[6,128,256]{2,1,0:T(8,128)S(1)}, bf16[6,128,256]{2,1,0:T(8,128)(2,1)S(1)}, bf16[1920,256]{1,0:T(8,128)(2,1)S(1)}, bf16[2176,256]{1,0:T(8,128...) custom-call(s32[9]{0:T(128)S(1)} %pad_add_fusion.scalars, ...), custom_call_target="tpu_custom_call" | custom-call | flops 3221225472 | bytes 1048576 | tf_op jit(solution)/shard_map/pallas_call | solution.py:139
  72.2 3.7 %collective-permute-start.7 = (bf16[6,128,256]{2,1,0:T(8,128)(2,1)S(1)}, bf16[6,128,256]{2,1,0:T(8,128)(2,1)S(1)}, u32[]{:S(2)}, u32[]{:S(2)}) collective-permute-start(bf16[6,128,256]{2,1,0:T(8,128)(2,1)S(1)} %get-tuple-element.26), channel_id=1, source_target_pairs={{0,16},{16,0},{1,17},{17,1},{2,18},{18,2},{3,19},{19,3},{4,20},{20... | collective-permute-start | bytes 1179656 | tf_op jit(solution)/shard_map/ppermute | solution.py:295
  75.9 5.7 %collective-permute-done.10.refs_6_ = bf16[1920,256]{1,0:T(8,128)(2,1)S(1)} collective-permute-done((bf16[1920,256]{1,0:T(8,128)(2,1)}, bf16[1920,256]{1,0:T(8,128)(2,1)S(1)}, u32[]{:S(2)}, u32[]{:S(2)}) %collective-permute-start.10) | collective-permute-done | bytes 983072 | tf_op jit(solution)/shard_map/ppermute | solution.py:266
  81.6 2.8 %collective-permute-start.2 = (bf16[3,128,256]{2,1,0:T(8,128)(2,1)S(1)}, bf16[3,128,256]{2,1,0:T(8,128)(2,1)S(1)}, u32[]{:S(2)}, u32[]{:S(2)}) collective-permute-start(bf16[3,128,256]{2,1,0:T(8,128)(2,1)S(1)} %get-tuple-element.23), channel_id=1, source_target_pairs={{0,16},{16,0},{1,17},{17,1},{2,18},{18,2},{3,19},{19,3},{4,20},{20... | collective-permute-start | bytes 589832 | tf_op jit(solution)/shard_map/ppermute | solution.py:295
  85.4 4.9 %shard_map.58 = (f32[7,128,256]{2,1,0:T(8,128)S(1)}, bf16[7,128,256]{2,1,0:T(8,128)(2,1)S(1)}) custom-call(s32[9]{0:T(128)S(1)} %pad_add_fusion.scalars, bf16[1920,256]{1,0:T(8,128)(2,1)S(1)} %collective-permute-done.8.refs_0_, bf16[2176,256]{1,0:T(8,128)(2,1)S(1)} %collective-permute-done.9.refs_1_, bf16[1920,256]{1,0:T(8,128)(2,1)S(1)} %get-tuple-element.27.refs_2_, ...), custom_call_target="tpu_custom_call" | custom-call | flops 3758096384 | bytes 1048576 | tf_op jit(solution)/shard_map/pallas_call | solution.py:139
  90.8 1.4 %collective-permute-done.12.refs_5_ = bf16[7,128,256]{2,1,0:T(8,128)(2,1)S(1)} collective-permute-done((bf16[7,128,256]{2,1,0:T(8,128)(2,1)S(1)}, bf16[7,128,256]{2,1,0:T(8,128)(2,1)S(1)}, u32[]{:S(2)}, u32[]{:S(2)}) %collective-permute-start.12) | collective-permute-done | bytes 458784 | tf_op jit(solution)/shard_map/ppermute | solution.py:295
  92.9 22.5 %all_to_all.5.parts_ref = bf16[16,128,256]{2,1,0:T(8,128)(2,1)S(1)} all-to-all(bf16[16,128,256]{2,1,0:T(8,128)(2,1)S(1)} %shard_map.59), channel_id=1, replica_groups=mesh['y'=4,'c'=2,'z'=4,'x'=4] {'y','x'}, dimensions={0} | all-to-all | bytes 2097152 | tf_op jit(solution)/shard_map/all_to_all | solution.py:297
  116.1 1.8 %collective-permute-start.13 = (f32[2,128,256]{2,1,0:T(8,128)S(1)}, f32[2,128,256]{2,1,0:T(8,128)S(1)}, u32[]{:S(2)}, u32[]{:S(2)}) collective-permute-start(f32[2,128,256]{2,1,0:T(8,128)S(1)} %shard_map.60), channel_id=1, source_target_pairs={{0,16},{16,0},{1,17},{17,1},{2,18},{18,2},{3,19},{19,3},{4,20},{20... | collective-permute-start | bytes 786440 | tf_op jit(solution)/shard_map/ppermute | solution.py:298
  117.9 1.3 %shard_map.61.whole_ref = f32[256,512]{1,0:T(8,128)} custom-call(s32[9]{0:T(128)S(1)} %pad_add_fusion.scalars, bf16[16,128,256]{2,1,0:T(8,128)(2,1)S(1)} %all_to_all.5.parts_ref), custom_call_target="tpu_custom_call" | custom-call | flops 1048576 | bytes 1048576 | tf_op jit(solution)/shard_map/pallas_call | solution.py:209
  119.3 1.3 %shard_map.62 = f32[256,512]{1,0:T(8,128)} custom-call(s32[9]{0:T(128)S(1)} %pad_add_fusion.scalars, f32[2,128,256]{2,1,0:T(8,128)S(1)} %collective-permute-done.13.other_ref, f32[256,512]{1,0:T(8,128)} %shard_map.61.whole_ref), custom_call_target="tpu_custom_call", output_to_operand_aliasing={{}: (2, {})} | custom-call | flops 262144 | bytes 524288 | tf_op jit(solution)/shard_map/pallas_call | solution.py:229
  (26 shorter events, 5.4 us)
Async XLA Ops:
  0.7 5.2 %copy-start = (bf16[16,64,64]{2,1,0:T(8,128)(2,1)S(1)}, bf16[16,64,64]{2,1,0:T(8,128)(2,1)}, u32[]{:S(2)}) copy-start(bf16[16,64,64]{2,1,0:T(8,128)(2,1)} %occ_ref.1) | copy-start | bytes 393220
  0.7 5.2 %copy-start.1 = (bf16[16,64,64]{2,1,0:T(8,128)(2,1)S(1)}, bf16[16,64,64]{2,1,0:T(8,128)(2,1)}, u32[]{:S(2)}) copy-start(bf16[16,64,64]{2,1,0:T(8,128)(2,1)} %virt_ref.1) | copy-start | bytes 393220
  0.7 5.2 %copy-start.2 = (s32[1,2]{1,0:T(1,128)S(1)}, s32[1,2]{1,0:T(1,128)}, u32[]{:S(2)}) copy-start(s32[1,2]{1,0:T(1,128)} %pairs.1) | copy-start | bytes 28
  2.5 53.8 %collective-permute-start = (bf16[4096,256]{1,0:T(8,128)(2,1)S(1)}, bf16[4096,256]{1,0:T(8,128)(2,1)}, u32[]{:S(2)}, u32[]{:S(2)}) collective-permute-start(bf16[4096,256]{1,0:T(8,128)(2,1)S(1)} %broadcast_multiply_fusion.tiles_ref.refs_0_), channel_id=1, source_target_pairs={{1,0},{2,1},{3,2},{0,3},{5,4},{6,5},{7,6},{4,7},{9,8},{10,9},{11,1... | collective-permute-start | bytes 6291464 | tf_op jit(solution)/shard_map/ppermute | solution.py:247
  5.9 47.5 %collective-permute-start.1 = (bf16[4096,256]{1,0:T(8,128)(2,1)S(1)}, bf16[4096,256]{1,0:T(8,128)(2,1)}, u32[]{:S(2)}, u32[]{:S(2)}) collective-permute-start(bf16[4096,256]{1,0:T(8,128)(2,1)S(1)} %broadcast_multiply_fusion.tiles_ref.refs_0_), channel_id=1, source_target_pairs={{3,0},{0,1},{1,2},{2,3},{7,4},{4,5},{5,6},{6,7},{11,8},{8,9},{9,10... | collective-permute-start | bytes 6291464 | tf_op jit(solution)/shard_map/ppermute | solution.py:247
  10.6 28.0 %collective-permute-start.6 = (bf16[2176,256]{1,0:T(8,128)(2,1)}, bf16[2176,256]{1,0:T(8,128)(2,1)S(1)}, u32[]{:S(2)}, u32[]{:S(2)}) collective-permute-start(bf16[2176,256]{1,0:T(8,128)(2,1)} %get-tuple-element.21.refs_4_), channel_id=1, source_target_pairs={{12,0},{0,4},{4,8},{8,12},{13,1},{1,5},{5,9},{9,13},{14,2},{2,6},{... | collective-permute-start | bytes 3342344 | tf_op jit(solution)/shard_map/ppermute | solution.py:263
  12.2 22.7 %collective-permute-start.3 = (bf16[1920,256]{1,0:T(8,128)(2,1)}, bf16[1920,256]{1,0:T(8,128)(2,1)}, u32[]{:S(2)}, u32[]{:S(2)}) collective-permute-start(bf16[1920,256]{1,0:T(8,128)(2,1)} %get-tuple-element.20.refs_3_), channel_id=1, source_target_pairs={{4,0},{8,4},{12,8},{0,12},{5,1},{9,5},{13,9},{1,13},{6,2},{10,6},{... | collective-permute-start | bytes 2949128 | tf_op jit(solution)/shard_map/ppermute | solution.py:262
  14.4 45.3 %collective-permute-start.5 = (bf16[1920,256]{1,0:T(8,128)(2,1)}, bf16[1920,256]{1,0:T(8,128)(2,1)}, u32[]{:S(2)}, u32[]{:S(2)}) collective-permute-start(bf16[1920,256]{1,0:T(8,128)(2,1)} %get-tuple-element.20.refs_3_), channel_id=1, source_target_pairs={{12,0},{0,4},{4,8},{8,12},{13,1},{1,5},{5,9},{9,13},{14,2},{2,6},{... | collective-permute-start | bytes 2949128 | tf_op jit(solution)/shard_map/ppermute | solution.py:265
  34.9 31.9 %collective-permute-start.4 = (bf16[2176,256]{1,0:T(8,128)(2,1)}, bf16[2176,256]{1,0:T(8,128)(2,1)S(1)}, u32[]{:S(2)}, u32[]{:S(2)}) collective-permute-start(bf16[2176,256]{1,0:T(8,128)(2,1)} %get-tuple-element.21.refs_4_), channel_id=1, source_target_pairs={{4,0},{8,4},{12,8},{0,12},{5,1},{9,5},{13,9},{1,13},{6,2},{10,6},{... | collective-permute-start | bytes 3342344 | tf_op jit(solution)/shard_map/ppermute | solution.py:264
  38.6 42.9 %collective-permute-start.10 = (bf16[1920,256]{1,0:T(8,128)(2,1)}, bf16[1920,256]{1,0:T(8,128)(2,1)S(1)}, u32[]{:S(2)}, u32[]{:S(2)}) collective-permute-start(bf16[1920,256]{1,0:T(8,128)(2,1)} %collective-permute-done.3.refs_0_), channel_id=1, source_target_pairs={{4,0},{8,4},{12,8},{0,12},{5,1},{9,5},{13,9},{1,13},{6,2},{10,6},{... | collective-permute-start | bytes 2949128 | tf_op jit(solution)/shard_map/ppermute | solution.py:266
  53.4 30.9 %collective-permute-start.11 = (bf16[2176,256]{1,0:T(8,128)(2,1)S(1)}, bf16[2176,256]{1,0:T(8,128)(2,1)S(1)}, u32[]{:S(2)}, u32[]{:S(2)}) collective-permute-start(bf16[2176,256]{1,0:T(8,128)(2,1)S(1)} %collective-permute-done.6.refs_3_), channel_id=1, source_target_pairs={{12,0},{0,4},{4,8},{8,12},{13,1},{1,5},{5,9},{9,13},{14,2},{2,6},{... | collective-permute-start | bytes 3342344 | tf_op jit(solution)/shard_map/ppermute | solution.py:267
  56.4 29.1 %collective-permute-start.9 = (bf16[2176,256]{1,0:T(8,128)(2,1)S(1)}, bf16[2176,256]{1,0:T(8,128)(2,1)S(1)}, u32[]{:S(2)}, u32[]{:S(2)}) collective-permute-start(bf16[2176,256]{1,0:T(8,128)(2,1)S(1)} %slice.9), channel_id=1, source_target_pairs={{3,0},{0,1},{1,2},{2,3},{7,4},{4,5},{5,6},{6,7},{11,8},{8,9},{9,10... | collective-permute-start | bytes 3342344 | tf_op jit(solution)/shard_map/ppermute | solution.py:255
  59.7 25.7 %collective-permute-start.8 = (bf16[1920,256]{1,0:T(8,128)(2,1)S(1)}, bf16[1920,256]{1,0:T(8,128)(2,1)S(1)}, u32[]{:S(2)}, u32[]{:S(2)}) collective-permute-start(bf16[1920,256]{1,0:T(8,128)(2,1)S(1)} %slice.8), channel_id=1, source_target_pairs={{1,0},{2,1},{3,2},{0,3},{5,4},{6,5},{7,6},{4,7},{9,8},{10,9},{11,1... | collective-permute-start | bytes 2949128 | tf_op jit(solution)/shard_map/ppermute | solution.py:254
  72.2 13.2 %collective-permute-start.7 = (bf16[6,128,256]{2,1,0:T(8,128)(2,1)S(1)}, bf16[6,128,256]{2,1,0:T(8,128)(2,1)S(1)}, u32[]{:S(2)}, u32[]{:S(2)}) collective-permute-start(bf16[6,128,256]{2,1,0:T(8,128)(2,1)S(1)} %get-tuple-element.26), channel_id=1, source_target_pairs={{0,16},{16,0},{1,17},{17,1},{2,18},{18,2},{3,19},{19,3},{4,20},{20... | collective-permute-start | bytes 1179656 | tf_op jit(solution)/shard_map/ppermute | solution.py:295
  81.6 3.9 %collective-permute-start.2 = (bf16[3,128,256]{2,1,0:T(8,128)(2,1)S(1)}, bf16[3,128,256]{2,1,0:T(8,128)(2,1)S(1)}, u32[]{:S(2)}, u32[]{:S(2)}) collective-permute-start(bf16[3,128,256]{2,1,0:T(8,128)(2,1)S(1)} %get-tuple-element.23), channel_id=1, source_target_pairs={{0,16},{16,0},{1,17},{17,1},{2,18},{18,2},{3,19},{19,3},{4,20},{20... | collective-permute-start | bytes 589832 | tf_op jit(solution)/shard_map/ppermute | solution.py:295
  90.3 1.9 %collective-permute-start.12 = (bf16[7,128,256]{2,1,0:T(8,128)(2,1)S(1)}, bf16[7,128,256]{2,1,0:T(8,128)(2,1)S(1)}, u32[]{:S(2)}, u32[]{:S(2)}) collective-permute-start(bf16[7,128,256]{2,1,0:T(8,128)(2,1)S(1)} %get-tuple-element.34), channel_id=1, source_target_pairs={{0,16},{16,0},{1,17},{17,1},{2,18},{18,2},{3,19},{19,3},{4,20},{20... | collective-permute-start | bytes 1376264 | tf_op jit(solution)/shard_map/ppermute | solution.py:295
  116.1 3.2 %collective-permute-start.13 = (f32[2,128,256]{2,1,0:T(8,128)S(1)}, f32[2,128,256]{2,1,0:T(8,128)S(1)}, u32[]{:S(2)}, u32[]{:S(2)}) collective-permute-start(f32[2,128,256]{2,1,0:T(8,128)S(1)} %shard_map.60), channel_id=1, source_target_pairs={{0,16},{16,0},{1,17},{17,1},{2,18},{18,2},{3,19},{19,3},{4,20},{20... | collective-permute-start | bytes 786440 | tf_op jit(solution)/shard_map/ppermute | solution.py:298

commit v7 on v6

--- a/solution.py
+++ b/solution.py
@@ -71,7 +71,7 @@
         scratch_shapes=[pltpu.VMEM((width, width, cols), BF16)],
         compiler_params=pltpu.CompilerParams(vmem_limit_bytes=12 * 2**20),
         cost_estimate=pl.CostEstimate(
-            flops=40 * 10**9, bytes_accessed=4 * 2**20, transcendentals=0
+            flops=5 * 10**9, bytes_accessed=4 * 2**20, transcendentals=0
         ),
     )(pairs, tiles, green_occ, green_virt)
 

time: 121 us -> 120 us (level)
    ppermute x1, waiting for transfers between devices: 13.6 us -> 11.3 us  [ring(): lax.ppermute(block, axis, take_prev)]
    ppermute x1, starting transfers between devices: 0.01 us -> 2.11 us  [ring(): lax.ppermute(block, axis, take_prev)]
    ppermute x1, starting transfers between devices: 3.38 us -> 1.35 us  [ring(): lax.ppermute(block, axis, take_next)]
    ppermute x1, waiting for transfers between devices: 1.98 us -> 4 us  [around(): before_low = lax.ppermute(low, axis, take_prev)]
where the time goes in v7:
time: 120 us
  waiting for transfers between devices  44.9 us (37%)
  starting transfers between devices  24.2 us (20%)
  Pallas kernels  23.5 us (20%)
  blocking collectives  21.7 us (18%)
  local copies, waits for them, and re-layouts  2.67 us (2%)
  other arithmetic  2.53 us (2%)
    all_to_all x1, blocking collectives, per_device(): parts = lax.all_to_all(sends, ('y', 'x'), 0, 0)  21.7 us
    ppermute x1, waiting for transfers between devices, around(): after_low = lax.ppermute(low, axis, take_next)  20.2 us
    pallas_call x3, Pallas kernels, products(): pl.pallas_call(functools.partial(products_kernel, pairs, left_at, right_a...  15 us
    ppermute x1, waiting for transfers between devices, ring(): lax.ppermute(block, axis, take_prev)  11.3 us
    ppermute x3, starting transfers between devices, per_device(): halves += [keep, lax.ppermute(send, 'c', swap)]  7.25 us
    ppermute x1, waiting for transfers between devices, around(): far_low = lax.ppermute(after_low, axis, take_next)  6.48 us
    pallas_call x1, Pallas kernels, contract(): pl.pallas_call(functools.partial(contract_kernel, width, 16), in_specs=[I...  4.67 us
    ppermute x1, waiting for transfers between devices, around(): before_low = lax.ppermute(low, axis, take_prev)  4 us
  transfers between devices with their start and end apart: 14, of which 7 were waited for; matrix products, arithmetic and copies ran while one was open for 2% of the time, Pallas kernels for 13%

profile of v7, /device:TPU:1, one launch (start us, length us, event | category | flops | bytes accessed | tf_op | source)
XLA Modules:
  0.0 119.6 jit_solution(10589572538918509180)
XLA Ops:
  0.7 1.8 %broadcast_multiply_fusion.tiles_ref.refs_0_ = bf16[4096,256]{1,0:T(8,128)(2,1)S(1)} fusion(bf16[4096,256]{1,0:T(8,128)(2,1)} %param.5, bf16[256]{0:T(256)(128)(2,1)S(1)} %broadcast_bitcast_fusion), kind=kLoop, calls=%fused_computation | loop fusion | flops 1048576 | bytes 4194816 | tf_op jit(solution)/shard_map/mul | solution.py:281
  2.5 2.1 %collective-permute-start.1 = (bf16[4096,256]{1,0:T(8,128)(2,1)S(1)}, bf16[4096,256]{1,0:T(8,128)(2,1)}, u32[]{:S(2)}, u32[]{:S(2)}) collective-permute-start(bf16[4096,256]{1,0:T(8,128)(2,1)S(1)} %broadcast_multiply_fusion.tiles_ref.refs_0_), channel_id=1, source_target_pairs={{3,0},{0,1},{1,2},{2,3},{7,4},{4,5},{5,6},{6,7},{11,8},{8,9},{9,10... | collective-permute-start | bytes 6291464 | tf_op jit(solution)/shard_map/ppermute | solution.py:247
  4.6 1.4 %collective-permute-start = (bf16[4096,256]{1,0:T(8,128)(2,1)S(1)}, bf16[4096,256]{1,0:T(8,128)(2,1)}, u32[]{:S(2)}, u32[]{:S(2)}) collective-permute-start(bf16[4096,256]{1,0:T(8,128)(2,1)S(1)} %broadcast_multiply_fusion.tiles_ref.refs_0_), channel_id=1, source_target_pairs={{1,0},{2,1},{3,2},{0,3},{5,4},{6,5},{7,6},{4,7},{9,8},{10,9},{11,1... | collective-permute-start | bytes 6291464 | tf_op jit(solution)/shard_map/ppermute | solution.py:247
  6.0 4.7 %shard_map.55 = (bf16[1920,256]{1,0:T(8,128)(2,1)}, bf16[2176,256]{1,0:T(8,128)(2,1)}) custom-call(s32[1,2]{1,0:T(1,128)S(1)} %copy-done.2, bf16[4096,256]{1,0:T(8,128)(2,1)S(1)} %broadcast_multiply_fusion.tiles_ref.refs_0_, bf16[16,64,64]{2,1,0:T(8,128)(2,1)S(1)} %copy-done, bf16[16,64,64]{2,1,0:T(8,128)(2,1)S(1)} %copy-done.1), custom_call_target="tpu_custom_call" | custom-call | flops 5000000000 | bytes 4194304 | tf_op jit(solution)/shard_map/pallas_call | solution.py:66
  10.7 1.8 %collective-permute-start.6 = (bf16[2176,256]{1,0:T(8,128)(2,1)}, bf16[2176,256]{1,0:T(8,128)(2,1)S(1)}, u32[]{:S(2)}, u32[]{:S(2)}) collective-permute-start(bf16[2176,256]{1,0:T(8,128)(2,1)} %get-tuple-element.21.refs_4_), channel_id=1, source_target_pairs={{12,0},{0,4},{4,8},{8,12},{13,1},{1,5},{5,9},{9,13},{14,2},{2,6},{... | collective-permute-start | bytes 3342344 | tf_op jit(solution)/shard_map/ppermute | solution.py:263
  12.4 2.1 %collective-permute-start.3 = (bf16[1920,256]{1,0:T(8,128)(2,1)}, bf16[1920,256]{1,0:T(8,128)(2,1)}, u32[]{:S(2)}, u32[]{:S(2)}) collective-permute-start(bf16[1920,256]{1,0:T(8,128)(2,1)} %get-tuple-element.20.refs_3_), channel_id=1, source_target_pairs={{4,0},{8,4},{12,8},{0,12},{5,1},{9,5},{13,9},{1,13},{6,2},{10,6},{... | collective-permute-start | bytes 2949128 | tf_op jit(solution)/shard_map/ppermute | solution.py:262
  14.6 20.2 %collective-permute-done.3.refs_0_ = bf16[1920,256]{1,0:T(8,128)(2,1)} collective-permute-done((bf16[1920,256]{1,0:T(8,128)(2,1)}, bf16[1920,256]{1,0:T(8,128)(2,1)}, u32[]{:S(2)}, u32[]{:S(2)}) %collective-permute-start.3) | collective-permute-done | bytes 983072 | tf_op jit(solution)/shard_map/ppermute | solution.py:262
  34.8 3.3 %collective-permute-start.4 = (bf16[2176,256]{1,0:T(8,128)(2,1)}, bf16[2176,256]{1,0:T(8,128)(2,1)S(1)}, u32[]{:S(2)}, u32[]{:S(2)}) collective-permute-start(bf16[2176,256]{1,0:T(8,128)(2,1)} %get-tuple-element.21.refs_4_), channel_id=1, source_target_pairs={{4,0},{8,4},{12,8},{0,12},{5,1},{9,5},{13,9},{1,13},{6,2},{10,6},{... | collective-permute-start | bytes 3342344 | tf_op jit(solution)/shard_map/ppermute | solution.py:264
  39.7 11.3 %collective-permute-done.1.refs_2_ = bf16[4096,256]{1,0:T(8,128)(2,1)} collective-permute-done((bf16[4096,256]{1,0:T(8,128)(2,1)S(1)}, bf16[4096,256]{1,0:T(8,128)(2,1)}, u32[]{:S(2)}, u32[]{:S(2)}) %collective-permute-start.1) | collective-permute-done | bytes 2097184 | tf_op jit(solution)/shard_map/ppermute | solution.py:247
  50.9 2.0 %collective-permute-start.11 = (bf16[2176,256]{1,0:T(8,128)(2,1)S(1)}, bf16[2176,256]{1,0:T(8,128)(2,1)S(1)}, u32[]{:S(2)}, u32[]{:S(2)}) collective-permute-start(bf16[2176,256]{1,0:T(8,128)(2,1)S(1)} %collective-permute-done.6.refs_3_), channel_id=1, source_target_pairs={{12,0},{0,4},{4,8},{8,12},{13,1},{1,5},{5,9},{9,13},{14,2},{2,6},{... | collective-permute-start | bytes 3342344 | tf_op jit(solution)/shard_map/ppermute | solution.py:267
  52.9 1.3 %slice.9 = bf16[2176,256]{1,0:T(8,128)(2,1)S(1)} slice(bf16[4096,256]{1,0:T(8,128)(2,1)} %collective-permute-done.1.refs_2_), slice={[1920:4096], [0:256]} | slice | bytes 2228224 | tf_op jit(solution)/shard_map/slice | solution.py:255
  54.3 1.3 %slice.8 = bf16[1920,256]{1,0:T(8,128)(2,1)S(1)} slice(bf16[4096,256]{1,0:T(8,128)(2,1)} %collective-permute-done.refs_1_), slice={[0:1920], [0:256]} | slice | bytes 1966080 | tf_op jit(solution)/shard_map/slice | solution.py:254
  55.6 4.0 %collective-permute-done.5.refs_2_ = bf16[1920,256]{1,0:T(8,128)(2,1)} collective-permute-done((bf16[1920,256]{1,0:T(8,128)(2,1)}, bf16[1920,256]{1,0:T(8,128)(2,1)}, u32[]{:S(2)}, u32[]{:S(2)}) %collective-permute-start.5) | collective-permute-done | bytes 983072 | tf_op jit(solution)/shard_map/ppermute | solution.py:265
  59.6 1.3 %collective-permute-start.8 = (bf16[1920,256]{1,0:T(8,128)(2,1)S(1)}, bf16[1920,256]{1,0:T(8,128)(2,1)S(1)}, u32[]{:S(2)}, u32[]{:S(2)}) collective-permute-start(bf16[1920,256]{1,0:T(8,128)(2,1)S(1)} %slice.8), channel_id=1, source_target_pairs={{1,0},{2,1},{3,2},{0,3},{5,4},{6,5},{7,6},{4,7},{9,8},{10,9},{11,1... | collective-permute-start | bytes 2949128 | tf_op jit(solution)/shard_map/ppermute | solution.py:254
  60.8 4.8 %shard_map.56 = (f32[3,128,256]{2,1,0:T(8,128)S(1)}, bf16[3,128,256]{2,1,0:T(8,128)(2,1)S(1)}, bf16[1920,256]{1,0:T(8,128)(2,1)S(1)}, bf16[2176,256]{1,0:T(8,128)(2,1)S(1)}, bf16[3,256,4096]{2,1,0:T(8,128)(2,1)S(1)}) custom-call(s32[9]{0:T(128)S(1)} %pad_add_fusion.scalars, bf16[4096,256]{1,0:T(8,128)(2,1)S(1)} %broadcast_multiply_fusion.tiles_ref.refs_0_, ...), custom_call_target="tpu_custom_call" | custom-call | flops 16106127360 | bytes 1048576 | tf_op jit(solution)/shard_map/pallas_call | solution.py:139
  65.6 5.3 %shard_map.57 = (f32[6,128,256]{2,1,0:T(8,128)S(1)}, bf16[6,128,256]{2,1,0:T(8,128)(2,1)S(1)}, bf16[1920,256]{1,0:T(8,128)(2,1)S(1)}, bf16[2176,256]{1,0:T(8,128...) custom-call(s32[9]{0:T(128)S(1)} %pad_add_fusion.scalars, ...), custom_call_target="tpu_custom_call" | custom-call | flops 3221225472 | bytes 1048576 | tf_op jit(solution)/shard_map/pallas_call | solution.py:139
  71.0 3.7 %collective-permute-start.7 = (bf16[6,128,256]{2,1,0:T(8,128)(2,1)S(1)}, bf16[6,128,256]{2,1,0:T(8,128)(2,1)S(1)}, u32[]{:S(2)}, u32[]{:S(2)}) collective-permute-start(bf16[6,128,256]{2,1,0:T(8,128)(2,1)S(1)} %get-tuple-element.26), channel_id=1, source_target_pairs={{0,16},{16,0},{1,17},{17,1},{2,18},{18,2},{3,19},{19,3},{4,20},{20... | collective-permute-start | bytes 1179656 | tf_op jit(solution)/shard_map/ppermute | solution.py:295
  74.7 6.5 %collective-permute-done.10.refs_6_ = bf16[1920,256]{1,0:T(8,128)(2,1)S(1)} collective-permute-done((bf16[1920,256]{1,0:T(8,128)(2,1)}, bf16[1920,256]{1,0:T(8,128)(2,1)S(1)}, u32[]{:S(2)}, u32[]{:S(2)}) %collective-permute-start.10) | collective-permute-done | bytes 983072 | tf_op jit(solution)/shard_map/ppermute | solution.py:266
  81.2 3.1 %collective-permute-start.2 = (bf16[3,128,256]{2,1,0:T(8,128)(2,1)S(1)}, bf16[3,128,256]{2,1,0:T(8,128)(2,1)S(1)}, u32[]{:S(2)}, u32[]{:S(2)}) collective-permute-start(bf16[3,128,256]{2,1,0:T(8,128)(2,1)S(1)} %get-tuple-element.23), channel_id=1, source_target_pairs={{0,16},{16,0},{1,17},{17,1},{2,18},{18,2},{3,19},{19,3},{4,20},{20... | collective-permute-start | bytes 589832 | tf_op jit(solution)/shard_map/ppermute | solution.py:295
  85.3 4.9 %shard_map.58 = (f32[7,128,256]{2,1,0:T(8,128)S(1)}, bf16[7,128,256]{2,1,0:T(8,128)(2,1)S(1)}) custom-call(s32[9]{0:T(128)S(1)} %pad_add_fusion.scalars, bf16[1920,256]{1,0:T(8,128)(2,1)S(1)} %collective-permute-done.8.refs_0_, bf16[2176,256]{1,0:T(8,128)(2,1)S(1)} %collective-permute-done.9.refs_1_, bf16[1920,256]{1,0:T(8,128)(2,1)S(1)} %get-tuple-element.27.refs_2_, ...), custom_call_target="tpu_custom_call" | custom-call | flops 3758096384 | bytes 1048576 | tf_op jit(solution)/shard_map/pallas_call | solution.py:139
  90.7 1.4 %collective-permute-done.12.refs_5_ = bf16[7,128,256]{2,1,0:T(8,128)(2,1)S(1)} collective-permute-done((bf16[7,128,256]{2,1,0:T(8,128)(2,1)S(1)}, bf16[7,128,256]{2,1,0:T(8,128)(2,1)S(1)}, u32[]{:S(2)}, u32[]{:S(2)}) %collective-permute-start.12) | collective-permute-done | bytes 458784 | tf_op jit(solution)/shard_map/ppermute | solution.py:295
  92.8 21.7 %all_to_all.5.parts_ref = bf16[16,128,256]{2,1,0:T(8,128)(2,1)S(1)} all-to-all(bf16[16,128,256]{2,1,0:T(8,128)(2,1)S(1)} %shard_map.59), channel_id=1, replica_groups=mesh['y'=4,'c'=2,'z'=4,'x'=4] {'y','x'}, dimensions={0} | all-to-all | bytes 2097152 | tf_op jit(solution)/shard_map/all_to_all | solution.py:297
  115.2 1.8 %collective-permute-start.13 = (f32[2,128,256]{2,1,0:T(8,128)S(1)}, f32[2,128,256]{2,1,0:T(8,128)S(1)}, u32[]{:S(2)}, u32[]{:S(2)}) collective-permute-start(f32[2,128,256]{2,1,0:T(8,128)S(1)} %shard_map.60), channel_id=1, source_target_pairs={{0,16},{16,0},{1,17},{17,1},{2,18},{18,2},{3,19},{19,3},{4,20},{20... | collective-permute-start | bytes 786440 | tf_op jit(solution)/shard_map/ppermute | solution.py:298
  117.0 1.3 %shard_map.61.whole_ref = f32[256,512]{1,0:T(8,128)} custom-call(s32[9]{0:T(128)S(1)} %pad_add_fusion.scalars, bf16[16,128,256]{2,1,0:T(8,128)(2,1)S(1)} %all_to_all.5.parts_ref), custom_call_target="tpu_custom_call" | custom-call | flops 1048576 | bytes 1048576 | tf_op jit(solution)/shard_map/pallas_call | solution.py:209
  (26 shorter events, 6.6 us)
Async XLA Ops:
  0.7 5.3 %copy-start = (bf16[16,64,64]{2,1,0:T(8,128)(2,1)S(1)}, bf16[16,64,64]{2,1,0:T(8,128)(2,1)}, u32[]{:S(2)}) copy-start(bf16[16,64,64]{2,1,0:T(8,128)(2,1)} %occ_ref.1) | copy-start | bytes 393220
  0.7 5.3 %copy-start.1 = (bf16[16,64,64]{2,1,0:T(8,128)(2,1)S(1)}, bf16[16,64,64]{2,1,0:T(8,128)(2,1)}, u32[]{:S(2)}) copy-start(bf16[16,64,64]{2,1,0:T(8,128)(2,1)} %virt_ref.1) | copy-start | bytes 393220
  0.7 5.3 %copy-start.2 = (s32[1,2]{1,0:T(1,128)S(1)}, s32[1,2]{1,0:T(1,128)}, u32[]{:S(2)}) copy-start(s32[1,2]{1,0:T(1,128)} %pairs.1) | copy-start | bytes 28
  2.5 48.4 %collective-permute-start.1 = (bf16[4096,256]{1,0:T(8,128)(2,1)S(1)}, bf16[4096,256]{1,0:T(8,128)(2,1)}, u32[]{:S(2)}, u32[]{:S(2)}) collective-permute-start(bf16[4096,256]{1,0:T(8,128)(2,1)S(1)} %broadcast_multiply_fusion.tiles_ref.refs_0_), channel_id=1, source_target_pairs={{3,0},{0,1},{1,2},{2,3},{7,4},{4,5},{5,6},{6,7},{11,8},{8,9},{9,10... | collective-permute-start | bytes 6291464 | tf_op jit(solution)/shard_map/ppermute | solution.py:247
  4.6 49.6 %collective-permute-start = (bf16[4096,256]{1,0:T(8,128)(2,1)S(1)}, bf16[4096,256]{1,0:T(8,128)(2,1)}, u32[]{:S(2)}, u32[]{:S(2)}) collective-permute-start(bf16[4096,256]{1,0:T(8,128)(2,1)S(1)} %broadcast_multiply_fusion.tiles_ref.refs_0_), channel_id=1, source_target_pairs={{1,0},{2,1},{3,2},{0,3},{5,4},{6,5},{7,6},{4,7},{9,8},{10,9},{11,1... | collective-permute-start | bytes 6291464 | tf_op jit(solution)/shard_map/ppermute | solution.py:247
  10.7 27.8 %collective-permute-start.6 = (bf16[2176,256]{1,0:T(8,128)(2,1)}, bf16[2176,256]{1,0:T(8,128)(2,1)S(1)}, u32[]{:S(2)}, u32[]{:S(2)}) collective-permute-start(bf16[2176,256]{1,0:T(8,128)(2,1)} %get-tuple-element.21.refs_4_), channel_id=1, source_target_pairs={{12,0},{0,4},{4,8},{8,12},{13,1},{1,5},{5,9},{9,13},{14,2},{2,6},{... | collective-permute-start | bytes 3342344 | tf_op jit(solution)/shard_map/ppermute | solution.py:263
  12.4 22.4 %collective-permute-start.3 = (bf16[1920,256]{1,0:T(8,128)(2,1)}, bf16[1920,256]{1,0:T(8,128)(2,1)}, u32[]{:S(2)}, u32[]{:S(2)}) collective-permute-start(bf16[1920,256]{1,0:T(8,128)(2,1)} %get-tuple-element.20.refs_3_), channel_id=1, source_target_pairs={{4,0},{8,4},{12,8},{0,12},{5,1},{9,5},{13,9},{1,13},{6,2},{10,6},{... | collective-permute-start | bytes 2949128 | tf_op jit(solution)/shard_map/ppermute | solution.py:262
  14.5 45.0 %collective-permute-start.5 = (bf16[1920,256]{1,0:T(8,128)(2,1)}, bf16[1920,256]{1,0:T(8,128)(2,1)}, u32[]{:S(2)}, u32[]{:S(2)}) collective-permute-start(bf16[1920,256]{1,0:T(8,128)(2,1)} %get-tuple-element.20.refs_3_), channel_id=1, source_target_pairs={{12,0},{0,4},{4,8},{8,12},{13,1},{1,5},{5,9},{9,13},{14,2},{2,6},{... | collective-permute-start | bytes 2949128 | tf_op jit(solution)/shard_map/ppermute | solution.py:265
  34.8 30.8 %collective-permute-start.4 = (bf16[2176,256]{1,0:T(8,128)(2,1)}, bf16[2176,256]{1,0:T(8,128)(2,1)S(1)}, u32[]{:S(2)}, u32[]{:S(2)}) collective-permute-start(bf16[2176,256]{1,0:T(8,128)(2,1)} %get-tuple-element.21.refs_4_), channel_id=1, source_target_pairs={{4,0},{8,4},{12,8},{0,12},{5,1},{9,5},{13,9},{1,13},{6,2},{10,6},{... | collective-permute-start | bytes 3342344 | tf_op jit(solution)/shard_map/ppermute | solution.py:264
  38.5 42.6 %collective-permute-start.10 = (bf16[1920,256]{1,0:T(8,128)(2,1)}, bf16[1920,256]{1,0:T(8,128)(2,1)S(1)}, u32[]{:S(2)}, u32[]{:S(2)}) collective-permute-start(bf16[1920,256]{1,0:T(8,128)(2,1)} %collective-permute-done.3.refs_0_), channel_id=1, source_target_pairs={{4,0},{8,4},{12,8},{0,12},{5,1},{9,5},{13,9},{1,13},{6,2},{10,6},{... | collective-permute-start | bytes 2949128 | tf_op jit(solution)/shard_map/ppermute | solution.py:266
  50.9 33.3 %collective-permute-start.11 = (bf16[2176,256]{1,0:T(8,128)(2,1)S(1)}, bf16[2176,256]{1,0:T(8,128)(2,1)S(1)}, u32[]{:S(2)}, u32[]{:S(2)}) collective-permute-start(bf16[2176,256]{1,0:T(8,128)(2,1)S(1)} %collective-permute-done.6.refs_3_), channel_id=1, source_target_pairs={{12,0},{0,4},{4,8},{8,12},{13,1},{1,5},{5,9},{9,13},{14,2},{2,6},{... | collective-permute-start | bytes 3342344 | tf_op jit(solution)/shard_map/ppermute | solution.py:267
  54.2 31.1 %collective-permute-start.9 = (bf16[2176,256]{1,0:T(8,128)(2,1)S(1)}, bf16[2176,256]{1,0:T(8,128)(2,1)S(1)}, u32[]{:S(2)}, u32[]{:S(2)}) collective-permute-start(bf16[2176,256]{1,0:T(8,128)(2,1)S(1)} %slice.9), channel_id=1, source_target_pairs={{3,0},{0,1},{1,2},{2,3},{7,4},{4,5},{5,6},{6,7},{11,8},{8,9},{9,10... | collective-permute-start | bytes 3342344 | tf_op jit(solution)/shard_map/ppermute | solution.py:255
  59.6 25.7 %collective-permute-start.8 = (bf16[1920,256]{1,0:T(8,128)(2,1)S(1)}, bf16[1920,256]{1,0:T(8,128)(2,1)S(1)}, u32[]{:S(2)}, u32[]{:S(2)}) collective-permute-start(bf16[1920,256]{1,0:T(8,128)(2,1)S(1)} %slice.8), channel_id=1, source_target_pairs={{1,0},{2,1},{3,2},{0,3},{5,4},{6,5},{7,6},{4,7},{9,8},{10,9},{11,1... | collective-permute-start | bytes 2949128 | tf_op jit(solution)/shard_map/ppermute | solution.py:254
  71.0 14.4 %collective-permute-start.7 = (bf16[6,128,256]{2,1,0:T(8,128)(2,1)S(1)}, bf16[6,128,256]{2,1,0:T(8,128)(2,1)S(1)}, u32[]{:S(2)}, u32[]{:S(2)}) collective-permute-start(bf16[6,128,256]{2,1,0:T(8,128)(2,1)S(1)} %get-tuple-element.26), channel_id=1, source_target_pairs={{0,16},{16,0},{1,17},{17,1},{2,18},{18,2},{3,19},{19,3},{4,20},{20... | collective-permute-start | bytes 1179656 | tf_op jit(solution)/shard_map/ppermute | solution.py:295
  81.2 4.2 %collective-permute-start.2 = (bf16[3,128,256]{2,1,0:T(8,128)(2,1)S(1)}, bf16[3,128,256]{2,1,0:T(8,128)(2,1)S(1)}, u32[]{:S(2)}, u32[]{:S(2)}) collective-permute-start(bf16[3,128,256]{2,1,0:T(8,128)(2,1)S(1)} %get-tuple-element.23), channel_id=1, source_target_pairs={{0,16},{16,0},{1,17},{17,1},{2,18},{18,2},{3,19},{19,3},{4,20},{20... | collective-permute-start | bytes 589832 | tf_op jit(solution)/shard_map/ppermute | solution.py:295
  90.2 1.9 %collective-permute-start.12 = (bf16[7,128,256]{2,1,0:T(8,128)(2,1)S(1)}, bf16[7,128,256]{2,1,0:T(8,128)(2,1)S(1)}, u32[]{:S(2)}, u32[]{:S(2)}) collective-permute-start(bf16[7,128,256]{2,1,0:T(8,128)(2,1)S(1)} %get-tuple-element.34), channel_id=1, source_target_pairs={{0,16},{16,0},{1,17},{17,1},{2,18},{18,2},{3,19},{19,3},{4,20},{20... | collective-permute-start | bytes 1376264 | tf_op jit(solution)/shard_map/ppermute | solution.py:295
  115.2 3.2 %collective-permute-start.13 = (f32[2,128,256]{2,1,0:T(8,128)S(1)}, f32[2,128,256]{2,1,0:T(8,128)S(1)}, u32[]{:S(2)}, u32[]{:S(2)}) collective-permute-start(f32[2,128,256]{2,1,0:T(8,128)S(1)} %shard_map.60), channel_id=1, source_target_pairs={{0,16},{16,0},{1,17},{17,1},{2,18},{18,2},{3,19},{19,3},{4,20},{20... | collective-permute-start | bytes 786440 | tf_op jit(solution)/shard_map/ppermute | solution.py:298

commit v8 on v7

--- a/solution.py
+++ b/solution.py
@@ -17,7 +17,7 @@
 )
 COSTS = (10, 1, 1)
 NEAR = (0, 1, 3)
-LIMIT = 12
+LIMIT = 24
 LOW = 1920
 IN_VMEM = pl.BlockSpec(memory_space=pltpu.VMEM)
 IN_SMEM = pl.BlockSpec(memory_space=pltpu.SMEM)

time: 120 us -> 120 us (level)
  no operation moved by 1% of the time
where the time goes in v8:
time: 120 us
  waiting for transfers between devices  44.9 us (37%)
  starting transfers between devices  24.2 us (20%)
  Pallas kernels  23.5 us (20%)
  blocking collectives  21.7 us (18%)
  local copies, waits for them, and re-layouts  2.67 us (2%)
  other arithmetic  2.53 us (2%)
    all_to_all x1, blocking collectives, per_device(): parts = lax.all_to_all(sends, ('y', 'x'), 0, 0)  21.7 us
    ppermute x1, waiting for transfers between devices, around(): after_low = lax.ppermute(low, axis, take_next)  20.2 us
    pallas_call x3, Pallas kernels, products(): pl.pallas_call(functools.partial(products_kernel, pairs, left_at, right_a...  15 us
    ppermute x1, waiting for transfers between devices, ring(): lax.ppermute(block, axis, take_prev)  11.3 us
    ppermute x3, starting transfers between devices, per_device(): halves += [keep, lax.ppermute(send, 'c', swap)]  7.25 us
    ppermute x1, waiting for transfers between devices, around(): far_low = lax.ppermute(after_low, axis, take_next)  6.48 us
    pallas_call x1, Pallas kernels, contract(): pl.pallas_call(functools.partial(contract_kernel, width, 16), in_specs=[I...  4.67 us
    ppermute x1, waiting for transfers between devices, around(): before_low = lax.ppermute(low, axis, take_prev)  4 us
  transfers between devices with their start and end apart: 14, of which 7 were waited for; matrix products, arithmetic and copies ran while one was open for 2% of the time, Pallas kernels for 13%

profile of v8, /device:TPU:1, one launch (start us, length us, event | category | flops | bytes accessed | tf_op | source)
XLA Modules:
  0.0 119.6 jit_solution(14511023338133318363)
XLA Ops:
  0.7 1.8 %broadcast_multiply_fusion.tiles_ref.refs_0_ = bf16[4096,256]{1,0:T(8,128)(2,1)S(1)} fusion(bf16[4096,256]{1,0:T(8,128)(2,1)} %param.5, bf16[256]{0:T(256)(128)(2,1)S(1)} %broadcast_bitcast_fusion), kind=kLoop, calls=%fused_computation | loop fusion | flops 1048576 | bytes 4194816 | tf_op jit(solution)/shard_map/mul | solution.py:281
  2.5 2.1 %collective-permute-start.1 = (bf16[4096,256]{1,0:T(8,128)(2,1)S(1)}, bf16[4096,256]{1,0:T(8,128)(2,1)}, u32[]{:S(2)}, u32[]{:S(2)}) collective-permute-start(bf16[4096,256]{1,0:T(8,128)(2,1)S(1)} %broadcast_multiply_fusion.tiles_ref.refs_0_), channel_id=1, source_target_pairs={{3,0},{0,1},{1,2},{2,3},{7,4},{4,5},{5,6},{6,7},{11,8},{8,9},{9,10... | collective-permute-start | bytes 6291464 | tf_op jit(solution)/shard_map/ppermute | solution.py:247
  4.6 1.4 %collective-permute-start = (bf16[4096,256]{1,0:T(8,128)(2,1)S(1)}, bf16[4096,256]{1,0:T(8,128)(2,1)}, u32[]{:S(2)}, u32[]{:S(2)}) collective-permute-start(bf16[4096,256]{1,0:T(8,128)(2,1)S(1)} %broadcast_multiply_fusion.tiles_ref.refs_0_), channel_id=1, source_target_pairs={{1,0},{2,1},{3,2},{0,3},{5,4},{6,5},{7,6},{4,7},{9,8},{10,9},{11,1... | collective-permute-start | bytes 6291464 | tf_op jit(solution)/shard_map/ppermute | solution.py:247
  6.0 4.7 %shard_map.55 = (bf16[1920,256]{1,0:T(8,128)(2,1)}, bf16[2176,256]{1,0:T(8,128)(2,1)}) custom-call(s32[1,2]{1,0:T(1,128)S(1)} %copy-done.2, bf16[4096,256]{1,0:T(8,128)(2,1)S(1)} %broadcast_multiply_fusion.tiles_ref.refs_0_, bf16[16,64,64]{2,1,0:T(8,128)(2,1)S(1)} %copy-done, bf16[16,64,64]{2,1,0:T(8,128)(2,1)S(1)} %copy-done.1), custom_call_target="tpu_custom_call" | custom-call | flops 5000000000 | bytes 4194304 | tf_op jit(solution)/shard_map/pallas_call | solution.py:66
  10.7 1.8 %collective-permute-start.6 = (bf16[2176,256]{1,0:T(8,128)(2,1)}, bf16[2176,256]{1,0:T(8,128)(2,1)S(1)}, u32[]{:S(2)}, u32[]{:S(2)}) collective-permute-start(bf16[2176,256]{1,0:T(8,128)(2,1)} %get-tuple-element.21.refs_4_), channel_id=1, source_target_pairs={{12,0},{0,4},{4,8},{8,12},{13,1},{1,5},{5,9},{9,13},{14,2},{2,6},{... | collective-permute-start | bytes 3342344 | tf_op jit(solution)/shard_map/ppermute | solution.py:263
  12.4 2.1 %collective-permute-start.3 = (bf16[1920,256]{1,0:T(8,128)(2,1)}, bf16[1920,256]{1,0:T(8,128)(2,1)}, u32[]{:S(2)}, u32[]{:S(2)}) collective-permute-start(bf16[1920,256]{1,0:T(8,128)(2,1)} %get-tuple-element.20.refs_3_), channel_id=1, source_target_pairs={{4,0},{8,4},{12,8},{0,12},{5,1},{9,5},{13,9},{1,13},{6,2},{10,6},{... | collective-permute-start | bytes 2949128 | tf_op jit(solution)/shard_map/ppermute | solution.py:262
  14.6 20.2 %collective-permute-done.3.refs_0_ = bf16[1920,256]{1,0:T(8,128)(2,1)} collective-permute-done((bf16[1920,256]{1,0:T(8,128)(2,1)}, bf16[1920,256]{1,0:T(8,128)(2,1)}, u32[]{:S(2)}, u32[]{:S(2)}) %collective-permute-start.3) | collective-permute-done | bytes 983072 | tf_op jit(solution)/shard_map/ppermute | solution.py:262
  34.8 3.3 %collective-permute-start.4 = (bf16[2176,256]{1,0:T(8,128)(2,1)}, bf16[2176,256]{1,0:T(8,128)(2,1)S(1)}, u32[]{:S(2)}, u32[]{:S(2)}) collective-permute-start(bf16[2176,256]{1,0:T(8,128)(2,1)} %get-tuple-element.21.refs_4_), channel_id=1, source_target_pairs={{4,0},{8,4},{12,8},{0,12},{5,1},{9,5},{13,9},{1,13},{6,2},{10,6},{... | collective-permute-start | bytes 3342344 | tf_op jit(solution)/shard_map/ppermute | solution.py:264
  39.7 11.3 %collective-permute-done.1.refs_2_ = bf16[4096,256]{1,0:T(8,128)(2,1)} collective-permute-done((bf16[4096,256]{1,0:T(8,128)(2,1)S(1)}, bf16[4096,256]{1,0:T(8,128)(2,1)}, u32[]{:S(2)}, u32[]{:S(2)}) %collective-permute-start.1) | collective-permute-done | bytes 2097184 | tf_op jit(solution)/shard_map/ppermute | solution.py:247
  50.9 2.0 %collective-permute-start.11 = (bf16[2176,256]{1,0:T(8,128)(2,1)S(1)}, bf16[2176,256]{1,0:T(8,128)(2,1)S(1)}, u32[]{:S(2)}, u32[]{:S(2)}) collective-permute-start(bf16[2176,256]{1,0:T(8,128)(2,1)S(1)} %collective-permute-done.6.refs_3_), channel_id=1, source_target_pairs={{12,0},{0,4},{4,8},{8,12},{13,1},{1,5},{5,9},{9,13},{14,2},{2,6},{... | collective-permute-start | bytes 3342344 | tf_op jit(solution)/shard_map/ppermute | solution.py:267
  52.9 1.3 %slice.9 = bf16[2176,256]{1,0:T(8,128)(2,1)S(1)} slice(bf16[4096,256]{1,0:T(8,128)(2,1)} %collective-permute-done.1.refs_2_), slice={[1920:4096], [0:256]} | slice | bytes 2228224 | tf_op jit(solution)/shard_map/slice | solution.py:255
  54.3 1.3 %slice.8 = bf16[1920,256]{1,0:T(8,128)(2,1)S(1)} slice(bf16[4096,256]{1,0:T(8,128)(2,1)} %collective-permute-done.refs_1_), slice={[0:1920], [0:256]} | slice | bytes 1966080 | tf_op jit(solution)/shard_map/slice | solution.py:254
  55.6 4.0 %collective-permute-done.5.refs_2_ = bf16[1920,256]{1,0:T(8,128)(2,1)} collective-permute-done((bf16[1920,256]{1,0:T(8,128)(2,1)}, bf16[1920,256]{1,0:T(8,128)(2,1)}, u32[]{:S(2)}, u32[]{:S(2)}) %collective-permute-start.5) | collective-permute-done | bytes 983072 | tf_op jit(solution)/shard_map/ppermute | solution.py:265
  59.6 1.3 %collective-permute-start.8 = (bf16[1920,256]{1,0:T(8,128)(2,1)S(1)}, bf16[1920,256]{1,0:T(8,128)(2,1)S(1)}, u32[]{:S(2)}, u32[]{:S(2)}) collective-permute-start(bf16[1920,256]{1,0:T(8,128)(2,1)S(1)} %slice.8), channel_id=1, source_target_pairs={{1,0},{2,1},{3,2},{0,3},{5,4},{6,5},{7,6},{4,7},{9,8},{10,9},{11,1... | collective-permute-start | bytes 2949128 | tf_op jit(solution)/shard_map/ppermute | solution.py:254
  60.8 4.8 %shard_map.56 = (f32[3,128,256]{2,1,0:T(8,128)S(1)}, bf16[3,128,256]{2,1,0:T(8,128)(2,1)S(1)}, bf16[1920,256]{1,0:T(8,128)(2,1)S(1)}, bf16[2176,256]{1,0:T(8,128)(2,1)S(1)}, bf16[3,256,4096]{2,1,0:T(8,128)(2,1)S(1)}) custom-call(s32[9]{0:T(128)S(1)} %pad_add_fusion.scalars, bf16[4096,256]{1,0:T(8,128)(2,1)S(1)} %broadcast_multiply_fusion.tiles_ref.refs_0_, ...), custom_call_target="tpu_custom_call" | custom-call | flops 16106127360 | bytes 1048576 | tf_op jit(solution)/shard_map/pallas_call | solution.py:139
  65.6 5.3 %shard_map.57 = (f32[6,128,256]{2,1,0:T(8,128)S(1)}, bf16[6,128,256]{2,1,0:T(8,128)(2,1)S(1)}, bf16[1920,256]{1,0:T(8,128)(2,1)S(1)}, bf16[2176,256]{1,0:T(8,128...) custom-call(s32[9]{0:T(128)S(1)} %pad_add_fusion.scalars, ...), custom_call_target="tpu_custom_call" | custom-call | flops 3221225472 | bytes 1048576 | tf_op jit(solution)/shard_map/pallas_call | solution.py:139
  71.0 3.7 %collective-permute-start.7 = (bf16[6,128,256]{2,1,0:T(8,128)(2,1)S(1)}, bf16[6,128,256]{2,1,0:T(8,128)(2,1)S(1)}, u32[]{:S(2)}, u32[]{:S(2)}) collective-permute-start(bf16[6,128,256]{2,1,0:T(8,128)(2,1)S(1)} %get-tuple-element.26), channel_id=1, source_target_pairs={{0,16},{16,0},{1,17},{17,1},{2,18},{18,2},{3,19},{19,3},{4,20},{20... | collective-permute-start | bytes 1179656 | tf_op jit(solution)/shard_map/ppermute | solution.py:295
  74.7 6.5 %collective-permute-done.10.refs_6_ = bf16[1920,256]{1,0:T(8,128)(2,1)S(1)} collective-permute-done((bf16[1920,256]{1,0:T(8,128)(2,1)}, bf16[1920,256]{1,0:T(8,128)(2,1)S(1)}, u32[]{:S(2)}, u32[]{:S(2)}) %collective-permute-start.10) | collective-permute-done | bytes 983072 | tf_op jit(solution)/shard_map/ppermute | solution.py:266
  81.2 3.1 %collective-permute-start.2 = (bf16[3,128,256]{2,1,0:T(8,128)(2,1)S(1)}, bf16[3,128,256]{2,1,0:T(8,128)(2,1)S(1)}, u32[]{:S(2)}, u32[]{:S(2)}) collective-permute-start(bf16[3,128,256]{2,1,0:T(8,128)(2,1)S(1)} %get-tuple-element.23), channel_id=1, source_target_pairs={{0,16},{16,0},{1,17},{17,1},{2,18},{18,2},{3,19},{19,3},{4,20},{20... | collective-permute-start | bytes 589832 | tf_op jit(solution)/shard_map/ppermute | solution.py:295
  85.3 4.9 %shard_map.58 = (f32[7,128,256]{2,1,0:T(8,128)S(1)}, bf16[7,128,256]{2,1,0:T(8,128)(2,1)S(1)}) custom-call(s32[9]{0:T(128)S(1)} %pad_add_fusion.scalars, bf16[1920,256]{1,0:T(8,128)(2,1)S(1)} %collective-permute-done.8.refs_0_, bf16[2176,256]{1,0:T(8,128)(2,1)S(1)} %collective-permute-done.9.refs_1_, bf16[1920,256]{1,0:T(8,128)(2,1)S(1)} %get-tuple-element.27.refs_2_, ...), custom_call_target="tpu_custom_call" | custom-call | flops 3758096384 | bytes 1048576 | tf_op jit(solution)/shard_map/pallas_call | solution.py:139
  90.7 1.4 %collective-permute-done.12.refs_5_ = bf16[7,128,256]{2,1,0:T(8,128)(2,1)S(1)} collective-permute-done((bf16[7,128,256]{2,1,0:T(8,128)(2,1)S(1)}, bf16[7,128,256]{2,1,0:T(8,128)(2,1)S(1)}, u32[]{:S(2)}, u32[]{:S(2)}) %collective-permute-start.12) | collective-permute-done | bytes 458784 | tf_op jit(solution)/shard_map/ppermute | solution.py:295
  92.8 21.7 %all_to_all.5.parts_ref = bf16[16,128,256]{2,1,0:T(8,128)(2,1)S(1)} all-to-all(bf16[16,128,256]{2,1,0:T(8,128)(2,1)S(1)} %shard_map.59), channel_id=1, replica_groups=mesh['y'=4,'c'=2,'z'=4,'x'=4] {'y','x'}, dimensions={0} | all-to-all | bytes 2097152 | tf_op jit(solution)/shard_map/all_to_all | solution.py:297
  115.2 1.8 %collective-permute-start.13 = (f32[2,128,256]{2,1,0:T(8,128)S(1)}, f32[2,128,256]{2,1,0:T(8,128)S(1)}, u32[]{:S(2)}, u32[]{:S(2)}) collective-permute-start(f32[2,128,256]{2,1,0:T(8,128)S(1)} %shard_map.60), channel_id=1, source_target_pairs={{0,16},{16,0},{1,17},{17,1},{2,18},{18,2},{3,19},{19,3},{4,20},{20... | collective-permute-start | bytes 786440 | tf_op jit(solution)/shard_map/ppermute | solution.py:298
  117.0 1.3 %shard_map.61.whole_ref = f32[256,512]{1,0:T(8,128)} custom-call(s32[9]{0:T(128)S(1)} %pad_add_fusion.scalars, bf16[16,128,256]{2,1,0:T(8,128)(2,1)S(1)} %all_to_all.5.parts_ref), custom_call_target="tpu_custom_call" | custom-call | flops 1048576 | bytes 1048576 | tf_op jit(solution)/shard_map/pallas_call | solution.py:209
  (26 shorter events, 6.6 us)
Async XLA Ops:
  0.7 5.3 %copy-start = (bf16[16,64,64]{2,1,0:T(8,128)(2,1)S(1)}, bf16[16,64,64]{2,1,0:T(8,128)(2,1)}, u32[]{:S(2)}) copy-start(bf16[16,64,64]{2,1,0:T(8,128)(2,1)} %occ_ref.1) | copy-start | bytes 393220
  0.7 5.3 %copy-start.1 = (bf16[16,64,64]{2,1,0:T(8,128)(2,1)S(1)}, bf16[16,64,64]{2,1,0:T(8,128)(2,1)}, u32[]{:S(2)}) copy-start(bf16[16,64,64]{2,1,0:T(8,128)(2,1)} %virt_ref.1) | copy-start | bytes 393220
  0.7 5.3 %copy-start.2 = (s32[1,2]{1,0:T(1,128)S(1)}, s32[1,2]{1,0:T(1,128)}, u32[]{:S(2)}) copy-start(s32[1,2]{1,0:T(1,128)} %pairs.1) | copy-start | bytes 28
  2.5 48.4 %collective-permute-start.1 = (bf16[4096,256]{1,0:T(8,128)(2,1)S(1)}, bf16[4096,256]{1,0:T(8,128)(2,1)}, u32[]{:S(2)}, u32[]{:S(2)}) collective-permute-start(bf16[4096,256]{1,0:T(8,128)(2,1)S(1)} %broadcast_multiply_fusion.tiles_ref.refs_0_), channel_id=1, source_target_pairs={{3,0},{0,1},{1,2},{2,3},{7,4},{4,5},{5,6},{6,7},{11,8},{8,9},{9,10... | collective-permute-start | bytes 6291464 | tf_op jit(solution)/shard_map/ppermute | solution.py:247
  4.6 49.6 %collective-permute-start = (bf16[4096,256]{1,0:T(8,128)(2,1)S(1)}, bf16[4096,256]{1,0:T(8,128)(2,1)}, u32[]{:S(2)}, u32[]{:S(2)}) collective-permute-start(bf16[4096,256]{1,0:T(8,128)(2,1)S(1)} %broadcast_multiply_fusion.tiles_ref.refs_0_), channel_id=1, source_target_pairs={{1,0},{2,1},{3,2},{0,3},{5,4},{6,5},{7,6},{4,7},{9,8},{10,9},{11,1... | collective-permute-start | bytes 6291464 | tf_op jit(solution)/shard_map/ppermute | solution.py:247
  10.7 27.8 %collective-permute-start.6 = (bf16[2176,256]{1,0:T(8,128)(2,1)}, bf16[2176,256]{1,0:T(8,128)(2,1)S(1)}, u32[]{:S(2)}, u32[]{:S(2)}) collective-permute-start(bf16[2176,256]{1,0:T(8,128)(2,1)} %get-tuple-element.21.refs_4_), channel_id=1, source_target_pairs={{12,0},{0,4},{4,8},{8,12},{13,1},{1,5},{5,9},{9,13},{14,2},{2,6},{... | collective-permute-start | bytes 3342344 | tf_op jit(solution)/shard_map/ppermute | solution.py:263
  12.4 22.4 %collective-permute-start.3 = (bf16[1920,256]{1,0:T(8,128)(2,1)}, bf16[1920,256]{1,0:T(8,128)(2,1)}, u32[]{:S(2)}, u32[]{:S(2)}) collective-permute-start(bf16[1920,256]{1,0:T(8,128)(2,1)} %get-tuple-element.20.refs_3_), channel_id=1, source_target_pairs={{4,0},{8,4},{12,8},{0,12},{5,1},{9,5},{13,9},{1,13},{6,2},{10,6},{... | collective-permute-start | bytes 2949128 | tf_op jit(solution)/shard_map/ppermute | solution.py:262
  14.5 45.0 %collective-permute-start.5 = (bf16[1920,256]{1,0:T(8,128)(2,1)}, bf16[1920,256]{1,0:T(8,128)(2,1)}, u32[]{:S(2)}, u32[]{:S(2)}) collective-permute-start(bf16[1920,256]{1,0:T(8,128)(2,1)} %get-tuple-element.20.refs_3_), channel_id=1, source_target_pairs={{12,0},{0,4},{4,8},{8,12},{13,1},{1,5},{5,9},{9,13},{14,2},{2,6},{... | collective-permute-start | bytes 2949128 | tf_op jit(solution)/shard_map/ppermute | solution.py:265
  34.8 30.8 %collective-permute-start.4 = (bf16[2176,256]{1,0:T(8,128)(2,1)}, bf16[2176,256]{1,0:T(8,128)(2,1)S(1)}, u32[]{:S(2)}, u32[]{:S(2)}) collective-permute-start(bf16[2176,256]{1,0:T(8,128)(2,1)} %get-tuple-element.21.refs_4_), channel_id=1, source_target_pairs={{4,0},{8,4},{12,8},{0,12},{5,1},{9,5},{13,9},{1,13},{6,2},{10,6},{... | collective-permute-start | bytes 3342344 | tf_op jit(solution)/shard_map/ppermute | solution.py:264
  38.5 42.6 %collective-permute-start.10 = (bf16[1920,256]{1,0:T(8,128)(2,1)}, bf16[1920,256]{1,0:T(8,128)(2,1)S(1)}, u32[]{:S(2)}, u32[]{:S(2)}) collective-permute-start(bf16[1920,256]{1,0:T(8,128)(2,1)} %collective-permute-done.3.refs_0_), channel_id=1, source_target_pairs={{4,0},{8,4},{12,8},{0,12},{5,1},{9,5},{13,9},{1,13},{6,2},{10,6},{... | collective-permute-start | bytes 2949128 | tf_op jit(solution)/shard_map/ppermute | solution.py:266
  50.9 33.3 %collective-permute-start.11 = (bf16[2176,256]{1,0:T(8,128)(2,1)S(1)}, bf16[2176,256]{1,0:T(8,128)(2,1)S(1)}, u32[]{:S(2)}, u32[]{:S(2)}) collective-permute-start(bf16[2176,256]{1,0:T(8,128)(2,1)S(1)} %collective-permute-done.6.refs_3_), channel_id=1, source_target_pairs={{12,0},{0,4},{4,8},{8,12},{13,1},{1,5},{5,9},{9,13},{14,2},{2,6},{... | collective-permute-start | bytes 3342344 | tf_op jit(solution)/shard_map/ppermute | solution.py:267
  54.2 31.1 %collective-permute-start.9 = (bf16[2176,256]{1,0:T(8,128)(2,1)S(1)}, bf16[2176,256]{1,0:T(8,128)(2,1)S(1)}, u32[]{:S(2)}, u32[]{:S(2)}) collective-permute-start(bf16[2176,256]{1,0:T(8,128)(2,1)S(1)} %slice.9), channel_id=1, source_target_pairs={{3,0},{0,1},{1,2},{2,3},{7,4},{4,5},{5,6},{6,7},{11,8},{8,9},{9,10... | collective-permute-start | bytes 3342344 | tf_op jit(solution)/shard_map/ppermute | solution.py:255
  59.6 25.7 %collective-permute-start.8 = (bf16[1920,256]{1,0:T(8,128)(2,1)S(1)}, bf16[1920,256]{1,0:T(8,128)(2,1)S(1)}, u32[]{:S(2)}, u32[]{:S(2)}) collective-permute-start(bf16[1920,256]{1,0:T(8,128)(2,1)S(1)} %slice.8), channel_id=1, source_target_pairs={{1,0},{2,1},{3,2},{0,3},{5,4},{6,5},{7,6},{4,7},{9,8},{10,9},{11,1... | collective-permute-start | bytes 2949128 | tf_op jit(solution)/shard_map/ppermute | solution.py:254
  71.0 14.4 %collective-permute-start.7 = (bf16[6,128,256]{2,1,0:T(8,128)(2,1)S(1)}, bf16[6,128,256]{2,1,0:T(8,128)(2,1)S(1)}, u32[]{:S(2)}, u32[]{:S(2)}) collective-permute-start(bf16[6,128,256]{2,1,0:T(8,128)(2,1)S(1)} %get-tuple-element.26), channel_id=1, source_target_pairs={{0,16},{16,0},{1,17},{17,1},{2,18},{18,2},{3,19},{19,3},{4,20},{20... | collective-permute-start | bytes 1179656 | tf_op jit(solution)/shard_map/ppermute | solution.py:295
  81.2 4.2 %collective-permute-start.2 = (bf16[3,128,256]{2,1,0:T(8,128)(2,1)S(1)}, bf16[3,128,256]{2,1,0:T(8,128)(2,1)S(1)}, u32[]{:S(2)}, u32[]{:S(2)}) collective-permute-start(bf16[3,128,256]{2,1,0:T(8,128)(2,1)S(1)} %get-tuple-element.23), channel_id=1, source_target_pairs={{0,16},{16,0},{1,17},{17,1},{2,18},{18,2},{3,19},{19,3},{4,20},{20... | collective-permute-start | bytes 589832 | tf_op jit(solution)/shard_map/ppermute | solution.py:295
  90.2 1.9 %collective-permute-start.12 = (bf16[7,128,256]{2,1,0:T(8,128)(2,1)S(1)}, bf16[7,128,256]{2,1,0:T(8,128)(2,1)S(1)}, u32[]{:S(2)}, u32[]{:S(2)}) collective-permute-start(bf16[7,128,256]{2,1,0:T(8,128)(2,1)S(1)} %get-tuple-element.34), channel_id=1, source_target_pairs={{0,16},{16,0},{1,17},{17,1},{2,18},{18,2},{3,19},{19,3},{4,20},{20... | collective-permute-start | bytes 1376264 | tf_op jit(solution)/shard_map/ppermute | solution.py:295
  115.2 3.2 %collective-permute-start.13 = (f32[2,128,256]{2,1,0:T(8,128)S(1)}, f32[2,128,256]{2,1,0:T(8,128)S(1)}, u32[]{:S(2)}, u32[]{:S(2)}) collective-permute-start(f32[2,128,256]{2,1,0:T(8,128)S(1)} %shard_map.60), channel_id=1, source_target_pairs={{0,16},{16,0},{1,17},{17,1},{2,18},{18,2},{3,19},{19,3},{4,20},{20... | collective-permute-start | bytes 786440 | tf_op jit(solution)/shard_map/ppermute | solution.py:298
